TPU v7x, 512 devices: a whole 4x8x8 slice. The times are simulated.
512 devices in a mesh: bl: 64 (over y, z), ta: 8 (over x, core).
Axes of the slice: x: 4, y: 8, z: 8, core: 2. Of those that a mesh axis runs over, the one named last changes fastest.
Arguments:
- visibilities: bfloat16 [128, 16384, 512], P('ta', 'bl'), may hold values from -12 to 12
- flags: int32 [128, 16384], P('ta', 'bl'), may hold values 0 or 1
- group_ids: int32 [16384], P('bl'), may hold values from 0 to 511, as said below
- group_order: int32 [512], replicated, may hold values from 0 to 511, each once
- taper: float32 [256], replicated, may hold values from 0.25 to 1.75
- inv_cov: float32 [256, 256], replicated, may hold values from -1 to 2
Outputs:
- spectrum: float32 [512, 256], P('bl')
Inputs may be any that keep to these rules, and one draw needn't show every extreme that they name: `group_ids`: within each block of 256 baselines the ids do not fall; a baseline of block i belongs to a group whose home block id // 8 equals (i - k) mod (64) for some k < 4.
All inputs are finite; a program needn't handle non-finite values. No bound on the sum of `flags` on one device may be relied on, other than what follows from the above.
Results may differ from a plain program's by a relative error of at most 0.00068.
Values may be sent and summed in bfloat16 or wider, within the bound.
No kernel may reach another device: no remote copies, remote signals or barrier semaphores. Data moves between devices by JAX's collectives and lax.ppermute only.
A program may use at most 64 MiB of HBM per device.

v0:
```python
import math

import jax
import jax.numpy as jnp
from jax import lax
from jax.sharding import PartitionSpec as P

GR_DEV = 8
ROUNDS = 3


def from_behind(shard, axis, by):
    devices = lax.axis_size(axis)
    return lax.ppermute(shard, axis, [(i, (i + by) % devices) for i in range(devices)])


def transform_matrix(taper, inv_cov):
    channels = taper.shape[0]
    ramp = jnp.arange(channels, dtype=jnp.int32)
    phase_index = ramp[:, None] * ramp[None, :] % channels
    angles = 2.0 * math.pi / channels * phase_index.astype(jnp.float32)
    norm_factor = 1.0 / math.sqrt(channels)
    cosines = jnp.cos(angles) * norm_factor
    sines = jnp.sin(angles) * norm_factor
    weighted = taper[:, None] * inv_cov
    cos_part = jnp.dot(
        weighted, cosines, precision=lax.Precision.HIGHEST, preferred_element_type=jnp.float32
    )
    sin_part = jnp.dot(
        weighted, sines, precision=lax.Precision.HIGHEST, preferred_element_type=jnp.float32
    )
    upper_half = jnp.concatenate([cos_part, -sin_part], axis=1)
    lower_half = jnp.concatenate([sin_part, cos_part], axis=1)
    return jnp.concatenate([upper_half, lower_half], axis=0).astype(jnp.bfloat16)


def group_sums(group_table, delays):
    sums = jnp.einsum("tsb,tbc->tsc", group_table, delays, preferred_element_type=jnp.float32)
    counts = jnp.sum(group_table.astype(jnp.float32), axis=-1)
    return (sums.astype(jnp.bfloat16), counts)


def over_time(owned_rows, counts):
    return lax.psum((owned_rows, counts), "ta")


def on_device(visibilities, flags, group_ids, group_order, taper, inv_cov):
    channels = taper.shape[0]
    slot_count = (ROUNDS + 1) * GR_DEV
    device_index = lax.axis_index("bl")
    block_total = lax.axis_size("bl")
    time_count, block_length, row_width = visibilities.shape
    matrix = transform_matrix(taper, inv_cov)
    delays = jnp.dot(
        visibilities.reshape(time_count * block_length, row_width),
        matrix,
        preferred_element_type=jnp.float32,
    )
    delays = delays.astype(jnp.bfloat16).reshape(time_count, block_length, row_width)
    slot_index = (device_index - group_ids // GR_DEV) % block_total * GR_DEV + group_ids % GR_DEV
    slot_range = jnp.arange(slot_count, dtype=jnp.int32)
    onehot = slot_index[None, :] == slot_range[:, None]
    group_table = jnp.where(onehot[None], flags[:, None, :], 0).astype(jnp.bfloat16)
    own_sums, own_counts = group_sums(group_table, delays)
    own_wire = own_counts.astype(jnp.bfloat16)
    partners = []
    for round_number in range(1, ROUNDS + 1):
        partners.append(from_behind((own_sums, own_wire), "bl", round_number))
    cross_power = jnp.zeros((slot_count, channels), jnp.float32)
    pair_count = jnp.zeros((slot_count,), jnp.float32)
    for round_number in range(1, ROUNDS + 1):
        far_sums, far_wire = partners[round_number - 1]
        far_counts = far_wire.astype(jnp.float32)
        offset = round_number * GR_DEV
        product = jnp.sum(
            own_sums[:, offset:, :].astype(jnp.float32)
            * far_sums[:, : slot_count - offset, :].astype(jnp.float32),
            axis=0,
        )
        power_term = product[:, :channels] + product[:, channels:]
        cross_power = cross_power + jnp.pad(power_term, ((offset, 0), (0, 0)))
        count_term = jnp.sum(own_counts[:, offset:] * far_counts[:, : slot_count - offset], axis=0)
        pair_count = pair_count + jnp.pad(count_term, (offset, 0))
    home_blocks = (device_index - slot_range // GR_DEV) % block_total
    groups = home_blocks * GR_DEV + slot_range % GR_DEV
    placement = (group_order[:, None] == groups[None, :]).astype(jnp.float32)
    table_rows = jnp.dot(
        placement, cross_power, precision=lax.Precision.HIGHEST, preferred_element_type=jnp.float32
    )
    table_counts = jnp.dot(
        placement, pair_count, precision=lax.Precision.HIGHEST, preferred_element_type=jnp.float32
    )
    owned_rows, counts = (
        lax.psum_scatter(table_rows, "bl", scatter_dimension=0, tiled=True),
        lax.psum_scatter(table_counts, "bl", scatter_dimension=0, tiled=True),
    )
    owned_rows, counts = over_time(owned_rows, counts)
    return owned_rows / jnp.maximum(counts, 1.0)[:, None]


def solution(mesh):
    return jax.shard_map(
        on_device,
        mesh=mesh,
        in_specs=(P("ta", "bl", None), P("ta", "bl"), P("bl"), P(), P(), P()),
        out_specs=P("bl", None),
        check_vma=False,
    )
```

profile of v0, /device:TPU:1, one launch (start us, length us, event | category | flops | bytes accessed | tf_op | source)
XLA Modules:
  0.0 297.3 jit_solution(5234596002714190670)
XLA Ops:
  6.5 0.0 all-reduce.11.cloned.1.call-start
  6.5 2.5 negate_convert_fusion
  9.1 2.5 convolution_convert_fusion.2
  11.6 6.5 %fusion = bf16[4096,512]{0,1:T(8,128)(2,1)} fusion(bf16[4096,512]{1,0:T(8,128)(2,1)} %bitcast.13, bf16[256,256]{0,1:T(8,128)(2,1)S(1)} %convolution_convert_fusion.2, bf16[256,256]{0,1:T(8,128)(2,1)S(1)} %get-tuple-element.8, bf16[256,256]{0,1:T(8,128)(2,1)S(1)} %get-tuple-element.7), kind=kOutput, calls=%fused_computation.1 | convolution fusion | flops 2151677952 | bytes 8781824 | tf_op jit(solution)/shard_map/dot_general | solution.py:54
  18.1 0.0 copy-start.2
  18.1 0.0 copy-start
  18.1 6.6 %copy.14 = bf16[4096,512]{1,0:T(8,128)(2,1)} copy(bf16[4096,512]{0,1:T(8,128)(2,1)} %fusion) | data formatting | bytes 8388608 | tf_op jit(solution)/shard_map/reshape | solution.py:59
  24.7 0.0 copy-start.1
  24.7 0.0 copy-done.2
  24.7 0.0 copy-done
  24.7 3.0 %convolution_convert_fusion.1 = bf16[16,32,512]{2,1,0:T(8,128)(2,1)S(1)} fusion(bf16[16,256,512]{2,1,0:T(8,128)(2,1)} %bitcast.11, s32[16,256]{1,0:T(8,128)S(1)} %copy-done, pred[32,256]{1,0:T(8,128)(4,1)S(1)} %iota_compare_fusion), kind=kOutput, calls=%fused_computation.2 | convolution fusion | flops 134742016 | bytes 4743168 | tf_op jit(solution)/shard_map/tsb,tbc->tsc/dot_general | solution.py:38
  27.7 4.8 %collective-permute-start = (bf16[16,32,512]{2,1,0:T(8,128)(2,1)S(1)}, bf16[16,32,512]{2,1,0:T(8,128)(2,1)S(1)}, u32[]{:S(2)}, u32[]{:S(2)}) collective-permute-start(bf16[16,32,512]{2,1,0:T(8,128)(2,1)S(1)} %convolution_convert_fusion.1), channel_id=1, source_target_pairs={{0,8},{8,16},{16,24},{24,32},{32,40},{40,48},{48,56},{56,64},{64,7... | collective-permute-start | bytes 1572872 | tf_op jit(solution)/shard_map/ppermute | solution.py:14
  32.6 5.8 %collective-permute-start.1 = (bf16[16,32,512]{2,1,0:T(8,128)(2,1)S(1)}, bf16[16,32,512]{2,1,0:T(8,128)(2,1)S(1)}, u32[]{:S(2)}, u32[]{:S(2)}) collective-permute-start(bf16[16,32,512]{2,1,0:T(8,128)(2,1)S(1)} %convolution_convert_fusion.1), channel_id=1, source_target_pairs={{0,16},{8,24},{16,32},{24,40},{32,48},{40,56},{48,64},{56,72},{64,... | collective-permute-start | bytes 1572872 | tf_op jit(solution)/shard_map/ppermute | solution.py:14
  38.4 7.0 %collective-permute-start.2 = (bf16[16,32,512]{2,1,0:T(8,128)(2,1)S(1)}, bf16[16,32,512]{2,1,0:T(8,128)(2,1)S(1)}, u32[]{:S(2)}, u32[]{:S(2)}) collective-permute-start(bf16[16,32,512]{2,1,0:T(8,128)(2,1)S(1)} %convolution_convert_fusion.1), channel_id=1, source_target_pairs={{0,24},{8,32},{16,40},{24,48},{32,56},{40,64},{48,72},{56,80},{64,... | collective-permute-start | bytes 1572872 | tf_op jit(solution)/shard_map/ppermute | solution.py:14
  45.4 0.1 convert_reduce_fusion
  45.6 2.8 collective-permute-start.5
  48.4 2.5 collective-permute-start.4
  51.0 1.3 dynamic-slice
  52.9 9.4 %collective-permute-done = bf16[16,32,512]{2,1,0:T(8,128)(2,1)S(1)} collective-permute-done((bf16[16,32,512]{2,1,0:T(8,128)(2,1)S(1)}, bf16[16,32,512]{2,1,0:T(8,128)(2,1)S(1)}, u32[]{:S(2)}, u32[]{:S(2)}) %collective-permute-start) | collective-permute-done | bytes 524320 | tf_op jit(solution)/shard_map/ppermute | solution.py:14
  62.3 1.9 collective-permute-start.3
  64.2 0.1 multiply_reduce_fusion
  64.4 12.0 %collective-permute-done.1 = bf16[16,32,512]{2,1,0:T(8,128)(2,1)S(1)} collective-permute-done((bf16[16,32,512]{2,1,0:T(8,128)(2,1)S(1)}, bf16[16,32,512]{2,1,0:T(8,128)(2,1)S(1)}, u32[]{:S(2)}, u32[]{:S(2)}) %collective-permute-start.1) | collective-permute-done | bytes 524320 | tf_op jit(solution)/shard_map/ppermute | solution.py:14
  76.4 0.1 multiply_reduce_fusion.1
  76.5 10.1 %collective-permute-done.2 = bf16[16,32,512]{2,1,0:T(8,128)(2,1)S(1)} collective-permute-done((bf16[16,32,512]{2,1,0:T(8,128)(2,1)S(1)}, bf16[16,32,512]{2,1,0:T(8,128)(2,1)S(1)}, u32[]{:S(2)}, u32[]{:S(2)}) %collective-permute-start.2) | collective-permute-done | bytes 524320 | tf_op jit(solution)/shard_map/ppermute | solution.py:14
  86.6 0.0 copy-done.1
  86.6 1.2 fusion.10
  87.8 0.0 all-reduce.11.cloned.1.call-update
  87.9 0.0 collective-permute-done.5
  87.9 0.1 fusion.43
  88.0 17.1 %collective-permute-done.4 = bf16[16,32]{1,0:T(8,128)(2,1)S(1)} collective-permute-done((bf16[16,32]{1,0:T(8,128)(2,1)S(1)}, bf16[16,32]{1,0:T(8,128)(2,1)S(1)}, u32[]{:S(2)}, u32[]{:S(2)}) %collective-permute-start.4) | collective-permute-done | bytes 1056 | tf_op jit(solution)/shard_map/ppermute | solution.py:14
  105.0 0.1 fusion.44
  105.1 5.0 %collective-permute-done.3 = bf16[16,32]{1,0:T(8,128)(2,1)S(1)} collective-permute-done((bf16[16,32]{1,0:T(8,128)(2,1)S(1)}, bf16[16,32]{1,0:T(8,128)(2,1)S(1)}, u32[]{:S(2)}, u32[]{:S(2)}) %collective-permute-start.3) | collective-permute-done | bytes 1056 | tf_op jit(solution)/shard_map/ppermute | solution.py:14
  110.2 0.1 fusion.45
  110.3 0.3 fusion.8
  110.6 122.4 %all-reduce.7 = f32[512]{0:T(512)S(1)} all-reduce(f32[512]{0:T(512)S(1)} %bitcast.12), channel_id=3, replica_groups=mesh['bl'=64,'ta'=8] {'bl'}, use_global_device_ids=true, to_apply=%region_9.10.clone | all-reduce | flops 512 | bytes 4096
  233.0 0.1 dynamic-slice.3
  233.1 39.0 %all-reduce.11.cloned.1.call-done = f32[512,256]{1,0:T(8,128)} async-done(((f32[512,256]{1,0:T(8,128)}), f32[512,256]{1,0:T(8,128)}) %all-reduce.11.cloned.1.call-update) | async-done | bytes 524304
  272.0 0.7 constant_dynamic-slice_fusion
  272.7 17.0 %all-reduce.8 = (f32[8,256]{1,0:T(8,128)S(1)}, f32[8]{0:T(128)S(1)}) all-reduce(f32[8,256]{1,0:T(8,128)S(1)} %constant_dynamic-slice_fusion, f32[8]{0:T(128)S(1)} %dynamic-slice.3), channel_id=1, replica_groups=mesh['bl'=64,'ta'=8] {'ta'}, use_global_device_ids=true, to_apply=%region_4.5 | all-reduce | flops 2056 | bytes 16448 | tf_op jit(solution)/shard_map/psum | solution.py:44
  289.8 0.7 broadcast_divide_fusion
  (9 shorter events, 0.1 us)
Async XLA Ops:
  6.5 265.5 %all-reduce.11.cloned.1.call-start = ((), (), s32[]{:S(2)}) async-start(), calls=%async_computation | async-start | bytes 1048576
  18.1 6.6 %copy-start.2 = (s32[256]{0:T(256)S(1)}, s32[256]{0:T(256)}, u32[]{:S(2)}) copy-start(s32[256]{0:T(256)} %param.8) | copy-start | bytes 3076
  18.1 6.6 %copy-start = (s32[16,256]{1,0:T(8,128)S(1)}, s32[16,256]{1,0:T(8,128)}, u32[]{:S(2)}) copy-start(s32[16,256]{1,0:T(8,128)} %param.7) | copy-start | bytes 49156
  24.7 61.9 %copy-start.1 = (s32[512]{0:T(512)S(1)}, s32[512]{0:T(512)}, u32[]{:S(2)}) copy-start(s32[512]{0:T(512)} %param.9) | copy-start | bytes 6148
  27.7 34.6 %collective-permute-start = (bf16[16,32,512]{2,1,0:T(8,128)(2,1)S(1)}, bf16[16,32,512]{2,1,0:T(8,128)(2,1)S(1)}, u32[]{:S(2)}, u32[]{:S(2)}) collective-permute-start(bf16[16,32,512]{2,1,0:T(8,128)(2,1)S(1)} %convolution_convert_fusion.1), channel_id=1, source_target_pairs={{0,8},{8,16},{16,24},{24,32},{32,40},{40,48},{48,56},{56,64},{64,7... | collective-permute-start | bytes 1572872 | tf_op jit(solution)/shard_map/ppermute | solution.py:14
  32.6 43.8 %collective-permute-start.1 = (bf16[16,32,512]{2,1,0:T(8,128)(2,1)S(1)}, bf16[16,32,512]{2,1,0:T(8,128)(2,1)S(1)}, u32[]{:S(2)}, u32[]{:S(2)}) collective-permute-start(bf16[16,32,512]{2,1,0:T(8,128)(2,1)S(1)} %convolution_convert_fusion.1), channel_id=1, source_target_pairs={{0,16},{8,24},{16,32},{24,40},{32,48},{40,56},{48,64},{56,72},{64,... | collective-permute-start | bytes 1572872 | tf_op jit(solution)/shard_map/ppermute | solution.py:14
  38.4 48.1 %collective-permute-start.2 = (bf16[16,32,512]{2,1,0:T(8,128)(2,1)S(1)}, bf16[16,32,512]{2,1,0:T(8,128)(2,1)S(1)}, u32[]{:S(2)}, u32[]{:S(2)}) collective-permute-start(bf16[16,32,512]{2,1,0:T(8,128)(2,1)S(1)} %convolution_convert_fusion.1), channel_id=1, source_target_pairs={{0,24},{8,32},{16,40},{24,48},{32,56},{40,64},{48,72},{56,80},{64,... | collective-permute-start | bytes 1572872 | tf_op jit(solution)/shard_map/ppermute | solution.py:14
  45.6 42.3 %collective-permute-start.5 = (bf16[16,32]{1,0:T(8,128)(2,1)S(1)}, bf16[16,32]{1,0:T(8,128)(2,1)S(1)}, u32[]{:S(2)}, u32[]{:S(2)}) collective-permute-start(bf16[16,32]{1,0:T(8,128)(2,1)S(1)} %convert_element_type.70), channel_id=1, source_target_pairs={{0,24},{8,32},{16,40},{24,48},{32,56},{40,64},{48,72},{56,80},{64,... | collective-permute-start | bytes 3080 | tf_op jit(solution)/shard_map/ppermute | solution.py:14
  48.4 56.6 %collective-permute-start.4 = (bf16[16,32]{1,0:T(8,128)(2,1)S(1)}, bf16[16,32]{1,0:T(8,128)(2,1)S(1)}, u32[]{:S(2)}, u32[]{:S(2)}) collective-permute-start(bf16[16,32]{1,0:T(8,128)(2,1)S(1)} %convert_element_type.70), channel_id=1, source_target_pairs={{0,16},{8,24},{16,32},{24,40},{32,48},{40,56},{48,64},{56,72},{64,... | collective-permute-start | bytes 3080 | tf_op jit(solution)/shard_map/ppermute | solution.py:14
  62.3 47.9 %collective-permute-start.3 = (bf16[16,32]{1,0:T(8,128)(2,1)S(1)}, bf16[16,32]{1,0:T(8,128)(2,1)S(1)}, u32[]{:S(2)}, u32[]{:S(2)}) collective-permute-start(bf16[16,32]{1,0:T(8,128)(2,1)S(1)} %convert_element_type.70), channel_id=1, source_target_pairs={{0,8},{8,16},{16,24},{24,32},{32,40},{40,48},{48,56},{56,64},{64,7... | collective-permute-start | bytes 3080 | tf_op jit(solution)/shard_map/ppermute | solution.py:14
Sparse Core Ops, SparseCore 0:
  88.0 183.9 all-reduce.10
where the time goes:
time: 298 us; the launch traced here: 297 us
  blocking collectives  139 us (47%)
  waiting for transfers between devices  92.6 us (31%)
  starting transfers between devices  25 us (8%)
  matrix products  16.1 us (5%)
  between operations  14.2 us (5%)
  local copies, waits for them, and re-layouts  8.62 us (3%)
    unnamed x1, blocking collectives  122 us
    ppermute x6, waiting for transfers between devices, from_behind(): lax.ppermute(shard, axis, [(i, (i + by) % devices) for i in range(devices)])  53.6 us
    unnamed x2, waiting for transfers between devices  39 us
    ppermute x6, starting transfers between devices, from_behind(): lax.ppermute(shard, axis, [(i, (i + by) % devices) for i in range(devices)])  25 us
    psum x1, blocking collectives, over_time(): return lax.psum((owned_rows, counts), 'ta')  17 us
    reshape x1, local copies, waits for them, and re-layouts, on_device(): delays.astype(jnp.bfloat16).reshape(time_count, block_length, row_width)  6.56 us
    dot_general x1, matrix products, on_device(): jnp.dot(visibilities.reshape(time_count * block_length, row_width), matri...  6.49 us
  transfers between devices with their start and end apart: 7, of which 6 were waited for; matrix products, arithmetic and copies ran while one was open for 1% of the time, Pallas kernels for 0%

commit v1 on v0

v1 whole, which is shorter than its diff:
```python
import math

import numpy as np
import jax
import jax.numpy as jnp
from jax import lax
from jax.sharding import PartitionSpec as P

GR_DEV = 8
SPAN = 4


def shifted(shard, axis, by):
    devices = lax.axis_size(axis)
    return lax.ppermute(shard, axis, [(i, (i + by) % devices) for i in range(devices)])


def fourier_tables(channels):
    ramp = np.arange(channels)
    angles = 2.0 * math.pi / channels * (ramp[:, None] * ramp[None, :] % channels)
    norm_factor = 1.0 / math.sqrt(channels)
    return (np.cos(angles) * norm_factor).astype(np.float32), (np.sin(angles) * norm_factor).astype(np.float32)


def transform_matrix(taper, inv_cov):
    cosines, sines = fourier_tables(taper.shape[0])
    weighted = taper[:, None] * inv_cov
    both = jnp.dot(
        weighted,
        jnp.asarray(np.concatenate([cosines, sines], axis=1)),
        precision=lax.Precision.HIGHEST,
        preferred_element_type=jnp.float32,
    )
    channels = taper.shape[0]
    cos_part, sin_part = both[:, :channels], both[:, channels:]
    upper_half = jnp.concatenate([cos_part, -sin_part], axis=1)
    lower_half = jnp.concatenate([sin_part, cos_part], axis=1)
    return jnp.concatenate([upper_half, lower_half], axis=0).astype(jnp.bfloat16)


def on_device(visibilities, flags, group_ids, group_order, taper, inv_cov):
    channels = taper.shape[0]
    device_index = lax.axis_index("bl")
    block_total = lax.axis_size("bl")
    time_count, block_length, row_width = visibilities.shape
    slot_count = SPAN * GR_DEV

    slot_index = (device_index - group_ids // GR_DEV) % block_total * GR_DEV + group_ids % GR_DEV
    onehot = slot_index[None, :] == jnp.arange(slot_count, dtype=jnp.int32)[:, None]
    group_table = jnp.where(onehot[None], flags[:, None, :], 0).astype(jnp.bfloat16)
    grouped = jnp.einsum(
        "tsb,tbc->tsc", group_table, visibilities, preferred_element_type=jnp.float32
    ).astype(jnp.bfloat16)
    counts = jnp.sum(group_table.astype(jnp.float32), axis=-1)
    count_rows = jnp.pad(counts.T.astype(jnp.bfloat16), ((0, 0), (0, row_width - time_count)))
    wire = jnp.concatenate([grouped, count_rows[None]], axis=0)

    slabs = [wire[:, k * GR_DEV : (k + 1) * GR_DEV] for k in range(SPAN)]
    far_behind = shifted(slabs[3], "bl", -2)
    behind = shifted(slabs[2], "bl", -1)
    ahead = shifted(slabs[0], "bl", 1)
    parts = [ahead, slabs[1], behind, far_behind]

    matrix = transform_matrix(taper, inv_cov)
    delays = [
        jnp.dot(
            part[:time_count].reshape(time_count * GR_DEV, row_width),
            matrix,
            preferred_element_type=jnp.float32,
        )
        for part in parts
    ]
    part_counts = [part[time_count, :, :time_count].astype(jnp.float32) for part in parts]

    def pair_sum(values):
        before = values[0]
        pairs = values[1] * before
        for value, earlier in ((values[2], values[1]), (values[3], values[2])):
            before = before + earlier
            pairs = pairs + value * before
        return pairs

    power = jnp.sum(pair_sum(delays).reshape(time_count, GR_DEV, row_width), axis=0)
    power = power[:, :channels] + power[:, channels:]
    pair_count = jnp.sum(pair_sum(part_counts), axis=1)
    power, pair_count = lax.psum((power, pair_count), "ta")
    spectrum = power / jnp.maximum(pair_count, 1.0)[:, None]

    table = lax.all_gather(spectrum, "bl", axis=0, tiled=True)
    wanted = lax.dynamic_slice_in_dim(group_order, device_index * GR_DEV, GR_DEV, 0)
    rows = (wanted // GR_DEV + 1) % block_total * GR_DEV + wanted % GR_DEV
    pick = (rows[:, None] == jnp.arange(table.shape[0], dtype=jnp.int32)[None, :]).astype(jnp.float32)
    return jnp.dot(pick, table, precision=lax.Precision.HIGHEST, preferred_element_type=jnp.float32)


def solution(mesh):
    return jax.shard_map(
        on_device,
        mesh=mesh,
        in_specs=(P("ta", "bl", None), P("ta", "bl"), P("bl"), P(), P(), P()),
        out_specs=P("bl", None),
        check_vma=False,
    )
```

time: 298 us -> 93.6 us (0.31)
  the two profiles are of different devices: /device:TPU:1 before, /device:TPU:8 now
where the time goes in v1:
time: 93.6 us; the launch traced here: 93.2 us
  blocking collectives  64.1 us (68%)
  starting transfers between devices  16.7 us (18%)
  matrix products  5.49 us (6%)
  waiting for transfers between devices  3.92 us (4%)
  other arithmetic  2.7 us (3%)
    all_gather x1, blocking collectives, on_device(): table = lax.all_gather(spectrum, 'bl', axis=0, tiled=True)  50.7 us
    ppermute x3, starting transfers between devices, shifted(): lax.ppermute(shard, axis, [(i, (i + by) % devices) for i in range(devices)])  16.7 us
    psum x1, blocking collectives, on_device(): power, pair_count = lax.psum((power, pair_count), 'ta')  13.4 us
    ppermute x3, waiting for transfers between devices, shifted(): lax.ppermute(shard, axis, [(i, (i + by) % devices) for i in range(devices)])  3.92 us
    dot_general x1, matrix products, on_device(): jnp.einsum('tsb,tbc->tsc', group_table, visibilities, preferred_element_t...  3.03 us
  transfers between devices with their start and end apart: 3, of which 1 were waited for; matrix products, arithmetic and copies ran while one was open for 2% of the time, Pallas kernels for 0%

profile of v1, /device:TPU:8, one launch (start us, length us, event | category | flops | bytes accessed | tf_op | source)
XLA Modules:
  0.0 93.2 jit_solution(10819614527837272543)
XLA Ops:
  0.0 0.0 copy-start
  0.0 0.0 copy-start.1
  0.0 0.0 copy-start.2
  0.0 0.8 fusion.20
  0.8 0.9 fusion.3
  1.7 0.1 copy.8
  1.8 3.0 %convolution_convert_fusion = bf16[16,32,512]{2,1,0:T(8,128)(2,1)S(1)} fusion(bf16[16,256,512]{2,1,0:T(8,128)(2,1)} %param.7, s32[16,256]{1,0:T(8,128)} %param.8, pred[32,256]{1,0:T(8,128)(4,1)S(1)} %iota_compare_fusion), kind=kOutput, calls=%fused_computation | convolution fusion | flops 134742016 | bytes 4743168 | tf_op jit(solution)/shard_map/tsb,tbc->tsc/dot_general | solution.py:51
  4.9 10.8 %collective-permute-start.2 = (bf16[17,8,512]{2,1,0:T(8,128)(2,1)S(1)}, bf16[17,8,512]{2,1,0:T(8,128)(2,1)S(1)}, u32[]{:S(2)}, u32[]{:S(2)}) collective-permute-start(bf16[17,8,512]{2,1,0:T(8,128)(2,1)S(1)} %get-tuple-element.7), channel_id=1, source_target_pairs={{0,496},{8,504},{16,0},{24,8},{32,16},{40,24},{48,32},{56,40},{64,... | collective-permute-start | bytes 417800 | tf_op jit(solution)/shard_map/ppermute | solution.py:15
  15.7 2.5 %collective-permute-start.1 = (bf16[17,8,512]{2,1,0:T(8,128)(2,1)S(1)}, bf16[17,8,512]{2,1,0:T(8,128)(2,1)S(1)}, u32[]{:S(2)}, u32[]{:S(2)}) collective-permute-start(bf16[17,8,512]{2,1,0:T(8,128)(2,1)S(1)} %get-tuple-element.8), channel_id=1, source_target_pairs={{0,504},{8,0},{16,8},{24,16},{32,24},{40,32},{48,40},{56,48},{64,5... | collective-permute-start | bytes 417800 | tf_op jit(solution)/shard_map/ppermute | solution.py:15
  18.2 3.4 %collective-permute-start = (bf16[17,8,512]{2,1,0:T(8,128)(2,1)S(1)}, bf16[17,8,512]{2,1,0:T(8,128)(2,1)S(1)}, u32[]{:S(2)}, u32[]{:S(2)}) collective-permute-start(bf16[17,8,512]{2,1,0:T(8,128)(2,1)S(1)} %get-tuple-element.9), channel_id=1, source_target_pairs={{0,8},{8,16},{16,24},{24,32},{32,40},{40,48},{48,56},{56,64},{64,7... | collective-permute-start | bytes 417800 | tf_op jit(solution)/shard_map/ppermute | solution.py:15
  21.5 0.0 copy-done
  21.6 0.0 copy-done.1
  21.6 0.0 copy-done.2
  21.6 0.6 fusion.4
  22.3 0.2 fusion.11
  22.5 0.8 fusion.22
  23.3 3.9 %collective-permute-done = bf16[17,8,512]{2,1,0:T(8,128)(2,1)S(1)} collective-permute-done((bf16[17,8,512]{2,1,0:T(8,128)(2,1)S(1)}, bf16[17,8,512]{2,1,0:T(8,128)(2,1)S(1)}, u32[]{:S(2)}, u32[]{:S(2)}) %collective-permute-start) | collective-permute-done | bytes 139296 | tf_op jit(solution)/shard_map/ppermute | solution.py:15
  27.2 0.2 fusion.10
  27.4 0.0 collective-permute-done.1
  27.5 0.2 fusion.9
  27.7 0.0 collective-permute-done.2
  27.7 0.2 fusion.2
  28.0 0.1 fusion.17
  28.1 13.4 %all-reduce.1 = (f32[8,256]{1,0:T(8,128)S(1)}, f32[8]{0:T(128)S(1)}) all-reduce(f32[8,256]{1,0:T(8,128)S(1)} %slice_add_fusion, f32[8]{0:T(128)S(1)} %fusion.17), channel_id=1, replica_groups=mesh['bl'=64,'ta'=8] {'ta'}, use_global_device_ids=true, to_apply=%region_2.3 | all-reduce | flops 2056 | bytes 16448 | tf_op jit(solution)/shard_map/psum | solution.py:86
  41.5 0.1 broadcast_divide_fusion
  41.6 50.7 %all_gather.3 = f32[512,256]{1,0:T(8,128)S(1)} all-gather(f32[8,256]{1,0:T(8,128)S(1)} %broadcast_divide_fusion), channel_id=1, replica_groups=mesh['bl'=64,'ta'=8] {'bl'}, dimensions={0}, use_global_device_ids=true | all-gather | bytes 532480 | tf_op jit(solution)/shard_map/all_gather | solution.py:89
  92.3 0.9 fusion.13
  (7 shorter events, 0.1 us)
Async XLA Ops:
  0.0 21.5 %copy-start = (f32[256,512]{1,0:T(8,128)S(1)}, f32[256,512]{1,0:T(8,128)}, u32[]{:S(2)}) copy-start(f32[256,512]{1,0:T(8,128)} %constant.82.clone) | copy-start | bytes 1572868
  0.0 21.6 %copy-start.1 = (f32[256,256]{1,0:T(8,128)S(1)}, f32[256,256]{1,0:T(8,128)}, u32[]{:S(2)}) copy-start(f32[256,256]{1,0:T(8,128)} %param.12) | copy-start | bytes 786436
  0.0 21.6 %copy-start.2 = (f32[256]{0:T(256)S(1)}, f32[256]{0:T(256)}, u32[]{:S(2)}) copy-start(f32[256]{0:T(256)} %param.11) | copy-start | bytes 3076
  4.9 22.8 %collective-permute-start.2 = (bf16[17,8,512]{2,1,0:T(8,128)(2,1)S(1)}, bf16[17,8,512]{2,1,0:T(8,128)(2,1)S(1)}, u32[]{:S(2)}, u32[]{:S(2)}) collective-permute-start(bf16[17,8,512]{2,1,0:T(8,128)(2,1)S(1)} %get-tuple-element.7), channel_id=1, source_target_pairs={{0,496},{8,504},{16,0},{24,8},{32,16},{40,24},{48,32},{56,40},{64,... | collective-permute-start | bytes 417800 | tf_op jit(solution)/shard_map/ppermute | solution.py:15
  15.7 11.8 %collective-permute-start.1 = (bf16[17,8,512]{2,1,0:T(8,128)(2,1)S(1)}, bf16[17,8,512]{2,1,0:T(8,128)(2,1)S(1)}, u32[]{:S(2)}, u32[]{:S(2)}) collective-permute-start(bf16[17,8,512]{2,1,0:T(8,128)(2,1)S(1)} %get-tuple-element.8), channel_id=1, source_target_pairs={{0,504},{8,0},{16,8},{24,16},{32,24},{40,32},{48,40},{56,48},{64,5... | collective-permute-start | bytes 417800 | tf_op jit(solution)/shard_map/ppermute | solution.py:15
  18.2 9.1 %collective-permute-start = (bf16[17,8,512]{2,1,0:T(8,128)(2,1)S(1)}, bf16[17,8,512]{2,1,0:T(8,128)(2,1)S(1)}, u32[]{:S(2)}, u32[]{:S(2)}) collective-permute-start(bf16[17,8,512]{2,1,0:T(8,128)(2,1)S(1)} %get-tuple-element.9), channel_id=1, source_target_pairs={{0,8},{8,16},{16,24},{24,32},{32,40},{40,48},{48,56},{56,64},{64,7... | collective-permute-start | bytes 417800 | tf_op jit(solution)/shard_map/ppermute | solution.py:15

commit v2 on v1

v2 whole, which is shorter than its diff:
```python
import functools
import math

import numpy as np
import jax
import jax.numpy as jnp
from jax import lax
from jax.experimental import pallas as pl
from jax.experimental.pallas import tpu as pltpu
from jax.sharding import Mesh
from jax.sharding import PartitionSpec as P

GR_DEV = 8
HALF = GR_DEV // 2
SPAN = 4
LANES = 128
BLOCK_AXES = ("y", "z")
COUNT_ROWS = 16
STEP_TIMES = 4


def shifted(shard, by):
    devices = lax.axis_size(BLOCK_AXES)
    return lax.ppermute(shard, BLOCK_AXES, [(i, (i + by) % devices) for i in range(devices)])


def exchange(chunks, axis):
    return lax.all_to_all(chunks, axis, 0, 0, tiled=True)


def fourier_table(channels):
    ramp = np.arange(channels)
    angles = 2.0 * math.pi / channels * (ramp[:, None] * ramp[None, :] % channels)
    both = np.concatenate([np.cos(angles), np.sin(angles)], axis=1) / math.sqrt(channels)
    return both.astype(np.float32)


def transform_parts(taper, inv_cov):
    weighted = taper[:, None] * inv_cov
    both = jnp.dot(
        weighted,
        jnp.asarray(fourier_table(taper.shape[0])),
        precision=lax.Precision.HIGHEST,
        preferred_element_type=jnp.float32,
    )
    return both.astype(jnp.bfloat16)


def rolled(rows):
    return jnp.concatenate([rows[HALF:], rows[:HALF]], axis=0)


def group_kernel(block_total, where_ref, ids_ref, flags_ref, vis_ref, a_ref, b_ref, c_ref, d1_ref, d2_ref, cnt_ref):
    step = pl.program_id(0)
    row_width = vis_ref.shape[2]
    ids = ids_ref[...]
    back = where_ref[0] - (ids >> 3)
    back = jnp.where(back < 0, back + block_total, back)
    member = ids & (GR_DEV - 1)
    block = (back - (member >= HALF).astype(jnp.int32)) & (SPAN - 1)
    row = lax.broadcasted_iota(jnp.int32, (SPAN * GR_DEV, ids.shape[1]), 0)
    even = (row == block * GR_DEV + member).astype(jnp.float32)
    odd = (row == block * GR_DEV + (member ^ HALF)).astype(jnp.float32)
    lane = lax.broadcasted_iota(jnp.int32, (SPAN * GR_DEV, LANES), 1)

    @pl.when(step == 0)
    def _():
        cnt_ref[...] = jnp.zeros_like(cnt_ref)

    sums = []
    counts = cnt_ref[...]
    for i in range(STEP_TIMES):
        flag = flags_ref[pl.ds(step * STEP_TIMES + i, 1), :].astype(jnp.float32)
        table = (odd if i % 2 else even) * flag
        sums.append(jnp.dot(table.astype(jnp.bfloat16), vis_ref[i], preferred_element_type=jnp.float32))
        total = jnp.sum(table, axis=1, keepdims=True)
        counts = jnp.where(lane == step * STEP_TIMES + i, total, counts)
    cnt_ref[...] = counts
    rows = pl.ds(pl.multiple_of(step * (STEP_TIMES * GR_DEV), STEP_TIMES * GR_DEV), STEP_TIMES * GR_DEV)
    for block_index, ref in enumerate((a_ref, b_ref, c_ref)):
        span = slice(block_index * GR_DEV, (block_index + 1) * GR_DEV)
        ref[rows, :] = jnp.concatenate([s[span] for s in sums], axis=0).astype(jnp.bfloat16)
    low = lax.broadcasted_iota(jnp.int32, (GR_DEV, row_width), 0) < HALF
    last = [s[3 * GR_DEV :] for s in sums]
    pairs = [(last[i], last[i + 1]) for i in range(0, STEP_TIMES, 2)]
    half_rows = pl.ds(pl.multiple_of(step * (STEP_TIMES * HALF), STEP_TIMES * HALF), STEP_TIMES * HALF)
    d1_ref[half_rows, :] = jnp.concatenate([jnp.where(low, x, y) for x, y in pairs], axis=0).astype(jnp.bfloat16)
    d2_ref[half_rows, :] = jnp.concatenate([jnp.where(low, y, x) for x, y in pairs], axis=0).astype(jnp.bfloat16)

    @pl.when(step == pl.num_programs(0) - 1)
    def _():
        for block_index, ref in enumerate((a_ref, b_ref, c_ref, d1_ref, d2_ref)):
            first = min(block_index, SPAN - 1) * GR_DEV
            mine = counts[first : first + GR_DEV]
            tile = jnp.concatenate([mine, jnp.zeros_like(mine)], axis=0)
            tile = jnp.concatenate([tile, jnp.zeros((COUNT_ROWS, row_width - LANES), jnp.float32)], axis=1)
            ref[ref.shape[0] - COUNT_ROWS :, :] = tile.astype(jnp.bfloat16)


def group_sums(visibilities, flags, group_ids, device_index, block_total):
    time_count, block_length, row_width = visibilities.shape
    full = time_count * GR_DEV + COUNT_ROWS
    part = time_count * HALF + COUNT_ROWS
    shapes = [full, full, full, part, part]
    return pl.pallas_call(
        functools.partial(group_kernel, block_total),
        grid_spec=pltpu.PrefetchScalarGridSpec(
            num_scalar_prefetch=1,
            grid=(time_count // STEP_TIMES,),
            in_specs=[
                pl.BlockSpec((1, block_length), lambda i, s: (0, 0)),
                pl.BlockSpec((time_count, block_length), lambda i, s: (0, 0)),
                pl.BlockSpec((STEP_TIMES, block_length, row_width), lambda i, s: (i, 0, 0)),
            ],
            out_specs=[pl.BlockSpec((n, row_width), lambda i, s: (0, 0)) for n in shapes],
            scratch_shapes=[pltpu.VMEM((SPAN * GR_DEV, LANES), jnp.float32)],
        ),
        out_shape=[jax.ShapeDtypeStruct((n, row_width), jnp.bfloat16) for n in shapes],
        compiler_params=pltpu.CompilerParams(vmem_limit_bytes=57 << 20),
        cost_estimate=pl.CostEstimate(
            flops=2 * time_count * SPAN * GR_DEV * block_length * row_width,
            bytes_accessed=visibilities.size * 2,
            transcendentals=0,
        ),
        name="group_sums",
    )(device_index[None], group_ids[None, :], flags, visibilities)


def pair_sum(a, b, c, d):
    return b * a + c * (a + b) + d * (a + b + c)


def power_kernel(parts_ref, a_ref, b_ref, c_ref, d1_ref, d2_ref, out_ref):
    channels = parts_ref.shape[0]
    time_count = (a_ref.shape[0] - COUNT_ROWS) // GR_DEV
    cosines = parts_ref[:, :channels]
    sines = parts_ref[:, channels:]

    def dot(x, y):
        return jnp.dot(x, y, preferred_element_type=jnp.float32)

    def delays(ref):
        rows = ref.shape[0] - COUNT_ROWS
        re, im = ref[:rows, :channels], ref[:rows, channels:]
        return dot(re, cosines) + dot(im, sines), dot(im, cosines) - dot(re, sines)

    low = lax.broadcasted_iota(jnp.int32, (GR_DEV, channels), 0) < HALF
    power = [jnp.zeros((GR_DEV, channels), jnp.float32) for _ in range(2)]
    for a, b, c, d1, d2 in zip(*(delays(ref) for ref in (a_ref, b_ref, c_ref, d1_ref, d2_ref))):
        for t in range(time_count):
            at = slice(t * GR_DEV, (t + 1) * GR_DEV)
            half_at = slice(t // 2 * GR_DEV, (t // 2 + 1) * GR_DEV)
            first, second = (d2, d1) if t % 2 else (d1, d2)
            d = jnp.where(low, first[half_at], second[half_at])
            power[t % 2] = power[t % 2] + pair_sum(a[at], b[at], c[at], d)
    power = power[0] + rolled(power[1])

    counts = []
    for ref in (a_ref, b_ref, c_ref, d1_ref, d2_ref):
        first = ref.shape[0] - COUNT_ROWS
        counts.append(ref[first:, :LANES].astype(jnp.float32)[:GR_DEV])
    row = lax.broadcasted_iota(jnp.int32, (GR_DEV, LANES), 0)
    even = lax.broadcasted_iota(jnp.int32, (GR_DEV, LANES), 1) % 2 == 0
    d = jnp.where((row < HALF) == even, counts[3], counts[4])
    pairs = pair_sum(counts[0], counts[1], counts[2], d)
    pairs = jnp.where(even, pairs, 0.0) + rolled(jnp.where(even, 0.0, pairs))
    count = jnp.broadcast_to(jnp.sum(pairs, axis=1, keepdims=True), (GR_DEV, LANES))
    rows = jnp.concatenate([power, count], axis=1)
    for copy in range(out_ref.shape[0]):
        out_ref[copy] = rows


def power_rows(parts, blocks, copies):
    channels = parts.shape[0]
    rows = sum(block.shape[0] - COUNT_ROWS for block in blocks)
    return pl.pallas_call(
        power_kernel,
        out_shape=jax.ShapeDtypeStruct((copies, GR_DEV, channels + LANES), jnp.float32),
        compiler_params=pltpu.CompilerParams(vmem_limit_bytes=16 << 20),
        cost_estimate=pl.CostEstimate(flops=8 * rows * channels * channels, bytes_accessed=2 << 20, transcendentals=0),
        name="power_rows",
    )(parts, *blocks)


def spectrum_kernel(in_ref, out_ref):
    channels = out_ref.shape[2]
    total = in_ref[0]
    for source in range(1, in_ref.shape[0]):
        total = total + in_ref[source]
    count = jnp.maximum(total[:, channels:], 1.0)
    count = jnp.concatenate([count] * (channels // LANES), axis=1)
    spectrum = total[:, :channels] / count
    for copy in range(out_ref.shape[0]):
        out_ref[copy] = spectrum


def spectrum_rows(partial_rows, channels, copies):
    return pl.pallas_call(
        spectrum_kernel,
        out_shape=jax.ShapeDtypeStruct((copies, GR_DEV, channels), jnp.float32),
        name="spectrum_rows",
    )(partial_rows)


def on_device(visibilities, flags, group_ids, group_order, taper, inv_cov):
    channels = taper.shape[0]
    y_size, z_size = lax.axis_size("y"), lax.axis_size("z")
    block_total = y_size * z_size
    device_index = lax.axis_index(BLOCK_AXES)

    a, b, c, d1, d2 = group_sums(visibilities, flags, group_ids, device_index, block_total)
    d1, d2 = shifted(d1, -2), shifted(d2, 2)
    c, a = shifted(c, -1), shifted(a, 1)
    parts = transform_parts(taper, inv_cov)
    rows = power_rows(parts, (a, b, c, d1, d2), lax.axis_size("ta"))

    spectrum = spectrum_rows(exchange(rows, "ta"), channels, z_size)

    plane = exchange(spectrum, "z").reshape(z_size * GR_DEV, channels)
    order = group_order.reshape(y_size, z_size, GR_DEV)
    wanted = lax.dynamic_index_in_dim(order, lax.axis_index("z"), 1, keepdims=False).reshape(-1)
    member = wanted % GR_DEV
    holder = (wanted // GR_DEV + jnp.where(member < HALF, 1, 2)) % block_total
    place = jnp.where(holder // z_size == lax.axis_index("y"), holder % z_size * GR_DEV + member, -1)
    pick = (place[:, None] == jnp.arange(z_size * GR_DEV, dtype=jnp.int32)[None, :]).astype(jnp.float32)
    chosen = jnp.dot(pick, plane, precision=lax.Precision.HIGHEST, preferred_element_type=jnp.float32)
    return jnp.sum(exchange(chosen.reshape(y_size, GR_DEV, channels), "y"), axis=0)


def solution(mesh):
    blocks, times = mesh.devices.shape
    y_size = 2 ** (int(math.log2(blocks)) // 2)
    cut = Mesh(mesh.devices.reshape(y_size, blocks // y_size, times), ("y", "z", "ta"))
    return jax.shard_map(
        on_device,
        mesh=cut,
        in_specs=(P("ta", BLOCK_AXES, None), P("ta", BLOCK_AXES), P(BLOCK_AXES), P(), P(), P()),
        out_specs=P(BLOCK_AXES, None),
        check_vma=False,
    )
```

time: 93.6 us -> 74.5 us (0.80)
  the two profiles are of different devices: /device:TPU:8 before, /device:TPU:1 now
where the time goes in v2:
time: 74.5 us; the launch traced here: 73.1 us
  starting transfers between devices  32.8 us (44%)
  waiting for transfers between devices  19.1 us (26%)
  blocking collectives  10.8 us (14%)
  Pallas kernels  7.14 us (10%)
  local copies, waits for them, and re-layouts  1.65 us (2%)
  matrix products  0.86 us (1%)
    ppermute x4, starting transfers between devices, shifted(): lax.ppermute(shard, BLOCK_AXES, [(i, (i + by) % devices) for i in range(d...  22.5 us
    all_to_all x2, waiting for transfers between devices, exchange(): return lax.all_to_all(chunks, axis, 0, 0, tiled=True)  12.2 us
    all_to_all x1, blocking collectives, exchange(): return lax.all_to_all(chunks, axis, 0, 0, tiled=True)  10.8 us
    all_to_all x2, starting transfers between devices, exchange(): return lax.all_to_all(chunks, axis, 0, 0, tiled=True)  10.3 us
    ppermute x4, waiting for transfers between devices, shifted(): lax.ppermute(shard, BLOCK_AXES, [(i, (i + by) % devices) for i in range(d...  6.88 us
    pallas_call x1, Pallas kernels, group_sums(): pl.pallas_call(functools.partial(group_kernel, block_total), grid_spec=pl...  4.39 us
    unnamed x12, local copies, waits for them, and re-layouts  1.56 us
    pallas_call x1, Pallas kernels, spectrum_rows(): pl.pallas_call(spectrum_kernel, out_shape=jax.ShapeDtypeStruct((copies, G...  1.55 us
  transfers between devices with their start and end apart: 6, of which 4 were waited for; matrix products, arithmetic and copies ran while one was open for 1% of the time, Pallas kernels for 0%

profile of v2, /device:TPU:1, one launch (start us, length us, event | category | flops | bytes accessed | tf_op | source)
XLA Modules:
  0.0 73.1 jit_solution(14354125168887929705)
XLA Ops:
  0.0 0.0 copy-start.1
  0.0 0.0 copy-start.5
  0.0 0.0 copy-start.3
  0.0 0.0 copy-start.4
  0.0 4.4 %group_sums.1 = (bf16[144,512]{1,0:T(8,128)(2,1)}, bf16[144,512]{1,0:T(8,128)(2,1)}, bf16[144,512]{1,0:T(8,128)(2,1)}, bf16[80,512]{1,0:T(8,128)(2,1)}, bf16[80,512]{1,0:T(8,128)(2,1)}) custom-call(s32[1]{0:T(128)} %bitcast.2.where_ref, s32[1,256]{1,0:T(1,128)} %bitcast.13, s32[16,256]{1,0:T(8,128)} %flags_ref.1, bf16[16,256,512]{2,1,0:T(8,128)(2,1)} %vis_ref.1), custom_call_target="tpu_custom_call" | custom-call | flops 134217728 | bytes 4194304 | tf_op jit(solution)/shard_map/group_sums/pallas_call | solution.py:105
  4.4 4.8 %collective-permute-start = (bf16[144,512]{1,0:T(8,128)(2,1)}, bf16[144,512]{1,0:T(8,128)(2,1)S(1)}, u32[]{:S(2)}, u32[]{:S(2)}) collective-permute-start(bf16[144,512]{1,0:T(8,128)(2,1)} %get-tuple-element.10), channel_id=1, source_target_pairs={{0,8},{8,16},{16,24},{24,32},{32,40},{40,48},{48,56},{56,64},{64,7... | collective-permute-start | bytes 442376 | tf_op jit(solution)/shard_map/ppermute | solution.py:24
  9.2 11.5 %collective-permute-start.1 = (bf16[144,512]{1,0:T(8,128)(2,1)}, bf16[144,512]{1,0:T(8,128)(2,1)S(1)}, u32[]{:S(2)}, u32[]{:S(2)}) collective-permute-start(bf16[144,512]{1,0:T(8,128)(2,1)} %get-tuple-element.12), channel_id=1, source_target_pairs={{0,504},{8,0},{16,8},{24,16},{32,24},{40,32},{48,40},{56,48},{64,5... | collective-permute-start | bytes 442376 | tf_op jit(solution)/shard_map/ppermute | solution.py:24
  20.7 3.4 %collective-permute-start.2 = (bf16[80,512]{1,0:T(8,128)(2,1)}, bf16[80,512]{1,0:T(8,128)(2,1)S(1)}, u32[]{:S(2)}, u32[]{:S(2)}) collective-permute-start(bf16[80,512]{1,0:T(8,128)(2,1)} %get-tuple-element.13), channel_id=1, source_target_pairs={{0,496},{8,504},{16,0},{24,8},{32,16},{40,24},{48,32},{56,40},{64,... | collective-permute-start | bytes 245768 | tf_op jit(solution)/shard_map/ppermute | solution.py:24
  24.1 2.8 %collective-permute-start.3 = (bf16[80,512]{1,0:T(8,128)(2,1)}, bf16[80,512]{1,0:T(8,128)(2,1)S(1)}, u32[]{:S(2)}, u32[]{:S(2)}) collective-permute-start(bf16[80,512]{1,0:T(8,128)(2,1)} %get-tuple-element.14), channel_id=1, source_target_pairs={{0,16},{8,24},{16,32},{24,40},{32,48},{40,56},{48,64},{56,72},{64,... | collective-permute-start | bytes 245768 | tf_op jit(solution)/shard_map/ppermute | solution.py:24
  26.9 0.0 copy-done.1
  27.0 0.0 copy-done.5
  27.0 0.0 copy-done.3
  27.0 0.6 convolution_convert_fusion.parts_ref
  27.6 0.0 copy-done.4
  27.6 0.1 reshape.127
  27.7 0.2 collective-permute-done.2.d1_ref
  27.9 6.7 %collective-permute-done.3.d2_ref = bf16[80,512]{1,0:T(8,128)(2,1)S(1)} collective-permute-done((bf16[80,512]{1,0:T(8,128)(2,1)}, bf16[80,512]{1,0:T(8,128)(2,1)S(1)}, u32[]{:S(2)}, u32[]{:S(2)}) %collective-permute-start.3) | collective-permute-done | bytes 81952 | tf_op jit(solution)/shard_map/ppermute | solution.py:24
  34.6 0.0 collective-permute-done.a_ref
  34.6 0.0 collective-permute-done.1.c_ref
  34.6 0.0 copy-start
  34.6 0.9 %copy-done = bf16[144,512]{1,0:T(8,128)(2,1)S(1)} copy-done((bf16[144,512]{1,0:T(8,128)(2,1)S(1)}, bf16[144,512]{1,0:T(8,128)(2,1)}, u32[]{:S(2)}) %copy-start) | copy-done | bytes 147480
  35.5 1.2 %power_rows.1 = f32[8,8,384]{2,1,0:T(8,128)} custom-call(bf16[256,512]{1,0:T(8,128)(2,1)S(1)} %convolution_convert_fusion.parts_ref, bf16[144,512]{1,0:T(8,128)(2,1)S(1)} %collective-permute-done.a_ref, bf16[144,512]{1,0:T(8,128)(2,1)S(1)} %copy-done, bf16[144,512]{1,0:T(8,128)(2,1)S(1)} %collective-permute-done.1.c_ref, ...), custom_call_target="tpu_custom_call" | custom-call | flops 268435456 | bytes 2097152 | tf_op jit(solution)/shard_map/power_rows/pallas_call | solution.py:176
  36.7 7.0 %all-to-all-start = ((f32[8,8,384]{2,1,0:T(8,128)}), f32[8,8,384]{2,1,0:T(8,128)S(1)}, u32[]{:S(2)}, u32[]{:S(2)}) async-start(f32[8,8,384]{2,1,0:T(8,128)} %power_rows.1), calls=%async_computation | async-start | bytes 196608 | tf_op jit(solution)/shard_map/all_to_all | solution.py:28
  43.7 5.0 %all-to-all-done.in_ref = f32[8,8,384]{2,1,0:T(8,128)S(1)} async-done(((f32[8,8,384]{2,1,0:T(8,128)}), f32[8,8,384]{2,1,0:T(8,128)S(1)}, u32[]{:S(2)}, u32[]{:S(2)}) %all-to-all-start) | async-done | bytes 98336 | tf_op jit(solution)/shard_map/all_to_all | solution.py:28
  48.7 0.0 copy-start.2
  48.7 0.6 copy-done.2
  49.3 1.5 %spectrum_rows.1 = f32[8,8,256]{2,1,0:T(8,128)} custom-call(f32[8,8,384]{2,1,0:T(8,128)} %copy-done.2), custom_call_target="tpu_custom_call" | custom-call | tf_op jit(solution)/shard_map/spectrum_rows/pallas_call | solution.py:198
  50.8 3.3 %all-to-all-start.1 = ((f32[8,8,256]{2,1,0:T(8,128)}), f32[8,8,256]{2,1,0:T(8,128)S(1)}, u32[]{:S(2)}, u32[]{:S(2)}) async-start(f32[8,8,256]{2,1,0:T(8,128)} %spectrum_rows.1), calls=%async_computation.1 | async-start | bytes 131072 | tf_op jit(solution)/shard_map/all_to_all | solution.py:28
  54.2 7.2 %all-to-all-done.1 = f32[8,8,256]{2,1,0:T(8,128)S(1)} async-done(((f32[8,8,256]{2,1,0:T(8,128)}), f32[8,8,256]{2,1,0:T(8,128)S(1)}, u32[]{:S(2)}, u32[]{:S(2)}) %all-to-all-start.1) | async-done | bytes 65568 | tf_op jit(solution)/shard_map/all_to_all | solution.py:28
  61.4 0.2 fusion.2
  61.7 10.8 %all_to_all.15 = f32[8,8,256]{2,1,0:T(8,128)S(1)} all-to-all(f32[8,8,256]{2,1,0:T(8,128)S(1)} %fusion.2), channel_id=1, replica_groups=mesh['y'=8,'z'=8,'ta'=8] {'y'}, dimensions={0} | all-to-all | bytes 131072 | tf_op jit(solution)/shard_map/all_to_all | solution.py:28
  72.5 0.6 reduce_sum.9
  (2 shorter events, 0.0 us)
Async XLA Ops:
  0.0 26.9 %copy-start.1 = (f32[256,512]{1,0:T(8,128)S(1)}, f32[256,512]{1,0:T(8,128)}, u32[]{:S(2)}) copy-start(f32[256,512]{1,0:T(8,128)} %constant.75.clone) | copy-start | bytes 1572868
  0.0 27.0 %copy-start.5 = (f32[256]{0:T(256)S(1)}, f32[256]{0:T(256)}, u32[]{:S(2)}) copy-start(f32[256]{0:T(256)} %param.11) | copy-start | bytes 3076
  0.0 27.0 %copy-start.3 = (f32[256,256]{1,0:T(8,128)S(1)}, f32[256,256]{1,0:T(8,128)}, u32[]{:S(2)}) copy-start(f32[256,256]{1,0:T(8,128)} %param.12) | copy-start | bytes 786436
  0.0 27.6 %copy-start.4 = (s32[512]{0:T(512)S(1)}, s32[512]{0:T(512)}, u32[]{:S(2)}) copy-start(s32[512]{0:T(512)} %param.10) | copy-start | bytes 6148
  4.4 30.2 %collective-permute-start = (bf16[144,512]{1,0:T(8,128)(2,1)}, bf16[144,512]{1,0:T(8,128)(2,1)S(1)}, u32[]{:S(2)}, u32[]{:S(2)}) collective-permute-start(bf16[144,512]{1,0:T(8,128)(2,1)} %get-tuple-element.10), channel_id=1, source_target_pairs={{0,8},{8,16},{16,24},{24,32},{32,40},{40,48},{48,56},{56,64},{64,7... | collective-permute-start | bytes 442376 | tf_op jit(solution)/shard_map/ppermute | solution.py:24
  9.2 25.3 %collective-permute-start.1 = (bf16[144,512]{1,0:T(8,128)(2,1)}, bf16[144,512]{1,0:T(8,128)(2,1)S(1)}, u32[]{:S(2)}, u32[]{:S(2)}) collective-permute-start(bf16[144,512]{1,0:T(8,128)(2,1)} %get-tuple-element.12), channel_id=1, source_target_pairs={{0,504},{8,0},{16,8},{24,16},{32,24},{40,32},{48,40},{56,48},{64,5... | collective-permute-start | bytes 442376 | tf_op jit(solution)/shard_map/ppermute | solution.py:24
  20.7 7.1 %collective-permute-start.2 = (bf16[80,512]{1,0:T(8,128)(2,1)}, bf16[80,512]{1,0:T(8,128)(2,1)S(1)}, u32[]{:S(2)}, u32[]{:S(2)}) collective-permute-start(bf16[80,512]{1,0:T(8,128)(2,1)} %get-tuple-element.13), channel_id=1, source_target_pairs={{0,496},{8,504},{16,0},{24,8},{32,16},{40,24},{48,32},{56,40},{64,... | collective-permute-start | bytes 245768 | tf_op jit(solution)/shard_map/ppermute | solution.py:24
  24.1 10.5 %collective-permute-start.3 = (bf16[80,512]{1,0:T(8,128)(2,1)}, bf16[80,512]{1,0:T(8,128)(2,1)S(1)}, u32[]{:S(2)}, u32[]{:S(2)}) collective-permute-start(bf16[80,512]{1,0:T(8,128)(2,1)} %get-tuple-element.14), channel_id=1, source_target_pairs={{0,16},{8,24},{16,32},{24,40},{32,48},{40,56},{48,64},{56,72},{64,... | collective-permute-start | bytes 245768 | tf_op jit(solution)/shard_map/ppermute | solution.py:24
  34.6 0.9 %copy-start = (bf16[144,512]{1,0:T(8,128)(2,1)S(1)}, bf16[144,512]{1,0:T(8,128)(2,1)}, u32[]{:S(2)}) copy-start(bf16[144,512]{1,0:T(8,128)(2,1)} %get-tuple-element.11.b_ref) | copy-start | bytes 442372
  36.7 11.9 %all-to-all-start = ((f32[8,8,384]{2,1,0:T(8,128)}), f32[8,8,384]{2,1,0:T(8,128)S(1)}, u32[]{:S(2)}, u32[]{:S(2)}) async-start(f32[8,8,384]{2,1,0:T(8,128)} %power_rows.1), calls=%async_computation | async-start | bytes 196608 | tf_op jit(solution)/shard_map/all_to_all | solution.py:28
  48.7 0.6 copy-start.2
  50.8 10.6 %all-to-all-start.1 = ((f32[8,8,256]{2,1,0:T(8,128)}), f32[8,8,256]{2,1,0:T(8,128)S(1)}, u32[]{:S(2)}, u32[]{:S(2)}) async-start(f32[8,8,256]{2,1,0:T(8,128)} %spectrum_rows.1), calls=%async_computation.1 | async-start | bytes 131072 | tf_op jit(solution)/shard_map/all_to_all | solution.py:28

commit v3 on v1

v3 whole, which is shorter than its diff:
```python
import functools
import math

import numpy as np
import jax
import jax.numpy as jnp
from jax import lax
from jax.experimental import pallas as pl
from jax.experimental.pallas import tpu as pltpu
from jax.sharding import Mesh
from jax.sharding import PartitionSpec as P

GR_DEV = 8
SPAN = 4
LANES = 128
BLOCK_AXES = ("y", "z")
COUNT_ROWS = 16
SLICE = 32
PACK = 4


def shifted(shard, by):
    devices = lax.axis_size(BLOCK_AXES)
    return lax.ppermute(shard, BLOCK_AXES, [(i, (i + by) % devices) for i in range(devices)])


def exchange(chunks, axis):
    return lax.all_to_all(chunks, axis, 0, 0, tiled=True)


def fourier_table(channels):
    ramp = np.arange(channels)
    angles = 2.0 * math.pi / channels * (ramp[:, None] * ramp[None, :] % channels)
    both = np.concatenate([np.cos(angles), np.sin(angles)], axis=1) / math.sqrt(channels)
    return both.astype(np.float32)


def exact_dot(x, y):
    return jnp.dot(x, y, precision=lax.Precision.HIGHEST, preferred_element_type=jnp.float32)


def transform_parts(taper, inv_cov):
    weighted = taper[:, None] * inv_cov
    return exact_dot(weighted, jnp.asarray(fourier_table(taper.shape[0]))).astype(jnp.bfloat16)


STEPS_BACK = (3, 2, 0, 1)


def group_kernel(block_total, place_ref, ids_ref, flags_ref, vis_ref, *rest):
    *refs, held_ref, sems = rest
    time_count, _, row_width = vis_ref.shape
    copies = [pltpu.make_async_copy(vis_ref.at[t], held_ref.at[t], sems.at[t]) for t in range(time_count)]
    for copy in copies:
        copy.start()
    ids = ids_ref[...]
    back = place_ref[0] - (ids >> 3)
    back = jnp.where(back < 0, back + block_total, back)
    row = lax.broadcasted_iota(jnp.int32, (SPAN * GR_DEV, ids.shape[1]), 0)
    onehot = (row == back * GR_DEV + (ids & (GR_DEV - 1))).astype(jnp.float32)
    lane = lax.broadcasted_iota(jnp.int32, (SPAN * GR_DEV, LANES), 1)
    counts = jnp.zeros((SPAN * GR_DEV, LANES), jnp.float32)
    pending = []
    for t in range(time_count):
        table = onehot * flags_ref[t : t + 1, :].astype(jnp.float32)
        counts = jnp.where(lane == t, jnp.sum(table, axis=1, keepdims=True), counts)
        copies[t].wait()
        pending.append(jnp.dot(table.astype(jnp.bfloat16), held_ref[t], preferred_element_type=jnp.float32))
        if len(pending) == 2:
            for block, ref in zip(STEPS_BACK, refs):
                span = slice(block * GR_DEV, (block + 1) * GR_DEV)
                both = jnp.concatenate([sums[span] for sums in pending], axis=0)
                ref[(t - 1) * GR_DEV : (t + 1) * GR_DEV, :] = both.astype(jnp.bfloat16)
            pending = []
    for block, ref in zip(STEPS_BACK, refs):
        mine = counts[block * GR_DEV : (block + 1) * GR_DEV]
        tile = jnp.concatenate([mine, jnp.zeros_like(mine)], axis=0)
        tile = jnp.concatenate([tile, jnp.zeros((COUNT_ROWS, row_width - LANES), jnp.float32)], axis=1)
        ref[time_count * GR_DEV :, :] = tile.astype(jnp.bfloat16)


def group_sums(visibilities, flags, group_ids, place, block_total):
    time_count, block_length, row_width = visibilities.shape
    shape = jax.ShapeDtypeStruct((time_count * GR_DEV + COUNT_ROWS, row_width), jnp.bfloat16)
    vmem = pl.BlockSpec(memory_space=pltpu.VMEM)
    return pl.pallas_call(
        functools.partial(group_kernel, block_total),
        in_specs=[pl.BlockSpec(memory_space=pltpu.SMEM), vmem, vmem, pl.BlockSpec(memory_space=pltpu.HBM)],
        out_specs=[vmem] * SPAN,
        out_shape=[shape] * SPAN,
        scratch_shapes=[
            pltpu.VMEM(visibilities.shape, visibilities.dtype),
            pltpu.SemaphoreType.DMA((time_count,)),
        ],
        compiler_params=pltpu.CompilerParams(vmem_limit_bytes=50 << 20),
        cost_estimate=pl.CostEstimate(
            flops=2 * time_count * SPAN * GR_DEV * block_length * row_width,
            bytes_accessed=visibilities.size * 2,
            transcendentals=0,
        ),
        name="group_sums",
    )(place, group_ids[None, :], flags, visibilities)


def pair_sum(a, b, c, d):
    return b * a + c * (a + b) + d * (a + b + c)


def lane_group(shape):
    return lax.broadcasted_iota(jnp.int32, shape, len(shape) - 1) // SLICE


def turned(rows, groups):
    return pltpu.roll(rows, groups % PACK * SLICE, 1) if groups % PACK else rows


def packed(rows, slice_index):
    group = lane_group(rows.shape)
    member = lax.broadcasted_iota(jnp.int32, rows.shape, 0) % PACK
    kept = jnp.zeros_like(rows)
    for b in range(PACK):
        kept = jnp.where((group == b) & (member == b), turned(rows, b - slice_index), kept)
    return jnp.concatenate(
        [jnp.sum(kept[a * PACK : (a + 1) * PACK], axis=0, keepdims=True) for a in range(2)], axis=0
    )


def power_kernel(parts_ref, d_ref, c_ref, a_ref, b_ref, out_ref):
    channels = parts_ref.shape[0]
    rows = a_ref.shape[0] - COUNT_ROWS
    slices = channels // SLICE
    cosines = parts_ref[:, :channels]
    sines = parts_ref[:, channels:]

    def dot(x, y):
        return jnp.dot(x, y, preferred_element_type=jnp.float32)

    def delays(ref):
        re, im = ref[:rows, :channels], ref[:rows, channels:]
        return dot(re, cosines) + dot(im, sines), dot(im, cosines) - dot(re, sines)

    blocks = [delays(ref) for ref in (a_ref, b_ref, c_ref, d_ref)]
    pairs = pair_sum(*(re for re, _ in blocks)) + pair_sum(*(im for _, im in blocks))
    power = jnp.sum(pairs.reshape(rows // GR_DEV, GR_DEV, channels), axis=0)
    counts = [ref[rows:, :LANES].astype(jnp.float32)[:GR_DEV] for ref in (a_ref, b_ref, c_ref, d_ref)]
    count = jnp.sum(pair_sum(*counts), axis=1, keepdims=True)
    count = packed(jnp.broadcast_to(count, (GR_DEV, LANES)), 0)
    for j in range(slices):
        half = power[:, j // PACK * LANES : (j // PACK + 1) * LANES]
        chunk = jnp.concatenate([packed(half, j % PACK), count], axis=0)
        for copy in range(out_ref.shape[0] // slices):
            out_ref[copy * slices + j] = chunk


def choose_kernel(times, spot_ref, in_ref, out_ref):
    spectrum = []
    for z in range(in_ref.shape[0] // times):
        total = in_ref[z * times]
        for time in range(1, times):
            total = total + in_ref[z * times + time]
        spectrum.append(total[:2] / jnp.maximum(total[2:], 1.0))
    spectrum = jnp.concatenate(spectrum, axis=0)
    first = lane_group(spectrum.shape) == 0
    rows = jnp.concatenate([jnp.where(first, turned(spectrum, -b), 0.0) for b in range(PACK)], axis=0)
    column = lax.broadcasted_iota(jnp.int32, (spot_ref.shape[0], rows.shape[0]), 1)
    pick = (spot_ref[...] == column).astype(jnp.float32)
    chosen = exact_dot(pick, rows)
    size = chosen.shape[0] // PACK
    chunks = turned(chosen[:size], 0)
    for b in range(1, PACK):
        chunks = chunks + turned(chosen[b * size : (b + 1) * size], b)
    copies = out_ref.shape[0] // (size // 2)
    for y in range(size // 2):
        for copy in range(copies):
            out_ref[y * copies + copy] = chunks[2 * y : 2 * y + 2]


def unpack_kernel(in_ref, out_ref):
    slices = out_ref.shape[1] // SLICE
    group = lane_group((GR_DEV, LANES))
    member = lax.broadcasted_iota(jnp.int32, (GR_DEV, LANES), 0) % PACK
    for half in range(slices // PACK):
        result = jnp.zeros((GR_DEV, LANES), jnp.float32)
        for k in range(PACK):
            j = half * PACK + k
            total = in_ref[j]
            for y in range(1, in_ref.shape[0] // slices):
                total = total + in_ref[y * slices + j]
            total = jnp.concatenate(
                [jnp.broadcast_to(total[a : a + 1], (PACK, LANES)) for a in range(2)], axis=0
            )
            for b in range(PACK):
                result = jnp.where((group == k) & (member == b), turned(total, k - b), result)
        out_ref[:, half * LANES : (half + 1) * LANES] = result


def small_call(kernel, shape, name):
    return pl.pallas_call(
        kernel,
        out_shape=jax.ShapeDtypeStruct(shape, jnp.float32),
        compiler_params=pltpu.CompilerParams(vmem_limit_bytes=16 << 20),
        name=name,
    )


def on_device(visibilities, flags, group_ids, group_order, taper, inv_cov):
    channels = taper.shape[0]
    y_size, z_size, times = (lax.axis_size(axis) for axis in ("y", "z", "ta"))
    block_total = y_size * z_size
    slices = channels // SLICE

    place = lax.axis_index(BLOCK_AXES)[None]
    d, c, a, b = group_sums(visibilities, flags, group_ids, place, block_total)
    d, c, a = shifted(d, -2), shifted(c, -1), shifted(a, 1)
    parts = transform_parts(taper, inv_cov)
    power = small_call(power_kernel, (z_size * slices, 4, LANES), "power_rows")(parts, d, c, a, b)

    gathered = exchange(power, ("z", "ta"))
    order = group_order.reshape(y_size, z_size, 2, PACK)
    wanted = lax.dynamic_index_in_dim(order, lax.axis_index("z"), 1, keepdims=False)
    wanted = wanted.transpose(2, 0, 1).reshape(-1, 1)
    holder = (wanted // GR_DEV + 1) % block_total
    member = wanted % GR_DEV
    spot = (member % PACK * z_size + holder % z_size) * 2 + member // PACK
    spot = jnp.where(holder // z_size == lax.axis_index("y"), spot, -1)
    choose = functools.partial(choose_kernel, times)
    chosen = small_call(choose, (y_size * times, 2, LANES), "choose_rows")(spot, gathered)

    found = exchange(chosen, ("y", "ta"))
    return small_call(unpack_kernel, (GR_DEV, channels), "unpack_rows")(found)


def solution(mesh):
    blocks, times = mesh.devices.shape
    y_size = 2 ** (int(math.log2(blocks)) // 2)
    cut = Mesh(mesh.devices.reshape(y_size, blocks // y_size, times), ("y", "z", "ta"))
    return jax.shard_map(
        on_device,
        mesh=cut,
        in_specs=(P("ta", BLOCK_AXES, None), P("ta", BLOCK_AXES), P(BLOCK_AXES), P(), P(), P()),
        out_specs=P(BLOCK_AXES, None),
        check_vma=False,
    )
```

time: 93.6 us -> 68.4 us (0.73)
  the two profiles are of different devices: /device:TPU:8 before, /device:TPU:1 now
where the time goes in v3:
time: 68.4 us; the launch traced here: 68.1 us
  starting transfers between devices  26.9 us (39%)
  blocking collectives  16.6 us (24%)
  waiting for transfers between devices  16 us (23%)
  Pallas kernels  5.88 us (9%)
  local copies, waits for them, and re-layouts  1.86 us (3%)
    ppermute x3, starting transfers between devices, shifted(): lax.ppermute(shard, BLOCK_AXES, [(i, (i + by) % devices) for i in range(d...  19.7 us
    all_to_all x1, blocking collectives, exchange(): return lax.all_to_all(chunks, axis, 0, 0, tiled=True)  16.6 us
    all_to_all x1, waiting for transfers between devices, exchange(): return lax.all_to_all(chunks, axis, 0, 0, tiled=True)  10.7 us
    all_to_all x1, starting transfers between devices, exchange(): return lax.all_to_all(chunks, axis, 0, 0, tiled=True)  7.24 us
    ppermute x3, waiting for transfers between devices, shifted(): lax.ppermute(shard, BLOCK_AXES, [(i, (i + by) % devices) for i in range(d...  5.25 us
    pallas_call x1, Pallas kernels, group_sums(): pl.pallas_call(functools.partial(group_kernel, block_total), in_specs=[pl...  3.66 us
    unnamed x12, local copies, waits for them, and re-layouts  1.43 us
  transfers between devices with their start and end apart: 4, of which 3 were waited for; matrix products, arithmetic and copies ran while one was open for 2% of the time, Pallas kernels for 0%

profile of v3, /device:TPU:1, one launch (start us, length us, event | category | flops | bytes accessed | tf_op | source)
XLA Modules:
  0.0 68.1 jit_solution(794822468305669246)
XLA Ops:
  0.0 0.0 copy-start.4
  0.0 0.0 copy-start.5
  0.0 0.0 copy-start
  0.0 0.7 %copy-done = s32[16,256]{1,0:T(8,128)S(1)} copy-done((s32[16,256]{1,0:T(8,128)S(1)}, s32[16,256]{1,0:T(8,128)}, u32[]{:S(2)}) %copy-start) | copy-done | bytes 16408
  0.8 0.0 copy-start.1
  0.8 0.7 copy-done.1
  1.4 0.0 copy-start.2
  1.4 0.0 copy-start.3
  1.4 3.7 %group_sums.1 = (bf16[144,512]{1,0:T(8,128)(2,1)S(1)}, bf16[144,512]{1,0:T(8,128)(2,1)S(1)}, bf16[144,512]{1,0:T(8,128)(2,1)S(1)}, bf16[144,512]{1,0:T(8,128)(2,1)S(1)}) custom-call(s32[1]{0:T(128)} %bitcast.2.place_ref, s32[1,256]{1,0:T(1,128)S(1)} %bitcast.6, s32[16,256]{1,0:T(8,128)S(1)} %copy-done, bf16[16,256,512]{2,1,0:T(8,128)(2,1)} %vis_ref.1), custom_call_target="tpu_custom_call" | custom-call | flops 134217728 | bytes 4194304 | tf_op jit(solution)/shard_map/group_sums/pallas_call | solution.py:86
  5.1 14.4 %collective-permute-start = (bf16[144,512]{1,0:T(8,128)(2,1)S(1)}, bf16[144,512]{1,0:T(8,128)(2,1)S(1)}, u32[]{:S(2)}, u32[]{:S(2)}) collective-permute-start(bf16[144,512]{1,0:T(8,128)(2,1)S(1)} %get-tuple-element.9), channel_id=1, source_target_pairs={{0,496},{8,504},{16,0},{24,8},{32,16},{40,24},{48,32},{56,40},{64,... | collective-permute-start | bytes 442376 | tf_op jit(solution)/shard_map/ppermute | solution.py:24
  19.5 2.2 %collective-permute-start.1 = (bf16[144,512]{1,0:T(8,128)(2,1)S(1)}, bf16[144,512]{1,0:T(8,128)(2,1)S(1)}, u32[]{:S(2)}, u32[]{:S(2)}) collective-permute-start(bf16[144,512]{1,0:T(8,128)(2,1)S(1)} %get-tuple-element.10), channel_id=1, source_target_pairs={{0,504},{8,0},{16,8},{24,16},{32,24},{40,32},{48,40},{56,48},{64,5... | collective-permute-start | bytes 442376 | tf_op jit(solution)/shard_map/ppermute | solution.py:24
  21.7 3.1 %collective-permute-start.2 = (bf16[144,512]{1,0:T(8,128)(2,1)S(1)}, bf16[144,512]{1,0:T(8,128)(2,1)S(1)}, u32[]{:S(2)}, u32[]{:S(2)}) collective-permute-start(bf16[144,512]{1,0:T(8,128)(2,1)S(1)} %get-tuple-element.11), channel_id=1, source_target_pairs={{0,8},{8,16},{16,24},{24,32},{32,40},{40,48},{48,56},{56,64},{64,7... | collective-permute-start | bytes 442376 | tf_op jit(solution)/shard_map/ppermute | solution.py:24
  24.8 0.0 copy-done.4
  24.8 0.1 reshape.384
  25.0 0.0 copy-done.5
  25.0 0.0 copy-done.2
  25.0 0.0 copy-done.3
  25.0 0.6 convolution_convert_fusion.parts_ref
  25.6 0.0 collective-permute-done.d_ref
  25.6 1.5 %collective-permute-done.1.c_ref = bf16[144,512]{1,0:T(8,128)(2,1)S(1)} collective-permute-done((bf16[144,512]{1,0:T(8,128)(2,1)S(1)}, bf16[144,512]{1,0:T(8,128)(2,1)S(1)}, u32[]{:S(2)}, u32[]{:S(2)}) %collective-permute-start.1) | collective-permute-done | bytes 147488 | tf_op jit(solution)/shard_map/ppermute | solution.py:24
  27.1 3.8 %collective-permute-done.2.a_ref = bf16[144,512]{1,0:T(8,128)(2,1)S(1)} collective-permute-done((bf16[144,512]{1,0:T(8,128)(2,1)S(1)}, bf16[144,512]{1,0:T(8,128)(2,1)S(1)}, u32[]{:S(2)}, u32[]{:S(2)}) %collective-permute-start.2) | collective-permute-done | bytes 147488 | tf_op jit(solution)/shard_map/ppermute | solution.py:24
  30.9 1.2 %power_rows.1 = f32[64,4,128]{2,1,0:T(4,128)} custom-call(bf16[256,512]{1,0:T(8,128)(2,1)S(1)} %convolution_convert_fusion.parts_ref, bf16[144,512]{1,0:T(8,128)(2,1)S(1)} %collective-permute-done.d_ref, bf16[144,512]{1,0:T(8,128)(2,1)S(1)} %collective-permute-done.1.c_ref, bf16[144,512]{1,0:T(8,128)(2,1)S(1)} %collective-permute-done.2.a_ref, ...), custom_call_target="tpu_custom_call" | custom-call | tf_op jit(solution)/shard_map/power_rows/pallas_call | solution.py:216
  32.1 7.2 %all-to-all-start = ((f32[64,4,128]{2,1,0:T(4,128)}), f32[64,4,128]{2,1,0:T(4,128)S(1)}, u32[]{:S(2)}, u32[]{:S(2)}) async-start(f32[64,4,128]{2,1,0:T(4,128)} %power_rows.1), calls=%async_computation | async-start | bytes 262144 | tf_op jit(solution)/shard_map/all_to_all | solution.py:28
  39.4 0.1 copy.13
  39.5 0.1 copy.14
  39.6 0.1 reshape.386
  39.6 0.1 fusion.9.spot_ref
  39.7 10.7 %all-to-all-done.in_ref = f32[64,4,128]{2,1,0:T(4,128)S(1)} async-done(((f32[64,4,128]{2,1,0:T(4,128)}), f32[64,4,128]{2,1,0:T(4,128)S(1)}, u32[]{:S(2)}, u32[]{:S(2)}) %all-to-all-start) | async-done | bytes 131104 | tf_op jit(solution)/shard_map/all_to_all | solution.py:28
  50.5 0.3 choose_rows.1
  50.8 16.6 %all_to_all.10.in_ref = f32[64,2,128]{2,1,0:T(2,128)S(1)} all-to-all(f32[64,2,128]{2,1,0:T(2,128)S(1)} %choose_rows.1), channel_id=1, replica_groups=mesh['y'=8,'z'=8,'ta'=8] {'y','ta'}, dimensions={0} | all-to-all | bytes 131072 | tf_op jit(solution)/shard_map/all_to_all | solution.py:28
  67.4 0.7 %unpack_rows.1 = f32[8,256]{1,0:T(8,128)} custom-call(f32[64,2,128]{2,1,0:T(2,128)S(1)} %all_to_all.10.in_ref), custom_call_target="tpu_custom_call" | custom-call | tf_op jit(solution)/shard_map/unpack_rows/pallas_call | solution.py:230
  (1 shorter events, 0.0 us)
Async XLA Ops:
  0.0 24.8 %copy-start.4 = (s32[512]{0:T(512)S(1)}, s32[512]{0:T(512)}, u32[]{:S(2)}) copy-start(s32[512]{0:T(512)} %param.10) | copy-start | bytes 6148
  0.0 25.0 %copy-start.5 = (f32[256]{0:T(256)S(1)}, f32[256]{0:T(256)}, u32[]{:S(2)}) copy-start(f32[256]{0:T(256)} %param.11) | copy-start | bytes 3076
  0.0 0.7 %copy-start = (s32[16,256]{1,0:T(8,128)S(1)}, s32[16,256]{1,0:T(8,128)}, u32[]{:S(2)}) copy-start(s32[16,256]{1,0:T(8,128)} %flags_ref.1) | copy-start | bytes 49156
  0.8 0.7 copy-start.1
  1.4 23.5 %copy-start.2 = (f32[256,512]{1,0:T(8,128)S(1)}, f32[256,512]{1,0:T(8,128)}, u32[]{:S(2)}) copy-start(f32[256,512]{1,0:T(8,128)} %constant.89.clone) | copy-start | bytes 1572868
  1.4 23.6 %copy-start.3 = (f32[256,256]{1,0:T(8,128)S(1)}, f32[256,256]{1,0:T(8,128)}, u32[]{:S(2)}) copy-start(f32[256,256]{1,0:T(8,128)} %param.12) | copy-start | bytes 786436
  5.1 20.5 %collective-permute-start = (bf16[144,512]{1,0:T(8,128)(2,1)S(1)}, bf16[144,512]{1,0:T(8,128)(2,1)S(1)}, u32[]{:S(2)}, u32[]{:S(2)}) collective-permute-start(bf16[144,512]{1,0:T(8,128)(2,1)S(1)} %get-tuple-element.9), channel_id=1, source_target_pairs={{0,496},{8,504},{16,0},{24,8},{32,16},{40,24},{48,32},{56,40},{64,... | collective-permute-start | bytes 442376 | tf_op jit(solution)/shard_map/ppermute | solution.py:24
  19.5 7.6 %collective-permute-start.1 = (bf16[144,512]{1,0:T(8,128)(2,1)S(1)}, bf16[144,512]{1,0:T(8,128)(2,1)S(1)}, u32[]{:S(2)}, u32[]{:S(2)}) collective-permute-start(bf16[144,512]{1,0:T(8,128)(2,1)S(1)} %get-tuple-element.10), channel_id=1, source_target_pairs={{0,504},{8,0},{16,8},{24,16},{32,24},{40,32},{48,40},{56,48},{64,5... | collective-permute-start | bytes 442376 | tf_op jit(solution)/shard_map/ppermute | solution.py:24
  21.7 9.2 %collective-permute-start.2 = (bf16[144,512]{1,0:T(8,128)(2,1)S(1)}, bf16[144,512]{1,0:T(8,128)(2,1)S(1)}, u32[]{:S(2)}, u32[]{:S(2)}) collective-permute-start(bf16[144,512]{1,0:T(8,128)(2,1)S(1)} %get-tuple-element.11), channel_id=1, source_target_pairs={{0,8},{8,16},{16,24},{24,32},{32,40},{40,48},{48,56},{56,64},{64,7... | collective-permute-start | bytes 442376 | tf_op jit(solution)/shard_map/ppermute | solution.py:24
  32.1 18.4 %all-to-all-start = ((f32[64,4,128]{2,1,0:T(4,128)}), f32[64,4,128]{2,1,0:T(4,128)S(1)}, u32[]{:S(2)}, u32[]{:S(2)}) async-start(f32[64,4,128]{2,1,0:T(4,128)} %power_rows.1), calls=%async_computation | async-start | bytes 262144 | tf_op jit(solution)/shard_map/all_to_all | solution.py:28

commit v4 on v3

v4 whole, which is shorter than its diff:
```python
import functools
import math

import numpy as np
import jax
import jax.numpy as jnp
from jax import lax
from jax.experimental import pallas as pl
from jax.experimental.pallas import tpu as pltpu
from jax.sharding import Mesh
from jax.sharding import PartitionSpec as P

GR_DEV = 8
SPAN = 4
LANES = 128
BLOCK_AXES = ("y", "z")
COUNT_ROWS = 16
TOGETHER = 4


def opposed(shard, by):
    blocks, times = lax.axis_size(BLOCK_AXES), lax.axis_size("ta")
    pairs = []
    for block in range(blocks):
        for time in range(times):
            target = (block + (-by if time % 2 else by)) % blocks
            pairs.append((block * times + time, target * times + time))
    return lax.ppermute(shard, (*BLOCK_AXES, "ta"), pairs)


def exchange(chunks, axis):
    return lax.all_to_all(chunks, axis, 0, 0, tiled=True)


def fourier_table(channels):
    ramp = np.arange(channels)
    angles = 2.0 * math.pi / channels * (ramp[:, None] * ramp[None, :] % channels)
    both = np.concatenate([np.cos(angles), np.sin(angles)], axis=1) / math.sqrt(channels)
    return both.astype(np.float32)


def exact_dot(x, y):
    return jnp.dot(x, y, precision=lax.Precision.HIGHEST, preferred_element_type=jnp.float32)


def transform_parts(taper, inv_cov):
    weighted = taper[:, None] * inv_cov
    return exact_dot(weighted, jnp.asarray(fourier_table(taper.shape[0]))).astype(jnp.bfloat16)


BLOCK_STEPS = (3, 2, 0, 1)


def group_kernel(block_total, place_ref, ids_hbm, flags_hbm, vis_hbm, *rest):
    *refs, ids_ref, flags_ref, held_ref, few_sems, sems = rest
    time_count, _, row_width = vis_hbm.shape
    few = [
        pltpu.make_async_copy(source, target, few_sems.at[i])
        for i, (source, target) in enumerate(((ids_hbm, ids_ref), (flags_hbm, flags_ref)))
    ]
    copies = [pltpu.make_async_copy(vis_hbm.at[t], held_ref.at[t], sems.at[t]) for t in range(time_count)]
    for copy in few + copies:
        copy.start()
    for copy in few:
        copy.wait()
    ids = ids_ref[...]
    back = place_ref[0] - (ids >> 3)
    back = jnp.where(back < 0, back + block_total, back)
    back = jnp.where(place_ref[1] == 1, SPAN - 1 - back, back)
    row = lax.broadcasted_iota(jnp.int32, (SPAN * GR_DEV, ids.shape[1]), 0)
    onehot = (row == back * GR_DEV + (ids & (GR_DEV - 1))).astype(jnp.float32)
    lane = lax.broadcasted_iota(jnp.int32, (SPAN * GR_DEV, LANES), 1)
    counts = jnp.zeros((SPAN * GR_DEV, LANES), jnp.float32)
    for first in range(0, time_count, TOGETHER):
        tables = []
        for t in range(first, first + TOGETHER):
            table = onehot * flags_ref[t : t + 1, :].astype(jnp.float32)
            counts = jnp.where(lane == t, jnp.sum(table, axis=1, keepdims=True), counts)
            tables.append(table.astype(jnp.bfloat16))
        for t in range(first, first + TOGETHER):
            copies[t].wait()
        sums = [
            jnp.dot(table, held_ref[first + i], preferred_element_type=jnp.float32)
            for i, table in enumerate(tables)
        ]
        for step, ref in zip(BLOCK_STEPS, refs):
            span = slice(step * GR_DEV, (step + 1) * GR_DEV)
            both = jnp.concatenate([one[span] for one in sums], axis=0)
            ref[first * GR_DEV : (first + TOGETHER) * GR_DEV, :] = both.astype(jnp.bfloat16)
    for step, ref in zip(BLOCK_STEPS, refs):
        mine = counts[step * GR_DEV : (step + 1) * GR_DEV]
        tile = jnp.concatenate([mine, jnp.zeros_like(mine)], axis=0)
        tile = jnp.concatenate([tile, jnp.zeros((COUNT_ROWS, row_width - LANES), jnp.float32)], axis=1)
        ref[time_count * GR_DEV :, :] = tile.astype(jnp.bfloat16)


def group_sums(visibilities, flags, group_ids, place, block_total):
    time_count, block_length, row_width = visibilities.shape
    block = pltpu.VMEM((time_count * GR_DEV + COUNT_ROWS, row_width), jnp.bfloat16)
    arrays = [pltpu.with_memory_space_constraint(x, pltpu.HBM) for x in (group_ids[None, :], flags, visibilities)]
    return pl.pallas_call(
        functools.partial(group_kernel, block_total),
        in_specs=[pl.BlockSpec(memory_space=pltpu.SMEM)] + [pl.BlockSpec(memory_space=pltpu.HBM)] * len(arrays),
        out_specs=[pl.BlockSpec(memory_space=pltpu.VMEM)] * SPAN,
        out_shape=[block] * SPAN,
        scratch_shapes=[pltpu.VMEM(x.shape, x.dtype) for x in arrays]
        + [pltpu.SemaphoreType.DMA((2,)), pltpu.SemaphoreType.DMA((time_count,))],
        compiler_params=pltpu.CompilerParams(vmem_limit_bytes=16 << 20),
        cost_estimate=pl.CostEstimate(
            flops=2 * time_count * SPAN * GR_DEV * block_length * row_width,
            bytes_accessed=visibilities.size * 2,
            transcendentals=0,
        ),
        name="group_sums",
    )(place, *arrays)


def pair_sum(a, b, c, d):
    return b * a + c * (a + b) + d * (a + b + c)


def power_kernel(parts_ref, a_ref, b_ref, c_ref, d_ref, out_ref):
    channels = parts_ref.shape[0]
    rows = a_ref.shape[0] - COUNT_ROWS
    cosines = parts_ref[:, :channels]
    sines = parts_ref[:, channels:]

    def dot(x, y):
        return jnp.dot(x, y, preferred_element_type=jnp.float32)

    def delays(ref):
        re, im = ref[:rows, :channels], ref[:rows, channels:]
        return dot(re, cosines) + dot(im, sines), dot(im, cosines) - dot(re, sines)

    blocks = [delays(ref) for ref in (a_ref, b_ref, c_ref, d_ref)]
    pairs = pair_sum(*(re for re, _ in blocks)) + pair_sum(*(im for _, im in blocks))
    power = jnp.sum(pairs.reshape(rows // GR_DEV, GR_DEV, channels), axis=0)
    counts = [ref[rows:, :LANES].astype(jnp.float32)[:GR_DEV] for ref in (a_ref, b_ref, c_ref, d_ref)]
    count = jnp.sum(pair_sum(*counts), axis=1, keepdims=True)
    result = jnp.concatenate([power, jnp.broadcast_to(count, (GR_DEV, LANES))], axis=1)
    for copy in range(out_ref.shape[0]):
        out_ref[copy] = result


def power_rows(parts, blocks, copies):
    channels = parts.shape[0]
    rows = sum(block.shape[0] - COUNT_ROWS for block in blocks)
    return pl.pallas_call(
        power_kernel,
        out_shape=jax.ShapeDtypeStruct((copies, GR_DEV, channels + LANES), jnp.float32),
        compiler_params=pltpu.CompilerParams(vmem_limit_bytes=16 << 20),
        cost_estimate=pl.CostEstimate(flops=8 * rows * channels * channels, bytes_accessed=2 << 20, transcendentals=0),
        name="power_rows",
    )(parts, *blocks)


def on_device(visibilities, flags, group_ids, group_order, taper, inv_cov):
    channels = taper.shape[0]
    y_size, z_size, times = (lax.axis_size(axis) for axis in ("y", "z", "ta"))
    block_total = y_size * z_size
    core = lax.axis_index("ta") % 2
    place = jnp.stack([lax.axis_index(BLOCK_AXES), core])

    blocks = group_sums(visibilities, flags, group_ids, place, block_total)
    blocks = [opposed(block, by) if by else block for block, by in zip(blocks, (-2, -1, 1, 0))]
    rows = power_rows(transform_parts(taper, inv_cov), blocks, z_size)

    plane = exchange(rows, "z").reshape(z_size * GR_DEV, channels + LANES)
    order = group_order.reshape(y_size, z_size, GR_DEV)
    wanted = lax.dynamic_index_in_dim(order, lax.axis_index("z"), 1, keepdims=False).reshape(-1)
    holder = (wanted // GR_DEV + 1 + core) % block_total
    spot = jnp.where(
        holder // z_size == lax.axis_index("y"), holder % z_size * GR_DEV + wanted % GR_DEV, -1
    )
    pick = spot[:, None] == jnp.arange(z_size * GR_DEV, dtype=jnp.int32)[None, :]
    chosen = exact_dot(pick.astype(jnp.float32), plane).reshape(y_size, GR_DEV, channels + LANES)
    found = exchange(chosen, "y").reshape(y_size * GR_DEV, channels + LANES)

    fold = np.tile(np.eye(GR_DEV, dtype=np.float32), (times, y_size))
    partial = exact_dot(jnp.asarray(fold), found).reshape(times, GR_DEV, channels + LANES)
    totals = jnp.sum(exchange(partial, "ta"), axis=0)
    return totals[:, :channels] / jnp.maximum(totals[:, channels : channels + 1], 1.0)


def solution(mesh):
    blocks, times = mesh.devices.shape
    y_size = 2 ** (int(math.log2(blocks)) // 2)
    cut = Mesh(mesh.devices.reshape(y_size, blocks // y_size, times), ("y", "z", "ta"))
    return jax.shard_map(
        on_device,
        mesh=cut,
        in_specs=(P("ta", BLOCK_AXES, None), P("ta", BLOCK_AXES), P(BLOCK_AXES), P(), P(), P()),
        out_specs=P(BLOCK_AXES, None),
        check_vma=False,
    )
```

time: 68.4 us -> 68.7 us (level)
  blocking collectives: 16.6 us -> 28.7 us
  waiting for transfers between devices: 16 us -> 10.7 us
  starting transfers between devices: 26.9 us -> 21.6 us
  local copies, waits for them, and re-layouts: 1.86 us -> 0.12 us
  other arithmetic: 0.11 us -> 0.92 us
  Pallas kernels: 5.88 us -> 5.07 us
    all_to_all x1 -> x2, blocking collectives: 16.6 us -> 28.7 us  [exchange(): return lax.all_to_all(chunks, axis, 0, 0, tiled=True)]
    all_to_all x1, starting transfers between devices: 7.24 us -> 3.36 us  [exchange(): return lax.all_to_all(chunks, axis, 0, 0, tiled=True)]
    all_to_all x1, waiting for transfers between devices: 10.7 us -> 7.45 us  [exchange(): return lax.all_to_all(chunks, axis, 0, 0, tiled=True)]
    ppermute x3, waiting for transfers between devices: 5.25 us -> 3.21 us  [opposed(): return lax.ppermute(shard, (*BLOCK_AXES, 'ta'), pairs)]
    ppermute x3, starting transfers between devices: 19.7 us -> 18.2 us  [opposed(): return lax.ppermute(shard, (*BLOCK_AXES, 'ta'), pairs)]
    unnamed x12 -> x10, local copies, waits for them, and re-layouts: 1.43 us -> 0.02 us
    pallas_call x3 -> x1, Pallas kernels: 2.22 us -> 1.09 us  [power_rows(): pl.pallas_call(power_kernel, out_shape=jax.ShapeDtypeStruct((copies, GR_D...]
  transfers between devices with their start and end apart: 4 -> 4, of which waited for: 3 -> 3; matrix products, arithmetic and copies ran while one was open for 2% -> 1% of each run, Pallas kernels for 0% -> 0%
where the time goes in v4:
time: 68.7 us; the launch traced here: 68.4 us
  blocking collectives  28.7 us (42%)
  starting transfers between devices  21.6 us (31%)
  waiting for transfers between devices  10.7 us (16%)
  Pallas kernels  5.07 us (7%)
  matrix products  1.09 us (2%)
  other arithmetic  0.92 us (1%)
    all_to_all x2, blocking collectives, exchange(): return lax.all_to_all(chunks, axis, 0, 0, tiled=True)  28.7 us
    ppermute x3, starting transfers between devices, opposed(): return lax.ppermute(shard, (*BLOCK_AXES, 'ta'), pairs)  18.2 us
    all_to_all x1, waiting for transfers between devices, exchange(): return lax.all_to_all(chunks, axis, 0, 0, tiled=True)  7.45 us
    pallas_call x1, Pallas kernels, group_sums(): pl.pallas_call(functools.partial(group_kernel, block_total), in_specs=[pl...  3.98 us
    all_to_all x1, starting transfers between devices, exchange(): return lax.all_to_all(chunks, axis, 0, 0, tiled=True)  3.36 us
    ppermute x3, waiting for transfers between devices, opposed(): return lax.ppermute(shard, (*BLOCK_AXES, 'ta'), pairs)  3.21 us
  transfers between devices with their start and end apart: 4, of which 3 were waited for; matrix products, arithmetic and copies ran while one was open for 1% of the time, Pallas kernels for 0%

profile of v4, /device:TPU:1, one launch (start us, length us, event | category | flops | bytes accessed | tf_op | source)
XLA Modules:
  0.0 68.4 jit_solution(14276694837989113056)
XLA Ops:
  0.0 0.0 copy-start
  0.0 0.0 copy-start.2
  0.0 0.0 copy-start.4
  0.0 0.0 copy-start.1
  0.0 0.0 copy-start.3
  0.0 0.1 pad_add_fusion.place_ref
  0.1 4.0 %group_sums.1 = (bf16[144,512]{1,0:T(8,128)(2,1)S(1)}, bf16[144,512]{1,0:T(8,128)(2,1)S(1)}, bf16[144,512]{1,0:T(8,128)(2,1)S(1)}, bf16[144,512]{1,0:T(8,128)(2,1)S(1)}) custom-call(s32[2]{0:T(128)S(1)} %pad_add_fusion.place_ref, s32[1,256]{1,0:T(1,128)} %bitcast.20, s32[16,256]{1,0:T(8,128)} %flags_hbm.1, bf16[16,256,512]{2,1,0:T(8,128)(2,1)} %vis_hbm.1), custom_call_target="tpu_custom_call" | custom-call | flops 134217728 | bytes 4194304 | tf_op jit(solution)/shard_map/group_sums/pallas_call | solution.py:101
  4.1 6.6 %collective-permute-start = (bf16[144,512]{1,0:T(8,128)(2,1)S(1)}, bf16[144,512]{1,0:T(8,128)(2,1)S(1)}, u32[]{:S(2)}, u32[]{:S(2)}) collective-permute-start(bf16[144,512]{1,0:T(8,128)(2,1)S(1)} %get-tuple-element.9), channel_id=1, source_target_pairs={{0,496},{1,17},{2,498},{3,19},{4,500},{5,21},{6,502},{7,23},{8,504... | collective-permute-start | bytes 442376 | tf_op jit(solution)/shard_map/ppermute | solution.py:28
  10.8 4.0 %collective-permute-start.1 = (bf16[144,512]{1,0:T(8,128)(2,1)S(1)}, bf16[144,512]{1,0:T(8,128)(2,1)S(1)}, u32[]{:S(2)}, u32[]{:S(2)}) collective-permute-start(bf16[144,512]{1,0:T(8,128)(2,1)S(1)} %get-tuple-element.10), channel_id=1, source_target_pairs={{0,504},{1,9},{2,506},{3,11},{4,508},{5,13},{6,510},{7,15},{8,0},{... | collective-permute-start | bytes 442376 | tf_op jit(solution)/shard_map/ppermute | solution.py:28
  14.8 7.6 %collective-permute-start.2 = (bf16[144,512]{1,0:T(8,128)(2,1)S(1)}, bf16[144,512]{1,0:T(8,128)(2,1)S(1)}, u32[]{:S(2)}, u32[]{:S(2)}) collective-permute-start(bf16[144,512]{1,0:T(8,128)(2,1)S(1)} %get-tuple-element.11), channel_id=1, source_target_pairs={{0,8},{1,505},{2,10},{3,507},{4,12},{5,509},{6,14},{7,511},{8,16},... | collective-permute-start | bytes 442376 | tf_op jit(solution)/shard_map/ppermute | solution.py:28
  22.4 0.0 copy-done
  22.4 0.0 copy-done.4
  22.4 0.0 copy-done.1
  22.4 0.6 convolution_convert_fusion.parts_ref
  23.1 0.0 copy-done.3
  23.1 0.1 reshape.132
  23.2 0.0 collective-permute-done.a_ref
  23.2 1.0 %collective-permute-done.1.b_ref = bf16[144,512]{1,0:T(8,128)(2,1)S(1)} collective-permute-done((bf16[144,512]{1,0:T(8,128)(2,1)S(1)}, bf16[144,512]{1,0:T(8,128)(2,1)S(1)}, u32[]{:S(2)}, u32[]{:S(2)}) %collective-permute-start.1) | collective-permute-done | bytes 147488 | tf_op jit(solution)/shard_map/ppermute | solution.py:28
  24.2 2.2 %collective-permute-done.2.c_ref = bf16[144,512]{1,0:T(8,128)(2,1)S(1)} collective-permute-done((bf16[144,512]{1,0:T(8,128)(2,1)S(1)}, bf16[144,512]{1,0:T(8,128)(2,1)S(1)}, u32[]{:S(2)}, u32[]{:S(2)}) %collective-permute-start.2) | collective-permute-done | bytes 147488 | tf_op jit(solution)/shard_map/ppermute | solution.py:28
  26.4 1.1 %power_rows.1 = f32[8,8,384]{2,1,0:T(8,128)} custom-call(bf16[256,512]{1,0:T(8,128)(2,1)S(1)} %convolution_convert_fusion.parts_ref, bf16[144,512]{1,0:T(8,128)(2,1)S(1)} %collective-permute-done.a_ref, bf16[144,512]{1,0:T(8,128)(2,1)S(1)} %collective-permute-done.1.b_ref, bf16[144,512]{1,0:T(8,128)(2,1)S(1)} %collective-permute-done.2.c_ref, ...), custom_call_target="tpu_custom_call" | custom-call | flops 268435456 | bytes 2097152 | tf_op jit(solution)/shard_map/power_rows/pallas_call | solution.py:148
  27.5 3.4 %all-to-all-start = ((f32[8,8,384]{2,1,0:T(8,128)}), f32[8,8,384]{2,1,0:T(8,128)S(1)}, u32[]{:S(2)}, u32[]{:S(2)}) async-start(f32[8,8,384]{2,1,0:T(8,128)} %power_rows.1), calls=%async_computation | async-start | bytes 196608 | tf_op jit(solution)/shard_map/all_to_all | solution.py:32
  30.9 7.4 %all-to-all-done = f32[8,8,384]{2,1,0:T(8,128)S(1)} async-done(((f32[8,8,384]{2,1,0:T(8,128)}), f32[8,8,384]{2,1,0:T(8,128)S(1)}, u32[]{:S(2)}, u32[]{:S(2)}) %all-to-all-start) | async-done | bytes 98336 | tf_op jit(solution)/shard_map/all_to_all | solution.py:32
  38.3 0.2 fusion.2
  38.6 13.4 %all_to_all.15 = f32[8,8,384]{2,1,0:T(8,128)S(1)} all-to-all(f32[8,8,384]{2,1,0:T(8,128)S(1)} %fusion.2), channel_id=1, replica_groups=mesh['y'=8,'z'=8,'ta'=8] {'y'}, dimensions={0} | all-to-all | bytes 196608 | tf_op jit(solution)/shard_map/all_to_all | solution.py:32
  51.9 0.0 copy-done.2
  52.0 0.2 convolution_bitcast_fusion
  52.2 15.4 %all_to_all.16 = f32[8,8,384]{2,1,0:T(8,128)S(1)} all-to-all(f32[8,8,384]{2,1,0:T(8,128)S(1)} %convolution_bitcast_fusion), channel_id=1, replica_groups=mesh['y'=8,'z'=8,'ta'=8] {'ta'}, dimensions={0} | all-to-all | bytes 196608 | tf_op jit(solution)/shard_map/all_to_all | solution.py:32
  67.6 0.1 fusion.15
  67.7 0.7 slice_divide_fusion
  (3 shorter events, 0.1 us)
Async XLA Ops:
  0.0 22.4 %copy-start = (f32[256,512]{1,0:T(8,128)S(1)}, f32[256,512]{1,0:T(8,128)}, u32[]{:S(2)}) copy-start(f32[256,512]{1,0:T(8,128)} %constant.88.clone) | copy-start | bytes 1572868
  0.0 51.9 %copy-start.2 = (f32[64,64]{1,0:T(8,128)S(1)}, f32[64,64]{1,0:T(8,128)}, u32[]{:S(2)}) copy-start(f32[64,64]{1,0:T(8,128)} %constant.89.clone) | copy-start | bytes 49156
  0.0 22.4 %copy-start.4 = (f32[256]{0:T(256)S(1)}, f32[256]{0:T(256)}, u32[]{:S(2)}) copy-start(f32[256]{0:T(256)} %param.12) | copy-start | bytes 3076
  0.0 22.4 %copy-start.1 = (f32[256,256]{1,0:T(8,128)S(1)}, f32[256,256]{1,0:T(8,128)}, u32[]{:S(2)}) copy-start(f32[256,256]{1,0:T(8,128)} %param.13) | copy-start | bytes 786436
  0.0 23.0 %copy-start.3 = (s32[512]{0:T(512)S(1)}, s32[512]{0:T(512)}, u32[]{:S(2)}) copy-start(s32[512]{0:T(512)} %param.11) | copy-start | bytes 6148
  4.1 19.1 %collective-permute-start = (bf16[144,512]{1,0:T(8,128)(2,1)S(1)}, bf16[144,512]{1,0:T(8,128)(2,1)S(1)}, u32[]{:S(2)}, u32[]{:S(2)}) collective-permute-start(bf16[144,512]{1,0:T(8,128)(2,1)S(1)} %get-tuple-element.9), channel_id=1, source_target_pairs={{0,496},{1,17},{2,498},{3,19},{4,500},{5,21},{6,502},{7,23},{8,504... | collective-permute-start | bytes 442376 | tf_op jit(solution)/shard_map/ppermute | solution.py:28
  10.8 13.4 %collective-permute-start.1 = (bf16[144,512]{1,0:T(8,128)(2,1)S(1)}, bf16[144,512]{1,0:T(8,128)(2,1)S(1)}, u32[]{:S(2)}, u32[]{:S(2)}) collective-permute-start(bf16[144,512]{1,0:T(8,128)(2,1)S(1)} %get-tuple-element.10), channel_id=1, source_target_pairs={{0,504},{1,9},{2,506},{3,11},{4,508},{5,13},{6,510},{7,15},{8,0},{... | collective-permute-start | bytes 442376 | tf_op jit(solution)/shard_map/ppermute | solution.py:28
  14.8 11.6 %collective-permute-start.2 = (bf16[144,512]{1,0:T(8,128)(2,1)S(1)}, bf16[144,512]{1,0:T(8,128)(2,1)S(1)}, u32[]{:S(2)}, u32[]{:S(2)}) collective-permute-start(bf16[144,512]{1,0:T(8,128)(2,1)S(1)} %get-tuple-element.11), channel_id=1, source_target_pairs={{0,8},{1,505},{2,10},{3,507},{4,12},{5,509},{6,14},{7,511},{8,16},... | collective-permute-start | bytes 442376 | tf_op jit(solution)/shard_map/ppermute | solution.py:28
  27.5 10.9 %all-to-all-start = ((f32[8,8,384]{2,1,0:T(8,128)}), f32[8,8,384]{2,1,0:T(8,128)S(1)}, u32[]{:S(2)}, u32[]{:S(2)}) async-start(f32[8,8,384]{2,1,0:T(8,128)} %power_rows.1), calls=%async_computation | async-start | bytes 196608 | tf_op jit(solution)/shard_map/all_to_all | solution.py:32

commit v5 on v3

--- a/solution.py
+++ b/solution.py
@@ -17,6 +17,7 @@
 COUNT_ROWS = 16
 SLICE = 32
 PACK = 4
+TOGETHER = 8
 
 
 def shifted(shard, by):
@@ -44,15 +45,21 @@
     return exact_dot(weighted, jnp.asarray(fourier_table(taper.shape[0]))).astype(jnp.bfloat16)
 
 
-STEPS_BACK = (3, 2, 0, 1)
-
-
-def group_kernel(block_total, place_ref, ids_ref, flags_ref, vis_ref, *rest):
-    *refs, held_ref, sems = rest
-    time_count, _, row_width = vis_ref.shape
-    copies = [pltpu.make_async_copy(vis_ref.at[t], held_ref.at[t], sems.at[t]) for t in range(time_count)]
-    for copy in copies:
+BLOCK_STEPS = (3, 2, 0, 1)
+
+
+def group_kernel(block_total, place_ref, ids_hbm, flags_hbm, vis_hbm, *rest):
+    *refs, ids_ref, flags_ref, held_ref, few_sems, sems = rest
+    time_count, _, row_width = vis_hbm.shape
+    few = [
+        pltpu.make_async_copy(source, target, few_sems.at[i])
+        for i, (source, target) in enumerate(((ids_hbm, ids_ref), (flags_hbm, flags_ref)))
+    ]
+    copies = [pltpu.make_async_copy(vis_hbm.at[t], held_ref.at[t], sems.at[t]) for t in range(time_count)]
+    for copy in few + copies:
         copy.start()
+    for copy in few:
+        copy.wait()
     ids = ids_ref[...]
     back = place_ref[0] - (ids >> 3)
     back = jnp.where(back < 0, back + block_total, back)
@@ -60,20 +67,24 @@
     onehot = (row == back * GR_DEV + (ids & (GR_DEV - 1))).astype(jnp.float32)
     lane = lax.broadcasted_iota(jnp.int32, (SPAN * GR_DEV, LANES), 1)
     counts = jnp.zeros((SPAN * GR_DEV, LANES), jnp.float32)
-    pending = []
-    for t in range(time_count):
-        table = onehot * flags_ref[t : t + 1, :].astype(jnp.float32)
-        counts = jnp.where(lane == t, jnp.sum(table, axis=1, keepdims=True), counts)
-        copies[t].wait()
-        pending.append(jnp.dot(table.astype(jnp.bfloat16), held_ref[t], preferred_element_type=jnp.float32))
-        if len(pending) == 2:
-            for block, ref in zip(STEPS_BACK, refs):
-                span = slice(block * GR_DEV, (block + 1) * GR_DEV)
-                both = jnp.concatenate([sums[span] for sums in pending], axis=0)
-                ref[(t - 1) * GR_DEV : (t + 1) * GR_DEV, :] = both.astype(jnp.bfloat16)
-            pending = []
-    for block, ref in zip(STEPS_BACK, refs):
-        mine = counts[block * GR_DEV : (block + 1) * GR_DEV]
+    for first in range(0, time_count, TOGETHER):
+        tables = []
+        for t in range(first, first + TOGETHER):
+            table = onehot * flags_ref[t : t + 1, :].astype(jnp.float32)
+            counts = jnp.where(lane == t, jnp.sum(table, axis=1, keepdims=True), counts)
+            tables.append(table.astype(jnp.bfloat16))
+        for t in range(first, first + TOGETHER):
+            copies[t].wait()
+        sums = [
+            jnp.dot(table, held_ref[first + i], preferred_element_type=jnp.float32)
+            for i, table in enumerate(tables)
+        ]
+        for step, ref in zip(BLOCK_STEPS, refs):
+            span = slice(step * GR_DEV, (step + 1) * GR_DEV)
+            both = jnp.concatenate([one[span] for one in sums], axis=0)
+            ref[first * GR_DEV : (first + TOGETHER) * GR_DEV, :] = both.astype(jnp.bfloat16)
+    for step, ref in zip(BLOCK_STEPS, refs):
+        mine = counts[step * GR_DEV : (step + 1) * GR_DEV]
         tile = jnp.concatenate([mine, jnp.zeros_like(mine)], axis=0)
         tile = jnp.concatenate([tile, jnp.zeros((COUNT_ROWS, row_width - LANES), jnp.float32)], axis=1)
         ref[time_count * GR_DEV :, :] = tile.astype(jnp.bfloat16)
@@ -81,25 +92,23 @@
 
 def group_sums(visibilities, flags, group_ids, place, block_total):
     time_count, block_length, row_width = visibilities.shape
-    shape = jax.ShapeDtypeStruct((time_count * GR_DEV + COUNT_ROWS, row_width), jnp.bfloat16)
-    vmem = pl.BlockSpec(memory_space=pltpu.VMEM)
+    block = pltpu.VMEM((time_count * GR_DEV + COUNT_ROWS, row_width), jnp.bfloat16)
+    arrays = [pltpu.with_memory_space_constraint(x, pltpu.HBM) for x in (group_ids[None, :], flags, visibilities)]
     return pl.pallas_call(
         functools.partial(group_kernel, block_total),
-        in_specs=[pl.BlockSpec(memory_space=pltpu.SMEM), vmem, vmem, pl.BlockSpec(memory_space=pltpu.HBM)],
-        out_specs=[vmem] * SPAN,
-        out_shape=[shape] * SPAN,
-        scratch_shapes=[
-            pltpu.VMEM(visibilities.shape, visibilities.dtype),
-            pltpu.SemaphoreType.DMA((time_count,)),
-        ],
-        compiler_params=pltpu.CompilerParams(vmem_limit_bytes=50 << 20),
+        in_specs=[pl.BlockSpec(memory_space=pltpu.SMEM)] + [pl.BlockSpec(memory_space=pltpu.HBM)] * len(arrays),
+        out_specs=[pl.BlockSpec(memory_space=pltpu.VMEM)] * SPAN,
+        out_shape=[block] * SPAN,
+        scratch_shapes=[pltpu.VMEM(x.shape, x.dtype) for x in arrays]
+        + [pltpu.SemaphoreType.DMA((2,)), pltpu.SemaphoreType.DMA((time_count,))],
+        compiler_params=pltpu.CompilerParams(vmem_limit_bytes=16 << 20),
         cost_estimate=pl.CostEstimate(
             flops=2 * time_count * SPAN * GR_DEV * block_length * row_width,
             bytes_accessed=visibilities.size * 2,
             transcendentals=0,
         ),
         name="group_sums",
-    )(place, group_ids[None, :], flags, visibilities)
+    )(place, *arrays)
 
 
 def pair_sum(a, b, c, d):
@@ -210,12 +219,10 @@
     slices = channels // SLICE
 
     place = lax.axis_index(BLOCK_AXES)[None]
-    d, c, a, b = group_sums(visibilities, flags, group_ids, place, block_total)
-    d, c, a = shifted(d, -2), shifted(c, -1), shifted(a, 1)
+    blocks = group_sums(visibilities, flags, group_ids, place, block_total)
+    blocks = [shifted(block, by) if by else block for block, by in zip(blocks, (-2, -1, 1, 0))]
     parts = transform_parts(taper, inv_cov)
-    power = small_call(power_kernel, (z_size * slices, 4, LANES), "power_rows")(parts, d, c, a, b)
-
-    gathered = exchange(power, ("z", "ta"))
+
     order = group_order.reshape(y_size, z_size, 2, PACK)
     wanted = lax.dynamic_index_in_dim(order, lax.axis_index("z"), 1, keepdims=False)
     wanted = wanted.transpose(2, 0, 1).reshape(-1, 1)
@@ -223,8 +230,11 @@
     member = wanted % GR_DEV
     spot = (member % PACK * z_size + holder % z_size) * 2 + member // PACK
     spot = jnp.where(holder // z_size == lax.axis_index("y"), spot, -1)
+    parts, spot = lax.optimization_barrier((parts, spot))
+
+    power = small_call(power_kernel, (z_size * slices, 4, LANES), "power_rows")(parts, *blocks)
     choose = functools.partial(choose_kernel, times)
-    chosen = small_call(choose, (y_size * times, 2, LANES), "choose_rows")(spot, gathered)
+    chosen = small_call(choose, (y_size * times, 2, LANES), "choose_rows")(spot, exchange(power, ("z", "ta")))
 
     found = exchange(chosen, ("y", "ta"))
     return small_call(unpack_kernel, (GR_DEV, channels), "unpack_rows")(found)

time: 68.4 us -> 65.6 us (0.959)
  blocking collectives: 16.6 us -> 34.7 us
  waiting for transfers between devices: 16 us -> 4.86 us
  starting transfers between devices: 26.9 us -> 19.7 us
  local copies, waits for them, and re-layouts: 1.86 us -> 0.44 us
  Pallas kernels: 5.88 us -> 4.82 us
    all_to_all x1 -> x2, blocking collectives: 16.6 us -> 34.7 us  [exchange(): return lax.all_to_all(chunks, axis, 0, 0, tiled=True)]
    all_to_all x1 -> x0, waiting for transfers between devices: 10.7 us -> none  [exchange(): return lax.all_to_all(chunks, axis, 0, 0, tiled=True)]
    all_to_all x1 -> x0, starting transfers between devices: 7.24 us -> none  [exchange(): return lax.all_to_all(chunks, axis, 0, 0, tiled=True)]
    unnamed x12 -> x8, local copies, waits for them, and re-layouts: 1.43 us -> 0.02 us
  transfers between devices with their start and end apart: 4 -> 3, of which waited for: 3 -> 2; matrix products, arithmetic and copies ran while one was open for 2% -> 2% of each run, Pallas kernels for 0% -> 0%
where the time goes in v5:
time: 65.6 us; the launch traced here: 65.4 us
  blocking collectives  34.7 us (53%)
  starting transfers between devices  19.7 us (30%)
  waiting for transfers between devices  4.86 us (7%)
  Pallas kernels  4.82 us (7%)
    all_to_all x2, blocking collectives, exchange(): return lax.all_to_all(chunks, axis, 0, 0, tiled=True)  34.7 us
    ppermute x3, starting transfers between devices, shifted(): lax.ppermute(shard, BLOCK_AXES, [(i, (i + by) % devices) for i in range(d...  19.7 us
    ppermute x3, waiting for transfers between devices, shifted(): lax.ppermute(shard, BLOCK_AXES, [(i, (i + by) % devices) for i in range(d...  4.86 us
    pallas_call x1, Pallas kernels, group_sums(): pl.pallas_call(functools.partial(group_kernel, block_total), in_specs=[pl...  3.24 us
  transfers between devices with their start and end apart: 3, of which 2 were waited for; matrix products, arithmetic and copies ran while one was open for 2% of the time, Pallas kernels for 0%

profile of v5, /device:TPU:1, one launch (start us, length us, event | category | flops | bytes accessed | tf_op | source)
XLA Modules:
  0.0 65.4 jit_solution(13248164712778237560)
XLA Ops:
  0.0 0.0 copy-start
  0.0 0.0 copy-start.2
  0.0 0.0 copy-start.1
  0.0 0.0 copy-start.3
  0.0 3.2 %group_sums.1 = (bf16[144,512]{1,0:T(8,128)(2,1)S(1)}, bf16[144,512]{1,0:T(8,128)(2,1)S(1)}, bf16[144,512]{1,0:T(8,128)(2,1)S(1)}, bf16[144,512]{1,0:T(8,128)(2,1)S(1)}) custom-call(s32[1]{0:T(128)} %bitcast.2.place_ref, s32[1,256]{1,0:T(1,128)} %bitcast.7, s32[16,256]{1,0:T(8,128)} %flags_hbm.1, bf16[16,256,512]{2,1,0:T(8,128)(2,1)} %vis_hbm.1), custom_call_target="tpu_custom_call" | custom-call | flops 134217728 | bytes 4194304 | tf_op jit(solution)/shard_map/group_sums/pallas_call | solution.py:97
  3.3 14.4 %collective-permute-start = (bf16[144,512]{1,0:T(8,128)(2,1)S(1)}, bf16[144,512]{1,0:T(8,128)(2,1)S(1)}, u32[]{:S(2)}, u32[]{:S(2)}) collective-permute-start(bf16[144,512]{1,0:T(8,128)(2,1)S(1)} %get-tuple-element.13), channel_id=1, source_target_pairs={{0,496},{8,504},{16,0},{24,8},{32,16},{40,24},{48,32},{56,40},{64,... | collective-permute-start | bytes 442376 | tf_op jit(solution)/shard_map/ppermute | solution.py:25
  17.7 2.2 %collective-permute-start.1 = (bf16[144,512]{1,0:T(8,128)(2,1)S(1)}, bf16[144,512]{1,0:T(8,128)(2,1)S(1)}, u32[]{:S(2)}, u32[]{:S(2)}) collective-permute-start(bf16[144,512]{1,0:T(8,128)(2,1)S(1)} %get-tuple-element.14), channel_id=1, source_target_pairs={{0,504},{8,0},{16,8},{24,16},{32,24},{40,32},{48,40},{56,48},{64,5... | collective-permute-start | bytes 442376 | tf_op jit(solution)/shard_map/ppermute | solution.py:25
  19.9 3.1 %collective-permute-start.2 = (bf16[144,512]{1,0:T(8,128)(2,1)S(1)}, bf16[144,512]{1,0:T(8,128)(2,1)S(1)}, u32[]{:S(2)}, u32[]{:S(2)}) collective-permute-start(bf16[144,512]{1,0:T(8,128)(2,1)S(1)} %get-tuple-element.15), channel_id=1, source_target_pairs={{0,8},{8,16},{16,24},{24,32},{32,40},{40,48},{48,56},{56,64},{64,7... | collective-permute-start | bytes 442376 | tf_op jit(solution)/shard_map/ppermute | solution.py:25
  23.0 0.0 copy-done.2
  23.0 0.1 reshape.384
  23.2 0.1 copy.13
  23.2 0.1 copy.14
  23.4 0.1 reshape.386
  23.4 0.0 copy-done
  23.4 0.0 copy-done.1
  23.4 0.0 copy-done.3
  23.4 0.6 convolution_convert_fusion.parts_ref
  24.1 0.1 fusion.9.spot_ref
  24.2 0.0 collective-permute-done.d_ref
  24.2 1.1 %collective-permute-done.1.c_ref = bf16[144,512]{1,0:T(8,128)(2,1)S(1)} collective-permute-done((bf16[144,512]{1,0:T(8,128)(2,1)S(1)}, bf16[144,512]{1,0:T(8,128)(2,1)S(1)}, u32[]{:S(2)}, u32[]{:S(2)}) %collective-permute-start.1) | collective-permute-done | bytes 147488 | tf_op jit(solution)/shard_map/ppermute | solution.py:25
  25.3 3.8 %collective-permute-done.2.a_ref = bf16[144,512]{1,0:T(8,128)(2,1)S(1)} collective-permute-done((bf16[144,512]{1,0:T(8,128)(2,1)S(1)}, bf16[144,512]{1,0:T(8,128)(2,1)S(1)}, u32[]{:S(2)}, u32[]{:S(2)}) %collective-permute-start.2) | collective-permute-done | bytes 147488 | tf_op jit(solution)/shard_map/ppermute | solution.py:25
  29.1 0.6 power_rows.1
  29.6 18.2 %all_to_all.10.in_ref = f32[64,4,128]{2,1,0:T(4,128)S(1)} all-to-all(f32[64,4,128]{2,1,0:T(4,128)S(1)} %power_rows.1), channel_id=1, replica_groups=mesh['y'=8,'z'=8,'ta'=8] {'z','ta'}, dimensions={0} | all-to-all | bytes 262144 | tf_op jit(solution)/shard_map/all_to_all | solution.py:29
  47.8 0.3 choose_rows.1
  48.1 16.6 %all_to_all.11.in_ref = f32[64,2,128]{2,1,0:T(2,128)S(1)} all-to-all(f32[64,2,128]{2,1,0:T(2,128)S(1)} %choose_rows.1), channel_id=1, replica_groups=mesh['y'=8,'z'=8,'ta'=8] {'y','ta'}, dimensions={0} | all-to-all | bytes 131072 | tf_op jit(solution)/shard_map/all_to_all | solution.py:29
  64.7 0.7 %unpack_rows.1 = f32[8,256]{1,0:T(8,128)} custom-call(f32[64,2,128]{2,1,0:T(2,128)S(1)} %all_to_all.11.in_ref), custom_call_target="tpu_custom_call" | custom-call | tf_op jit(solution)/shard_map/unpack_rows/pallas_call | solution.py:240
  (1 shorter events, 0.0 us)
Async XLA Ops:
  0.0 23.4 %copy-start = (f32[256,512]{1,0:T(8,128)S(1)}, f32[256,512]{1,0:T(8,128)}, u32[]{:S(2)}) copy-start(f32[256,512]{1,0:T(8,128)} %constant.89.clone) | copy-start | bytes 1572868
  0.0 23.0 %copy-start.2 = (s32[512]{0:T(512)S(1)}, s32[512]{0:T(512)}, u32[]{:S(2)}) copy-start(s32[512]{0:T(512)} %param.10) | copy-start | bytes 6148
  0.0 23.4 %copy-start.1 = (f32[256,256]{1,0:T(8,128)S(1)}, f32[256,256]{1,0:T(8,128)}, u32[]{:S(2)}) copy-start(f32[256,256]{1,0:T(8,128)} %param.12) | copy-start | bytes 786436
  0.0 23.4 %copy-start.3 = (f32[256]{0:T(256)S(1)}, f32[256]{0:T(256)}, u32[]{:S(2)}) copy-start(f32[256]{0:T(256)} %param.11) | copy-start | bytes 3076
  3.3 20.9 %collective-permute-start = (bf16[144,512]{1,0:T(8,128)(2,1)S(1)}, bf16[144,512]{1,0:T(8,128)(2,1)S(1)}, u32[]{:S(2)}, u32[]{:S(2)}) collective-permute-start(bf16[144,512]{1,0:T(8,128)(2,1)S(1)} %get-tuple-element.13), channel_id=1, source_target_pairs={{0,496},{8,504},{16,0},{24,8},{32,16},{40,24},{48,32},{56,40},{64,... | collective-permute-start | bytes 442376 | tf_op jit(solution)/shard_map/ppermute | solution.py:25
  17.7 7.6 %collective-permute-start.1 = (bf16[144,512]{1,0:T(8,128)(2,1)S(1)}, bf16[144,512]{1,0:T(8,128)(2,1)S(1)}, u32[]{:S(2)}, u32[]{:S(2)}) collective-permute-start(bf16[144,512]{1,0:T(8,128)(2,1)S(1)} %get-tuple-element.14), channel_id=1, source_target_pairs={{0,504},{8,0},{16,8},{24,16},{32,24},{40,32},{48,40},{56,48},{64,5... | collective-permute-start | bytes 442376 | tf_op jit(solution)/shard_map/ppermute | solution.py:25
  19.9 9.2 %collective-permute-start.2 = (bf16[144,512]{1,0:T(8,128)(2,1)S(1)}, bf16[144,512]{1,0:T(8,128)(2,1)S(1)}, u32[]{:S(2)}, u32[]{:S(2)}) collective-permute-start(bf16[144,512]{1,0:T(8,128)(2,1)S(1)} %get-tuple-element.15), channel_id=1, source_target_pairs={{0,8},{8,16},{16,24},{24,32},{32,40},{40,48},{48,56},{56,64},{64,7... | collective-permute-start | bytes 442376 | tf_op jit(solution)/shard_map/ppermute | solution.py:25

commit v6 on v4

--- a/solution.py
+++ b/solution.py
@@ -14,18 +14,15 @@
 SPAN = 4
 LANES = 128
 BLOCK_AXES = ("y", "z")
+TIME_AXES = ("x", "core")
 COUNT_ROWS = 16
-TOGETHER = 4
-
-
-def opposed(shard, by):
-    blocks, times = lax.axis_size(BLOCK_AXES), lax.axis_size("ta")
-    pairs = []
-    for block in range(blocks):
-        for time in range(times):
-            target = (block + (-by if time % 2 else by)) % blocks
-            pairs.append((block * times + time, target * times + time))
-    return lax.ppermute(shard, (*BLOCK_AXES, "ta"), pairs)
+SLICE = 64
+TOGETHER = 8
+
+
+def shifted(shard, by):
+    devices = lax.axis_size(BLOCK_AXES)
+    return lax.ppermute(shard, BLOCK_AXES, [(i, (i + by) % devices) for i in range(devices)])
 
 
 def exchange(chunks, axis):
@@ -66,7 +63,6 @@
     ids = ids_ref[...]
     back = place_ref[0] - (ids >> 3)
     back = jnp.where(back < 0, back + block_total, back)
-    back = jnp.where(place_ref[1] == 1, SPAN - 1 - back, back)
     row = lax.broadcasted_iota(jnp.int32, (SPAN * GR_DEV, ids.shape[1]), 0)
     onehot = (row == back * GR_DEV + (ids & (GR_DEV - 1))).astype(jnp.float32)
     lane = lax.broadcasted_iota(jnp.int32, (SPAN * GR_DEV, LANES), 1)
@@ -119,9 +115,10 @@
     return b * a + c * (a + b) + d * (a + b + c)
 
 
-def power_kernel(parts_ref, a_ref, b_ref, c_ref, d_ref, out_ref):
+def power_kernel(parts_ref, d_ref, c_ref, a_ref, b_ref, out_ref):
     channels = parts_ref.shape[0]
     rows = a_ref.shape[0] - COUNT_ROWS
+    slices = channels // SLICE
     cosines = parts_ref[:, :channels]
     sines = parts_ref[:, channels:]
 
@@ -137,59 +134,95 @@
     power = jnp.sum(pairs.reshape(rows // GR_DEV, GR_DEV, channels), axis=0)
     counts = [ref[rows:, :LANES].astype(jnp.float32)[:GR_DEV] for ref in (a_ref, b_ref, c_ref, d_ref)]
     count = jnp.sum(pair_sum(*counts), axis=1, keepdims=True)
-    result = jnp.concatenate([power, jnp.broadcast_to(count, (GR_DEV, LANES))], axis=1)
-    for copy in range(out_ref.shape[0]):
-        out_ref[copy] = result
-
-
-def power_rows(parts, blocks, copies):
-    channels = parts.shape[0]
-    rows = sum(block.shape[0] - COUNT_ROWS for block in blocks)
+    count = jnp.broadcast_to(count, (GR_DEV, LANES))
+    low = lax.broadcasted_iota(jnp.int32, (GR_DEV, LANES), 1) < SLICE
+    for j in range(slices):
+        lanes = power[:, j * SLICE // LANES * LANES :][:, :LANES]
+        if j % 2:
+            lanes = pltpu.roll(lanes, SLICE, 1)
+        chunk = jnp.where(low, lanes, count)
+        for copy in range(out_ref.shape[0] // slices):
+            out_ref[copy * slices + j] = chunk
+
+
+def choose_kernel(slices, spot_ref, in_ref, out_ref):
+    rows = []
+    for z in range(in_ref.shape[0] // slices):
+        total = in_ref[z * slices]
+        for x in range(1, slices):
+            total = total + in_ref[z * slices + x]
+        rows.append(total)
+    rows = jnp.concatenate(rows, axis=0)
+    column = lax.broadcasted_iota(jnp.int32, (spot_ref.shape[0], rows.shape[0]), 1)
+    chosen = exact_dot((spot_ref[...] == column).astype(jnp.float32), rows)
+    for y in range(out_ref.shape[0] // slices):
+        for copy in range(slices):
+            out_ref[y * slices + copy] = chosen[y * GR_DEV : (y + 1) * GR_DEV]
+
+
+def join_kernel(slices, in_ref, out_ref):
+    low = lax.broadcasted_iota(jnp.int32, (GR_DEV, LANES), 1) < SLICE
+    totals = []
+    for x in range(slices):
+        total = in_ref[x]
+        for y in range(1, in_ref.shape[0] // slices):
+            total = total + in_ref[y * slices + x]
+        totals.append(total)
+    for pair in range(slices // 2):
+        after = pltpu.roll(totals[2 * pair + 1], SLICE, 1)
+        out_ref[:, pair * LANES : (pair + 1) * LANES] = jnp.where(low, totals[2 * pair], after)
+    out_ref[:, slices // 2 * LANES :] = jnp.where(low, pltpu.roll(totals[0], SLICE, 1), totals[0])
+
+
+def small_call(kernel, shape, name):
     return pl.pallas_call(
-        power_kernel,
-        out_shape=jax.ShapeDtypeStruct((copies, GR_DEV, channels + LANES), jnp.float32),
+        kernel,
+        out_shape=jax.ShapeDtypeStruct(shape, jnp.float32),
         compiler_params=pltpu.CompilerParams(vmem_limit_bytes=16 << 20),
-        cost_estimate=pl.CostEstimate(flops=8 * rows * channels * channels, bytes_accessed=2 << 20, transcendentals=0),
-        name="power_rows",
-    )(parts, *blocks)
+        name=name,
+    )
 
 
 def on_device(visibilities, flags, group_ids, group_order, taper, inv_cov):
     channels = taper.shape[0]
-    y_size, z_size, times = (lax.axis_size(axis) for axis in ("y", "z", "ta"))
+    y_size, z_size, slices = (lax.axis_size(axis) for axis in ("y", "z", "x"))
     block_total = y_size * z_size
-    core = lax.axis_index("ta") % 2
-    place = jnp.stack([lax.axis_index(BLOCK_AXES), core])
-
+
+    place = lax.axis_index(BLOCK_AXES)[None]
     blocks = group_sums(visibilities, flags, group_ids, place, block_total)
-    blocks = [opposed(block, by) if by else block for block, by in zip(blocks, (-2, -1, 1, 0))]
-    rows = power_rows(transform_parts(taper, inv_cov), blocks, z_size)
-
-    plane = exchange(rows, "z").reshape(z_size * GR_DEV, channels + LANES)
+    blocks = [shifted(block, by) if by else block for block, by in zip(blocks, (-2, -1, 1, 0))]
+    parts = transform_parts(taper, inv_cov)
+
     order = group_order.reshape(y_size, z_size, GR_DEV)
-    wanted = lax.dynamic_index_in_dim(order, lax.axis_index("z"), 1, keepdims=False).reshape(-1)
-    holder = (wanted // GR_DEV + 1 + core) % block_total
-    spot = jnp.where(
-        holder // z_size == lax.axis_index("y"), holder % z_size * GR_DEV + wanted % GR_DEV, -1
-    )
-    pick = spot[:, None] == jnp.arange(z_size * GR_DEV, dtype=jnp.int32)[None, :]
-    chosen = exact_dot(pick.astype(jnp.float32), plane).reshape(y_size, GR_DEV, channels + LANES)
-    found = exchange(chosen, "y").reshape(y_size * GR_DEV, channels + LANES)
-
-    fold = np.tile(np.eye(GR_DEV, dtype=np.float32), (times, y_size))
-    partial = exact_dot(jnp.asarray(fold), found).reshape(times, GR_DEV, channels + LANES)
-    totals = jnp.sum(exchange(partial, "ta"), axis=0)
+    wanted = lax.dynamic_index_in_dim(order, lax.axis_index("z"), 1, keepdims=False).reshape(-1, 1)
+    holder = (wanted // GR_DEV + 1) % block_total
+    spot = holder % z_size * GR_DEV + wanted % GR_DEV
+    spot = jnp.where(holder // z_size == lax.axis_index("y"), spot, -1)
+    parts, spot = lax.optimization_barrier((parts, spot))
+
+    power = small_call(power_kernel, (z_size * slices, GR_DEV, LANES), "power_rows")(parts, *blocks)
+    choose = functools.partial(choose_kernel, slices)
+    shape = (y_size * slices, GR_DEV, LANES)
+    chosen = small_call(choose, shape, "choose_rows")(spot, exchange(power, ("z", "x")))
+
+    join = functools.partial(join_kernel, slices)
+    found = exchange(chosen, ("y", "x"))
+    partial = small_call(join, (GR_DEV, channels + LANES), "join_slices")(found)
+
+    totals = partial + lax.ppermute(partial, "core", [(0, 1), (1, 0)])
     return totals[:, :channels] / jnp.maximum(totals[:, channels : channels + 1], 1.0)
 
 
 def solution(mesh):
     blocks, times = mesh.devices.shape
     y_size = 2 ** (int(math.log2(blocks)) // 2)
-    cut = Mesh(mesh.devices.reshape(y_size, blocks // y_size, times), ("y", "z", "ta"))
+    cut = Mesh(
+        mesh.devices.reshape(y_size, blocks // y_size, times // 2, 2), ("y", "z", "x", "core")
+    )
     return jax.shard_map(
         on_device,
         mesh=cut,
-        in_specs=(P("ta", BLOCK_AXES, None), P("ta", BLOCK_AXES), P(BLOCK_AXES), P(), P(), P()),
+        in_specs=(P(TIME_AXES, BLOCK_AXES, None), P(TIME_AXES, BLOCK_AXES), P(BLOCK_AXES), P(), P(), P()),
         out_specs=P(BLOCK_AXES, None),
         check_vma=False,
     )

time: 68.7 us -> 67.3 us (0.980)
  waiting for transfers between devices: 10.7 us -> 5.94 us
  starting transfers between devices: 21.6 us -> 25.8 us
  Pallas kernels: 5.07 us -> 4.06 us
  blocking collectives: 28.7 us -> 29.4 us
    ppermute x3 -> x4, starting transfers between devices: 18.2 us -> 25.8 us  [the longest x3 19.7 us: shifted(): lax.ppermute(shard, BLOCK_AXES, [(i, (i + by) % devices) for i in range(d...]
    all_to_all x1 -> x0, waiting for transfers between devices: 7.45 us -> none  [exchange(): return lax.all_to_all(chunks, axis, 0, 0, tiled=True)]
    all_to_all x1 -> x0, starting transfers between devices: 3.36 us -> none  [exchange(): return lax.all_to_all(chunks, axis, 0, 0, tiled=True)]
    ppermute x3 -> x4, waiting for transfers between devices: 3.21 us -> 5.94 us  [the longest x3 5.13 us: shifted(): lax.ppermute(shard, BLOCK_AXES, [(i, (i + by) % devices) for i in range(d...]
    pallas_call x1, Pallas kernels: 3.98 us -> 3.24 us  [group_sums(): pl.pallas_call(functools.partial(group_kernel, block_total), in_specs=[pl...]
where the time goes in v6:
time: 67.3 us; the launch traced here: 67.1 us
  blocking collectives  29.4 us (44%)
  starting transfers between devices  25.8 us (38%)
  waiting for transfers between devices  5.94 us (9%)
  Pallas kernels  4.06 us (6%)
  other arithmetic  0.89 us (1%)
    all_to_all x2, blocking collectives, exchange(): return lax.all_to_all(chunks, axis, 0, 0, tiled=True)  29.4 us
    ppermute x3, starting transfers between devices, shifted(): lax.ppermute(shard, BLOCK_AXES, [(i, (i + by) % devices) for i in range(d...  19.7 us
    ppermute x1, starting transfers between devices, on_device(): totals = partial + lax.ppermute(partial, 'core', [(0, 1), (1, 0)])  6.14 us
    ppermute x3, waiting for transfers between devices, shifted(): lax.ppermute(shard, BLOCK_AXES, [(i, (i + by) % devices) for i in range(d...  5.13 us
    pallas_call x1, Pallas kernels, group_sums(): pl.pallas_call(functools.partial(group_kernel, block_total), in_specs=[pl...  3.24 us
  transfers between devices with their start and end apart: 4, of which 3 were waited for; matrix products, arithmetic and copies ran while one was open for 1% of the time, Pallas kernels for 0%

profile of v6, /device:TPU:1, one launch (start us, length us, event | category | flops | bytes accessed | tf_op | source)
XLA Modules:
  0.0 67.1 jit_solution(2826232880837065279)
XLA Ops:
  0.0 0.0 copy-start
  0.0 0.0 copy-start.2
  0.0 0.0 copy-start.1
  0.0 0.0 copy-start.3
  0.0 3.2 %group_sums.1 = (bf16[144,512]{1,0:T(8,128)(2,1)S(1)}, bf16[144,512]{1,0:T(8,128)(2,1)S(1)}, bf16[144,512]{1,0:T(8,128)(2,1)S(1)}, bf16[144,512]{1,0:T(8,128)(2,1)S(1)}) custom-call(s32[1]{0:T(128)} %bitcast.place_ref, s32[1,256]{1,0:T(1,128)} %bitcast.3, s32[16,256]{1,0:T(8,128)} %flags_hbm.1, bf16[16,256,512]{2,1,0:T(8,128)(2,1)} %vis_hbm.1), custom_call_target="tpu_custom_call" | custom-call | flops 134217728 | bytes 4194304 | tf_op jit(solution)/shard_map/group_sums/pallas_call | solution.py:97
  3.3 14.4 %collective-permute-start = (bf16[144,512]{1,0:T(8,128)(2,1)S(1)}, bf16[144,512]{1,0:T(8,128)(2,1)S(1)}, u32[]{:S(2)}, u32[]{:S(2)}) collective-permute-start(bf16[144,512]{1,0:T(8,128)(2,1)S(1)} %get-tuple-element.13), channel_id=1, source_target_pairs={{0,496},{8,504},{16,0},{24,8},{32,16},{40,24},{48,32},{56,40},{64,... | collective-permute-start | bytes 442376 | tf_op jit(solution)/shard_map/ppermute | solution.py:25
  17.7 2.2 %collective-permute-start.1 = (bf16[144,512]{1,0:T(8,128)(2,1)S(1)}, bf16[144,512]{1,0:T(8,128)(2,1)S(1)}, u32[]{:S(2)}, u32[]{:S(2)}) collective-permute-start(bf16[144,512]{1,0:T(8,128)(2,1)S(1)} %get-tuple-element.14), channel_id=1, source_target_pairs={{0,504},{8,0},{16,8},{24,16},{32,24},{40,32},{48,40},{56,48},{64,5... | collective-permute-start | bytes 442376 | tf_op jit(solution)/shard_map/ppermute | solution.py:25
  19.9 3.1 %collective-permute-start.2 = (bf16[144,512]{1,0:T(8,128)(2,1)S(1)}, bf16[144,512]{1,0:T(8,128)(2,1)S(1)}, u32[]{:S(2)}, u32[]{:S(2)}) collective-permute-start(bf16[144,512]{1,0:T(8,128)(2,1)S(1)} %get-tuple-element.15), channel_id=1, source_target_pairs={{0,8},{8,16},{16,24},{24,32},{32,40},{40,48},{48,56},{56,64},{64,7... | collective-permute-start | bytes 442376 | tf_op jit(solution)/shard_map/ppermute | solution.py:25
  23.0 0.0 copy-done.2
  23.0 0.1 reshape.289
  23.1 0.1 reshape.291
  23.2 0.0 copy-done
  23.2 0.0 copy-done.1
  23.2 0.0 copy-done.3
  23.2 0.6 convolution_convert_fusion.parts_ref
  23.8 0.1 fusion.7.spot_ref
  23.9 0.0 collective-permute-done.d_ref
  23.9 1.4 %collective-permute-done.1.c_ref = bf16[144,512]{1,0:T(8,128)(2,1)S(1)} collective-permute-done((bf16[144,512]{1,0:T(8,128)(2,1)S(1)}, bf16[144,512]{1,0:T(8,128)(2,1)S(1)}, u32[]{:S(2)}, u32[]{:S(2)}) %collective-permute-start.1) | collective-permute-done | bytes 147488 | tf_op jit(solution)/shard_map/ppermute | solution.py:25
  25.3 3.8 %collective-permute-done.2.a_ref = bf16[144,512]{1,0:T(8,128)(2,1)S(1)} collective-permute-done((bf16[144,512]{1,0:T(8,128)(2,1)S(1)}, bf16[144,512]{1,0:T(8,128)(2,1)S(1)}, u32[]{:S(2)}, u32[]{:S(2)}) %collective-permute-start.2) | collective-permute-done | bytes 147488 | tf_op jit(solution)/shard_map/ppermute | solution.py:25
  29.1 0.5 power_rows.1
  29.6 13.6 %all_to_all.10.in_ref = f32[32,8,128]{2,1,0:T(8,128)S(1)} all-to-all(f32[32,8,128]{2,1,0:T(8,128)S(1)} %power_rows.1), channel_id=1, replica_groups=mesh['y'=8,'z'=8,'x'=4,'core'=2] {'z','x'}, dimensions={0} | all-to-all | bytes 262144 | tf_op jit(solution)/shard_map/all_to_all | solution.py:29
  43.2 0.2 choose_rows.1
  43.4 15.8 %all_to_all.11.in_ref = f32[32,8,128]{2,1,0:T(8,128)S(1)} all-to-all(f32[32,8,128]{2,1,0:T(8,128)S(1)} %choose_rows.1), channel_id=1, replica_groups=mesh['y'=8,'z'=8,'x'=4,'core'=2] {'y','x'}, dimensions={0} | all-to-all | bytes 262144 | tf_op jit(solution)/shard_map/all_to_all | solution.py:29
  59.2 0.1 join_slices.1
  59.3 6.1 %collective-permute-start.3 = (f32[8,384]{1,0:T(8,128)S(1)}, f32[8,384]{1,0:T(8,128)S(1)}, u32[]{:S(2)}, u32[]{:S(2)}) collective-permute-start(f32[8,384]{1,0:T(8,128)S(1)} %join_slices.1), channel_id=1, source_target_pairs={{0,1},{1,0},{2,3},{3,2},{4,5},{5,4},{6,7},{7,6},{8,9},{9,8},{10,11... | collective-permute-start | bytes 36872 | tf_op jit(solution)/shard_map/ppermute | solution.py:212
  65.4 0.8 %collective-permute-done.3 = f32[8,384]{1,0:T(8,128)S(1)} collective-permute-done((f32[8,384]{1,0:T(8,128)S(1)}, f32[8,384]{1,0:T(8,128)S(1)}, u32[]{:S(2)}, u32[]{:S(2)}) %collective-permute-start.3) | collective-permute-done | bytes 12320 | tf_op jit(solution)/shard_map/ppermute | solution.py:212
  66.3 0.1 fusion.11
  66.4 0.7 %slice_divide_fusion = f32[8,256]{1,0:T(8,128)} fusion(f32[8,384]{1,0:T(8,128)S(1)} %add.96, f32[8]{0:T(128)S(1)} %fusion.11), kind=kLoop, calls=%fused_computation.27 | loop fusion | flops 2048 | bytes 16416 | tf_op jit(solution)/shard_map/div | solution.py:213
  (2 shorter events, 0.0 us)
Async XLA Ops:
  0.0 23.2 %copy-start = (f32[256,512]{1,0:T(8,128)S(1)}, f32[256,512]{1,0:T(8,128)}, u32[]{:S(2)}) copy-start(f32[256,512]{1,0:T(8,128)} %constant.71.clone) | copy-start | bytes 1572868
  0.0 23.0 %copy-start.2 = (s32[512]{0:T(512)S(1)}, s32[512]{0:T(512)}, u32[]{:S(2)}) copy-start(s32[512]{0:T(512)} %param.10) | copy-start | bytes 6148
  0.0 23.2 %copy-start.1 = (f32[256,256]{1,0:T(8,128)S(1)}, f32[256,256]{1,0:T(8,128)}, u32[]{:S(2)}) copy-start(f32[256,256]{1,0:T(8,128)} %param.12) | copy-start | bytes 786436
  0.0 23.2 %copy-start.3 = (f32[256]{0:T(256)S(1)}, f32[256]{0:T(256)}, u32[]{:S(2)}) copy-start(f32[256]{0:T(256)} %param.11) | copy-start | bytes 3076
  3.3 20.7 %collective-permute-start = (bf16[144,512]{1,0:T(8,128)(2,1)S(1)}, bf16[144,512]{1,0:T(8,128)(2,1)S(1)}, u32[]{:S(2)}, u32[]{:S(2)}) collective-permute-start(bf16[144,512]{1,0:T(8,128)(2,1)S(1)} %get-tuple-element.13), channel_id=1, source_target_pairs={{0,496},{8,504},{16,0},{24,8},{32,16},{40,24},{48,32},{56,40},{64,... | collective-permute-start | bytes 442376 | tf_op jit(solution)/shard_map/ppermute | solution.py:25
  17.7 7.6 %collective-permute-start.1 = (bf16[144,512]{1,0:T(8,128)(2,1)S(1)}, bf16[144,512]{1,0:T(8,128)(2,1)S(1)}, u32[]{:S(2)}, u32[]{:S(2)}) collective-permute-start(bf16[144,512]{1,0:T(8,128)(2,1)S(1)} %get-tuple-element.14), channel_id=1, source_target_pairs={{0,504},{8,0},{16,8},{24,16},{32,24},{40,32},{48,40},{56,48},{64,5... | collective-permute-start | bytes 442376 | tf_op jit(solution)/shard_map/ppermute | solution.py:25
  19.9 9.2 %collective-permute-start.2 = (bf16[144,512]{1,0:T(8,128)(2,1)S(1)}, bf16[144,512]{1,0:T(8,128)(2,1)S(1)}, u32[]{:S(2)}, u32[]{:S(2)}) collective-permute-start(bf16[144,512]{1,0:T(8,128)(2,1)S(1)} %get-tuple-element.15), channel_id=1, source_target_pairs={{0,8},{8,16},{16,24},{24,32},{32,40},{40,48},{48,56},{56,64},{64,7... | collective-permute-start | bytes 442376 | tf_op jit(solution)/shard_map/ppermute | solution.py:25
  59.3 7.0 %collective-permute-start.3 = (f32[8,384]{1,0:T(8,128)S(1)}, f32[8,384]{1,0:T(8,128)S(1)}, u32[]{:S(2)}, u32[]{:S(2)}) collective-permute-start(f32[8,384]{1,0:T(8,128)S(1)} %join_slices.1), channel_id=1, source_target_pairs={{0,1},{1,0},{2,3},{3,2},{4,5},{5,4},{6,7},{7,6},{8,9},{9,8},{10,11... | collective-permute-start | bytes 36872 | tf_op jit(solution)/shard_map/ppermute | solution.py:212

commit v7 on v6

--- a/solution.py
+++ b/solution.py
@@ -20,9 +20,15 @@
 TOGETHER = 8
 
 
-def shifted(shard, by):
-    devices = lax.axis_size(BLOCK_AXES)
-    return lax.ppermute(shard, BLOCK_AXES, [(i, (i + by) % devices) for i in range(devices)])
+def opposed(shard, by):
+    blocks = lax.axis_size(BLOCK_AXES)
+    times = lax.axis_size(TIME_AXES)
+    pairs = []
+    for block in range(blocks):
+        for time in range(times):
+            target = (block + (by if time % 2 else -by)) % blocks
+            pairs.append((block * times + time, target * times + time))
+    return lax.ppermute(shard, (*BLOCK_AXES, *TIME_AXES), pairs)
 
 
 def exchange(chunks, axis):
@@ -63,6 +69,7 @@
     ids = ids_ref[...]
     back = place_ref[0] - (ids >> 3)
     back = jnp.where(back < 0, back + block_total, back)
+    back = jnp.where(place_ref[1] == 0, SPAN - 1 - back, back)
     row = lax.broadcasted_iota(jnp.int32, (SPAN * GR_DEV, ids.shape[1]), 0)
     onehot = (row == back * GR_DEV + (ids & (GR_DEV - 1))).astype(jnp.float32)
     lane = lax.broadcasted_iota(jnp.int32, (SPAN * GR_DEV, LANES), 1)
@@ -134,44 +141,83 @@
     power = jnp.sum(pairs.reshape(rows // GR_DEV, GR_DEV, channels), axis=0)
     counts = [ref[rows:, :LANES].astype(jnp.float32)[:GR_DEV] for ref in (a_ref, b_ref, c_ref, d_ref)]
     count = jnp.sum(pair_sum(*counts), axis=1, keepdims=True)
-    count = jnp.broadcast_to(count, (GR_DEV, LANES))
-    low = lax.broadcasted_iota(jnp.int32, (GR_DEV, LANES), 1) < SLICE
+    count = pack_counts(count)
+    low = low_lanes(1)
     for j in range(slices):
         lanes = power[:, j * SLICE // LANES * LANES :][:, :LANES]
-        if j % 2:
-            lanes = pltpu.roll(lanes, SLICE, 1)
-        chunk = jnp.where(low, lanes, count)
+        turned = pltpu.roll(lanes, SLICE, 1)
+        first, second = (turned, lanes) if j % 2 else (lanes, turned)
         for copy in range(out_ref.shape[0] // slices):
-            out_ref[copy * slices + j] = chunk
+            store_chunk(out_ref, copy * slices + j, first, second, count)
+
+
+def low_lanes(rows):
+    return lax.broadcasted_iota(jnp.int32, (rows, LANES), 1) < SLICE
+
+
+def count_lanes(rows):
+    lane = lax.broadcasted_iota(jnp.int32, (rows, LANES), 1)
+    return lane == lax.broadcasted_iota(jnp.int32, (rows, LANES), 0) % GR_DEV * (LANES // GR_DEV)
+
+
+def pack_counts(count):
+    return jnp.sum(jnp.where(count_lanes(GR_DEV), count, 0.0), axis=0, keepdims=True)
+
+
+def store_chunk(out_ref, index, first, second, count):
+    low = low_lanes(1)
+    for i in range(GR_DEV // 2):
+        row = jnp.where(low, first[2 * i : 2 * i + 1], second[2 * i + 1 : 2 * i + 2])
+        out_ref[index, :, i * LANES : (i + 1) * LANES] = row
+    out_ref[index, :, GR_DEV // 2 * LANES :] = count
 
 
 def choose_kernel(slices, spot_ref, in_ref, out_ref):
-    rows = []
+    planes = []
     for z in range(in_ref.shape[0] // slices):
         total = in_ref[z * slices]
         for x in range(1, slices):
             total = total + in_ref[z * slices + x]
-        rows.append(total)
-    rows = jnp.concatenate(rows, axis=0)
-    column = lax.broadcasted_iota(jnp.int32, (spot_ref.shape[0], rows.shape[0]), 1)
-    chosen = exact_dot((spot_ref[...] == column).astype(jnp.float32), rows)
+        planes.append(total)
+    planes = jnp.concatenate(planes, axis=0)
+    spot = spot_ref[...]
+    member = spot & (GR_DEV - 1)
+    column = lax.broadcasted_iota(jnp.int32, (spot.shape[0], planes.shape[0]), 1)
+    found = exact_dot((spot >> 3 == column).astype(jnp.float32), planes)
+    lanes = jnp.zeros((spot.shape[0], LANES), jnp.float32)
+    for i in range(GR_DEV // 2):
+        lanes = jnp.where(member >> 1 == i, found[:, i * LANES : (i + 1) * LANES], lanes)
+    turned = pltpu.roll(lanes, SLICE, 1)
+    first = jnp.where(member & 1 == 0, lanes, turned)
+    second = jnp.where(member & 1 == 0, turned, lanes)
+    lane = lax.broadcasted_iota(jnp.int32, lanes.shape, 1)
+    count = jnp.where(lane == member * (LANES // GR_DEV), found[:, GR_DEV // 2 * LANES :], 0.0)
+    count = jnp.sum(count, axis=1, keepdims=True)
     for y in range(out_ref.shape[0] // slices):
+        rows = slice(y * GR_DEV, (y + 1) * GR_DEV)
+        packed = pack_counts(count[rows])
         for copy in range(slices):
-            out_ref[y * slices + copy] = chosen[y * GR_DEV : (y + 1) * GR_DEV]
+            store_chunk(out_ref, y * slices + copy, first[rows], second[rows], packed)
 
 
 def join_kernel(slices, in_ref, out_ref):
-    low = lax.broadcasted_iota(jnp.int32, (GR_DEV, LANES), 1) < SLICE
     totals = []
     for x in range(slices):
         total = in_ref[x]
         for y in range(1, in_ref.shape[0] // slices):
             total = total + in_ref[y * slices + x]
         totals.append(total)
+    low = low_lanes(1)
     for pair in range(slices // 2):
-        after = pltpu.roll(totals[2 * pair + 1], SLICE, 1)
-        out_ref[:, pair * LANES : (pair + 1) * LANES] = jnp.where(low, totals[2 * pair], after)
-    out_ref[:, slices // 2 * LANES :] = jnp.where(low, pltpu.roll(totals[0], SLICE, 1), totals[0])
+        rows = []
+        for i in range(GR_DEV // 2):
+            left, right = (totals[2 * pair + k][:, i * LANES : (i + 1) * LANES] for k in range(2))
+            rows.append(jnp.where(low, left, pltpu.roll(right, SLICE, 1)))
+            rows.append(jnp.where(low, pltpu.roll(left, SLICE, 1), right))
+        out_ref[:, pair * LANES : (pair + 1) * LANES] = jnp.concatenate(rows, axis=0)
+    count = jnp.broadcast_to(totals[0][:, GR_DEV // 2 * LANES :], (GR_DEV, LANES))
+    count = jnp.sum(jnp.where(count_lanes(GR_DEV), count, 0.0), axis=1, keepdims=True)
+    out_ref[:, slices // 2 * LANES :] = jnp.broadcast_to(count, (GR_DEV, LANES))
 
 
 def small_call(kernel, shape, name):
@@ -187,22 +233,24 @@
     channels = taper.shape[0]
     y_size, z_size, slices = (lax.axis_size(axis) for axis in ("y", "z", "x"))
     block_total = y_size * z_size
-
-    place = lax.axis_index(BLOCK_AXES)[None]
+    width = GR_DEV * SLICE + LANES
+
+    core = lax.axis_index("core")
+    place = jnp.stack([lax.axis_index(BLOCK_AXES), core])
     blocks = group_sums(visibilities, flags, group_ids, place, block_total)
-    blocks = [shifted(block, by) if by else block for block, by in zip(blocks, (-2, -1, 1, 0))]
+    blocks = [opposed(block, by) if by else block for block, by in zip(blocks, (-2, -1, 1, 0))]
     parts = transform_parts(taper, inv_cov)
 
     order = group_order.reshape(y_size, z_size, GR_DEV)
     wanted = lax.dynamic_index_in_dim(order, lax.axis_index("z"), 1, keepdims=False).reshape(-1, 1)
-    holder = (wanted // GR_DEV + 1) % block_total
+    holder = (wanted // GR_DEV + 2 - core) % block_total
     spot = holder % z_size * GR_DEV + wanted % GR_DEV
-    spot = jnp.where(holder // z_size == lax.axis_index("y"), spot, -1)
+    spot = jnp.where(holder // z_size == lax.axis_index("y"), spot, z_size * GR_DEV)
     parts, spot = lax.optimization_barrier((parts, spot))
 
-    power = small_call(power_kernel, (z_size * slices, GR_DEV, LANES), "power_rows")(parts, *blocks)
+    power = small_call(power_kernel, (z_size * slices, 1, width), "power_rows")(parts, *blocks)
     choose = functools.partial(choose_kernel, slices)
-    shape = (y_size * slices, GR_DEV, LANES)
+    shape = (y_size * slices, 1, width)
     chosen = small_call(choose, shape, "choose_rows")(spot, exchange(power, ("z", "x")))
 
     join = functools.partial(join_kernel, slices)

time: 67.3 us -> 66.7 us (level)
  blocking collectives: 29.4 us -> 27 us
  starting transfers between devices: 25.8 us -> 26.7 us
  Pallas kernels: 4.06 us -> 4.92 us
    all_to_all x2, blocking collectives: 29.4 us -> 27 us  [exchange(): return lax.all_to_all(chunks, axis, 0, 0, tiled=True)]
    ppermute x1, starting transfers between devices: 6.14 us -> 6.99 us  [on_device(): totals = partial + lax.ppermute(partial, 'core', [(0, 1), (1, 0)])]
where the time goes in v7:
time: 66.7 us; the launch traced here: 66.4 us
  blocking collectives  27 us (40%)
  starting transfers between devices  26.7 us (40%)
  waiting for transfers between devices  5.94 us (9%)
  Pallas kernels  4.92 us (7%)
  other arithmetic  0.96 us (1%)
    all_to_all x2, blocking collectives, exchange(): return lax.all_to_all(chunks, axis, 0, 0, tiled=True)  27 us
    ppermute x3, starting transfers between devices, opposed(): return lax.ppermute(shard, (*BLOCK_AXES, *TIME_AXES), pairs)  19.7 us
    ppermute x1, starting transfers between devices, on_device(): totals = partial + lax.ppermute(partial, 'core', [(0, 1), (1, 0)])  6.99 us
    ppermute x3, waiting for transfers between devices, opposed(): return lax.ppermute(shard, (*BLOCK_AXES, *TIME_AXES), pairs)  5.13 us
    pallas_call x1, Pallas kernels, group_sums(): pl.pallas_call(functools.partial(group_kernel, block_total), in_specs=[pl...  3.78 us
  transfers between devices with their start and end apart: 4, of which 3 were waited for; matrix products, arithmetic and copies ran while one was open for 1% of the time, Pallas kernels for 0%

profile of v7, /device:TPU:1, one launch (start us, length us, event | category | flops | bytes accessed | tf_op | source)
XLA Modules:
  0.0 66.4 jit_solution(15381473505363545827)
XLA Ops:
  0.0 0.0 copy-start
  0.0 0.0 copy-start.2
  0.0 0.0 copy-start.1
  0.0 0.0 copy-start.3
  0.0 0.1 pad_add_fusion.place_ref
  0.1 3.8 %group_sums.1 = (bf16[144,512]{1,0:T(8,128)(2,1)S(1)}, bf16[144,512]{1,0:T(8,128)(2,1)S(1)}, bf16[144,512]{1,0:T(8,128)(2,1)S(1)}, bf16[144,512]{1,0:T(8,128)(2,1)S(1)}) custom-call(s32[2]{0:T(128)S(1)} %pad_add_fusion.place_ref, s32[1,256]{1,0:T(1,128)} %bitcast.4, s32[16,256]{1,0:T(8,128)} %flags_hbm.1, bf16[16,256,512]{2,1,0:T(8,128)(2,1)} %vis_hbm.1), custom_call_target="tpu_custom_call" | custom-call | flops 134217728 | bytes 4194304 | tf_op jit(solution)/shard_map/group_sums/pallas_call | solution.py:104
  3.9 14.4 %collective-permute-start = (bf16[144,512]{1,0:T(8,128)(2,1)S(1)}, bf16[144,512]{1,0:T(8,128)(2,1)S(1)}, u32[]{:S(2)}, u32[]{:S(2)}) collective-permute-start(bf16[144,512]{1,0:T(8,128)(2,1)S(1)} %get-tuple-element.13), channel_id=1, source_target_pairs={{0,16},{1,497},{2,18},{3,499},{4,20},{5,501},{6,22},{7,503},{8,24}... | collective-permute-start | bytes 442376 | tf_op jit(solution)/shard_map/ppermute | solution.py:31
  18.3 2.2 %collective-permute-start.1 = (bf16[144,512]{1,0:T(8,128)(2,1)S(1)}, bf16[144,512]{1,0:T(8,128)(2,1)S(1)}, u32[]{:S(2)}, u32[]{:S(2)}) collective-permute-start(bf16[144,512]{1,0:T(8,128)(2,1)S(1)} %get-tuple-element.14), channel_id=1, source_target_pairs={{0,8},{1,505},{2,10},{3,507},{4,12},{5,509},{6,14},{7,511},{8,16},... | collective-permute-start | bytes 442376 | tf_op jit(solution)/shard_map/ppermute | solution.py:31
  20.5 3.1 %collective-permute-start.2 = (bf16[144,512]{1,0:T(8,128)(2,1)S(1)}, bf16[144,512]{1,0:T(8,128)(2,1)S(1)}, u32[]{:S(2)}, u32[]{:S(2)}) collective-permute-start(bf16[144,512]{1,0:T(8,128)(2,1)S(1)} %get-tuple-element.15), channel_id=1, source_target_pairs={{0,504},{1,9},{2,506},{3,11},{4,508},{5,13},{6,510},{7,15},{8,0},{... | collective-permute-start | bytes 442376 | tf_op jit(solution)/shard_map/ppermute | solution.py:31
  23.6 0.0 copy-done.2
  23.6 0.1 reshape.293
  23.7 0.1 reshape.295
  23.8 0.0 copy-done
  23.8 0.0 copy-done.1
  23.8 0.0 copy-done.3
  23.8 0.6 convolution_convert_fusion.parts_ref
  24.5 0.1 fusion.8.spot_ref
  24.6 0.0 collective-permute-done.d_ref
  24.6 0.7 %collective-permute-done.1.c_ref = bf16[144,512]{1,0:T(8,128)(2,1)S(1)} collective-permute-done((bf16[144,512]{1,0:T(8,128)(2,1)S(1)}, bf16[144,512]{1,0:T(8,128)(2,1)S(1)}, u32[]{:S(2)}, u32[]{:S(2)}) %collective-permute-start.1) | collective-permute-done | bytes 147488 | tf_op jit(solution)/shard_map/ppermute | solution.py:31
  25.3 4.4 %collective-permute-done.2.a_ref = bf16[144,512]{1,0:T(8,128)(2,1)S(1)} collective-permute-done((bf16[144,512]{1,0:T(8,128)(2,1)S(1)}, bf16[144,512]{1,0:T(8,128)(2,1)S(1)}, u32[]{:S(2)}, u32[]{:S(2)}) %collective-permute-start.2) | collective-permute-done | bytes 147488 | tf_op jit(solution)/shard_map/ppermute | solution.py:31
  29.7 0.6 power_rows.1
  30.3 14.0 %all_to_all.10.in_ref = f32[32,1,640]{2,1,0:T(1,128)S(1)} all-to-all(f32[32,1,640]{2,1,0:T(1,128)S(1)} %power_rows.1), channel_id=1, replica_groups=mesh['y'=8,'z'=8,'x'=4,'core'=2] {'z','x'}, dimensions={0} | all-to-all | bytes 163840 | tf_op jit(solution)/shard_map/all_to_all | solution.py:35
  44.3 0.5 choose_rows.1
  44.7 13.0 %all_to_all.11.in_ref = f32[32,1,640]{2,1,0:T(1,128)S(1)} all-to-all(f32[32,1,640]{2,1,0:T(1,128)S(1)} %choose_rows.1), channel_id=1, replica_groups=mesh['y'=8,'z'=8,'x'=4,'core'=2] {'y','x'}, dimensions={0} | all-to-all | bytes 163840 | tf_op jit(solution)/shard_map/all_to_all | solution.py:35
  57.7 0.1 join_slices.1
  57.8 7.0 %collective-permute-start.3 = (f32[8,384]{1,0:T(8,128)S(1)}, f32[8,384]{1,0:T(8,128)S(1)}, u32[]{:S(2)}, u32[]{:S(2)}) collective-permute-start(f32[8,384]{1,0:T(8,128)S(1)} %join_slices.1), channel_id=1, source_target_pairs={{0,1},{1,0},{2,3},{3,2},{4,5},{5,4},{6,7},{7,6},{8,9},{9,8},{10,11... | collective-permute-start | bytes 36872 | tf_op jit(solution)/shard_map/ppermute | solution.py:260
  64.8 0.8 %collective-permute-done.3 = f32[8,384]{1,0:T(8,128)S(1)} collective-permute-done((f32[8,384]{1,0:T(8,128)S(1)}, f32[8,384]{1,0:T(8,128)S(1)}, u32[]{:S(2)}, u32[]{:S(2)}) %collective-permute-start.3) | collective-permute-done | bytes 12320 | tf_op jit(solution)/shard_map/ppermute | solution.py:260
  65.6 0.1 fusion.12
  65.7 0.7 %slice_divide_fusion = f32[8,256]{1,0:T(8,128)} fusion(f32[8,384]{1,0:T(8,128)S(1)} %add.99, f32[8]{0:T(128)S(1)} %fusion.12), kind=kLoop, calls=%fused_computation.28 | loop fusion | flops 2048 | bytes 16416 | tf_op jit(solution)/shard_map/div | solution.py:261
  (2 shorter events, 0.0 us)
Async XLA Ops:
  0.0 23.8 %copy-start = (f32[256,512]{1,0:T(8,128)S(1)}, f32[256,512]{1,0:T(8,128)}, u32[]{:S(2)}) copy-start(f32[256,512]{1,0:T(8,128)} %constant.75.clone) | copy-start | bytes 1572868
  0.0 23.6 %copy-start.2 = (s32[512]{0:T(512)S(1)}, s32[512]{0:T(512)}, u32[]{:S(2)}) copy-start(s32[512]{0:T(512)} %param.10) | copy-start | bytes 6148
  0.0 23.8 %copy-start.1 = (f32[256,256]{1,0:T(8,128)S(1)}, f32[256,256]{1,0:T(8,128)}, u32[]{:S(2)}) copy-start(f32[256,256]{1,0:T(8,128)} %param.12) | copy-start | bytes 786436
  0.0 23.8 %copy-start.3 = (f32[256]{0:T(256)S(1)}, f32[256]{0:T(256)}, u32[]{:S(2)}) copy-start(f32[256]{0:T(256)} %param.11) | copy-start | bytes 3076
  3.9 20.7 %collective-permute-start = (bf16[144,512]{1,0:T(8,128)(2,1)S(1)}, bf16[144,512]{1,0:T(8,128)(2,1)S(1)}, u32[]{:S(2)}, u32[]{:S(2)}) collective-permute-start(bf16[144,512]{1,0:T(8,128)(2,1)S(1)} %get-tuple-element.13), channel_id=1, source_target_pairs={{0,16},{1,497},{2,18},{3,499},{4,20},{5,501},{6,22},{7,503},{8,24}... | collective-permute-start | bytes 442376 | tf_op jit(solution)/shard_map/ppermute | solution.py:31
  18.3 7.0 %collective-permute-start.1 = (bf16[144,512]{1,0:T(8,128)(2,1)S(1)}, bf16[144,512]{1,0:T(8,128)(2,1)S(1)}, u32[]{:S(2)}, u32[]{:S(2)}) collective-permute-start(bf16[144,512]{1,0:T(8,128)(2,1)S(1)} %get-tuple-element.14), channel_id=1, source_target_pairs={{0,8},{1,505},{2,10},{3,507},{4,12},{5,509},{6,14},{7,511},{8,16},... | collective-permute-start | bytes 442376 | tf_op jit(solution)/shard_map/ppermute | solution.py:31
  20.5 9.2 %collective-permute-start.2 = (bf16[144,512]{1,0:T(8,128)(2,1)S(1)}, bf16[144,512]{1,0:T(8,128)(2,1)S(1)}, u32[]{:S(2)}, u32[]{:S(2)}) collective-permute-start(bf16[144,512]{1,0:T(8,128)(2,1)S(1)} %get-tuple-element.15), channel_id=1, source_target_pairs={{0,504},{1,9},{2,506},{3,11},{4,508},{5,13},{6,510},{7,15},{8,0},{... | collective-permute-start | bytes 442376 | tf_op jit(solution)/shard_map/ppermute | solution.py:31
  57.8 7.8 %collective-permute-start.3 = (f32[8,384]{1,0:T(8,128)S(1)}, f32[8,384]{1,0:T(8,128)S(1)}, u32[]{:S(2)}, u32[]{:S(2)}) collective-permute-start(f32[8,384]{1,0:T(8,128)S(1)} %join_slices.1), channel_id=1, source_target_pairs={{0,1},{1,0},{2,3},{3,2},{4,5},{5,4},{6,7},{7,6},{8,9},{9,8},{10,11... | collective-permute-start | bytes 36872 | tf_op jit(solution)/shard_map/ppermute | solution.py:260

commit v8 on v5

--- a/solution.py
+++ b/solution.py
@@ -20,9 +20,15 @@
 TOGETHER = 8
 
 
-def shifted(shard, by):
-    devices = lax.axis_size(BLOCK_AXES)
-    return lax.ppermute(shard, BLOCK_AXES, [(i, (i + by) % devices) for i in range(devices)])
+def opposed(shard, by):
+    blocks = lax.axis_size(BLOCK_AXES)
+    times = lax.axis_size("ta")
+    pairs = []
+    for block in range(blocks):
+        for time in range(times):
+            target = (block + (by if time % 2 else -by)) % blocks
+            pairs.append((block * times + time, target * times + time))
+    return lax.ppermute(shard, (*BLOCK_AXES, "ta"), pairs)
 
 
 def exchange(chunks, axis):
@@ -61,8 +67,9 @@
     for copy in few:
         copy.wait()
     ids = ids_ref[...]
-    back = place_ref[0] - (ids >> 3)
+    back = (place_ref[0] >> 1) - (ids >> 3)
     back = jnp.where(back < 0, back + block_total, back)
+    back = jnp.where(place_ref[0] & 1 == 0, SPAN - 1 - back, back)
     row = lax.broadcasted_iota(jnp.int32, (SPAN * GR_DEV, ids.shape[1]), 0)
     onehot = (row == back * GR_DEV + (ids & (GR_DEV - 1))).astype(jnp.float32)
     lane = lax.broadcasted_iota(jnp.int32, (SPAN * GR_DEV, LANES), 1)
@@ -153,54 +160,79 @@
     power = jnp.sum(pairs.reshape(rows // GR_DEV, GR_DEV, channels), axis=0)
     counts = [ref[rows:, :LANES].astype(jnp.float32)[:GR_DEV] for ref in (a_ref, b_ref, c_ref, d_ref)]
     count = jnp.sum(pair_sum(*counts), axis=1, keepdims=True)
-    count = packed(jnp.broadcast_to(count, (GR_DEV, LANES)), 0)
+    count = pack_counts(count)
     for j in range(slices):
         half = power[:, j // PACK * LANES : (j // PACK + 1) * LANES]
-        chunk = jnp.concatenate([packed(half, j % PACK), count], axis=0)
+        chunk = packed(half, j % PACK)
         for copy in range(out_ref.shape[0] // slices):
-            out_ref[copy * slices + j] = chunk
+            store_chunk(out_ref, copy * slices + j, chunk, count)
+
+
+def count_lanes(rows):
+    lane = lax.broadcasted_iota(jnp.int32, (rows, LANES), 1)
+    return lane == lax.broadcasted_iota(jnp.int32, (rows, LANES), 0) % GR_DEV * (LANES // GR_DEV)
+
+
+def pack_counts(count):
+    return jnp.sum(jnp.where(count_lanes(GR_DEV), count, 0.0), axis=0, keepdims=True)
+
+
+def store_chunk(out_ref, index, rows, count):
+    out_ref[index, :, :LANES] = rows[:1]
+    out_ref[index, :, LANES : 2 * LANES] = rows[1:]
+    out_ref[index, :, 2 * LANES :] = count
 
 
 def choose_kernel(times, spot_ref, in_ref, out_ref):
-    spectrum = []
-    for z in range(in_ref.shape[0] // times):
-        total = in_ref[z * times]
-        for time in range(1, times):
-            total = total + in_ref[z * times + time]
-        spectrum.append(total[:2] / jnp.maximum(total[2:], 1.0))
-    spectrum = jnp.concatenate(spectrum, axis=0)
-    first = lane_group(spectrum.shape) == 0
-    rows = jnp.concatenate([jnp.where(first, turned(spectrum, -b), 0.0) for b in range(PACK)], axis=0)
-    column = lax.broadcasted_iota(jnp.int32, (spot_ref.shape[0], rows.shape[0]), 1)
-    pick = (spot_ref[...] == column).astype(jnp.float32)
-    chosen = exact_dot(pick, rows)
-    size = chosen.shape[0] // PACK
-    chunks = turned(chosen[:size], 0)
+    planes = []
+    for core in range(2):
+        for z in range(in_ref.shape[0] // times):
+            total = in_ref[z * times + core]
+            for time in range(core + 2, times, 2):
+                total = total + in_ref[z * times + time]
+            planes.append(total)
+    planes = jnp.concatenate(planes, axis=0)
+    member = spot_ref[:, 2:3]
+    column = lax.broadcasted_iota(jnp.int32, (member.shape[0], planes.shape[0]), 1)
+    pick = (spot_ref[:, 0:1] == column) | (spot_ref[:, 1:2] == column)
+    found = exact_dot(pick.astype(jnp.float32), planes)
+    lanes = jnp.where(member < PACK, found[:, :LANES], found[:, LANES : 2 * LANES])
+    rows = lanes
     for b in range(1, PACK):
-        chunks = chunks + turned(chosen[b * size : (b + 1) * size], b)
-    copies = out_ref.shape[0] // (size // 2)
-    for y in range(size // 2):
+        rows = jnp.where(member % PACK == b, turned(lanes, -b), rows)
+    lane = lax.broadcasted_iota(jnp.int32, rows.shape, 1)
+    count = jnp.where(lane == member * (LANES // GR_DEV), found[:, 2 * LANES :], 0.0)
+    count = jnp.sum(count, axis=1, keepdims=True)
+    copies = times
+    for y in range(out_ref.shape[0] // copies):
+        span = slice(y * GR_DEV, (y + 1) * GR_DEV)
+        chunk, counts = packed(rows[span], 0), pack_counts(count[span])
         for copy in range(copies):
-            out_ref[y * copies + copy] = chunks[2 * y : 2 * y + 2]
+            store_chunk(out_ref, y * copies + copy, chunk, counts)
 
 
 def unpack_kernel(in_ref, out_ref):
     slices = out_ref.shape[1] // SLICE
     group = lane_group((GR_DEV, LANES))
     member = lax.broadcasted_iota(jnp.int32, (GR_DEV, LANES), 0) % PACK
+    totals = []
+    for j in range(slices):
+        total = in_ref[j]
+        for y in range(1, in_ref.shape[0] // slices):
+            total = total + in_ref[y * slices + j]
+        totals.append(total)
+    count = jnp.where(count_lanes(GR_DEV), jnp.broadcast_to(totals[0][:, 2 * LANES :], (GR_DEV, LANES)), 0.0)
+    count = jnp.maximum(jnp.sum(count, axis=1, keepdims=True), 1.0)
     for half in range(slices // PACK):
         result = jnp.zeros((GR_DEV, LANES), jnp.float32)
         for k in range(PACK):
-            j = half * PACK + k
-            total = in_ref[j]
-            for y in range(1, in_ref.shape[0] // slices):
-                total = total + in_ref[y * slices + j]
-            total = jnp.concatenate(
-                [jnp.broadcast_to(total[a : a + 1], (PACK, LANES)) for a in range(2)], axis=0
+            total = totals[half * PACK + k]
+            rows = jnp.concatenate(
+                [jnp.broadcast_to(total[:, a * LANES : (a + 1) * LANES], (PACK, LANES)) for a in range(2)], axis=0
             )
             for b in range(PACK):
-                result = jnp.where((group == k) & (member == b), turned(total, k - b), result)
-        out_ref[:, half * LANES : (half + 1) * LANES] = result
+                result = jnp.where((group == k) & (member == b), turned(rows, k - b), result)
+        out_ref[:, half * LANES : (half + 1) * LANES] = result / count
 
 
 def small_call(kernel, shape, name):
@@ -217,24 +249,27 @@
     y_size, z_size, times = (lax.axis_size(axis) for axis in ("y", "z", "ta"))
     block_total = y_size * z_size
     slices = channels // SLICE
-
-    place = lax.axis_index(BLOCK_AXES)[None]
+    width = GR_DEV * SLICE + LANES
+
+    place = (lax.axis_index(BLOCK_AXES) * 2 + lax.axis_index("ta") % 2)[None]
     blocks = group_sums(visibilities, flags, group_ids, place, block_total)
-    blocks = [shifted(block, by) if by else block for block, by in zip(blocks, (-2, -1, 1, 0))]
+    blocks = [opposed(block, by) if by else block for block, by in zip(blocks, (-2, -1, 1, 0))]
     parts = transform_parts(taper, inv_cov)
 
-    order = group_order.reshape(y_size, z_size, 2, PACK)
-    wanted = lax.dynamic_index_in_dim(order, lax.axis_index("z"), 1, keepdims=False)
-    wanted = wanted.transpose(2, 0, 1).reshape(-1, 1)
-    holder = (wanted // GR_DEV + 1) % block_total
-    member = wanted % GR_DEV
-    spot = (member % PACK * z_size + holder % z_size) * 2 + member // PACK
-    spot = jnp.where(holder // z_size == lax.axis_index("y"), spot, -1)
+    order = group_order.reshape(y_size, z_size, GR_DEV)
+    wanted = lax.dynamic_index_in_dim(order, lax.axis_index("z"), 1, keepdims=False).reshape(-1)
+    columns = []
+    for core in range(2):
+        holder = (wanted // GR_DEV + 2 - core) % block_total
+        column = core * z_size + holder % z_size
+        columns.append(jnp.where(holder // z_size == lax.axis_index("y"), column, -1))
+    spot = jnp.stack([*columns, wanted % GR_DEV], axis=1)
     parts, spot = lax.optimization_barrier((parts, spot))
 
-    power = small_call(power_kernel, (z_size * slices, 4, LANES), "power_rows")(parts, *blocks)
+    power = small_call(power_kernel, (z_size * slices, 1, width), "power_rows")(parts, *blocks)
     choose = functools.partial(choose_kernel, times)
-    chosen = small_call(choose, (y_size * times, 2, LANES), "choose_rows")(spot, exchange(power, ("z", "ta")))
+    shape = (y_size * times, 1, width)
+    chosen = small_call(choose, shape, "choose_rows")(spot, exchange(power, ("z", "ta")))
 
     found = exchange(chosen, ("y", "ta"))
     return small_call(unpack_kernel, (GR_DEV, channels), "unpack_rows")(found)

time: 65.6 us -> 65.6 us (level)
  blocking collectives: 34.7 us -> 18.3 us
  waiting for transfers between devices: 4.86 us -> 15.6 us
  starting transfers between devices: 19.7 us -> 24.6 us
  Pallas kernels: 4.82 us -> 5.66 us
    all_to_all x2 -> x1, blocking collectives: 34.7 us -> 18.3 us  [exchange(): return lax.all_to_all(chunks, axis, 0, 0, tiled=True)]
    all_to_all x0 -> x1, waiting for transfers between devices: none -> 10.5 us  [exchange(): return lax.all_to_all(chunks, axis, 0, 0, tiled=True)]
    all_to_all x0 -> x1, starting transfers between devices: none -> 4.97 us  [exchange(): return lax.all_to_all(chunks, axis, 0, 0, tiled=True)]
    pallas_call x2, Pallas kernels: 0.88 us -> 1.71 us  [the longest x1 1.21 us: on_device(): small_call(power_kernel, (z_size * slices, 1, width), 'power_rows')]
  transfers between devices with their start and end apart: 3 -> 4, of which waited for: 2 -> 3; matrix products, arithmetic and copies ran while one was open for 2% -> 2% of each run, Pallas kernels for 0% -> 0%
where the time goes in v8:
time: 65.6 us; the launch traced here: 65.4 us
  starting transfers between devices  24.6 us (38%)
  blocking collectives  18.3 us (28%)
  waiting for transfers between devices  15.6 us (24%)
  Pallas kernels  5.66 us (9%)
    ppermute x3, starting transfers between devices, opposed(): return lax.ppermute(shard, (*BLOCK_AXES, 'ta'), pairs)  19.7 us
    all_to_all x1, blocking collectives, exchange(): return lax.all_to_all(chunks, axis, 0, 0, tiled=True)  18.3 us
    all_to_all x1, waiting for transfers between devices, exchange(): return lax.all_to_all(chunks, axis, 0, 0, tiled=True)  10.5 us
    ppermute x3, waiting for transfers between devices, opposed(): return lax.ppermute(shard, (*BLOCK_AXES, 'ta'), pairs)  5.13 us
    all_to_all x1, starting transfers between devices, exchange(): return lax.all_to_all(chunks, axis, 0, 0, tiled=True)  4.97 us
    pallas_call x1, Pallas kernels, group_sums(): pl.pallas_call(functools.partial(group_kernel, block_total), in_specs=[pl...  3.24 us
  transfers between devices with their start and end apart: 4, of which 3 were waited for; matrix products, arithmetic and copies ran while one was open for 2% of the time, Pallas kernels for 0%

profile of v8, /device:TPU:1, one launch (start us, length us, event | category | flops | bytes accessed | tf_op | source)
XLA Modules:
  0.0 65.4 jit_solution(12611813187174497577)
XLA Ops:
  0.0 0.0 copy-start
  0.0 0.0 copy-start.2
  0.0 0.0 copy-start.3
  0.0 0.0 copy-start.1
  0.0 3.2 %group_sums.1 = (bf16[144,512]{1,0:T(8,128)(2,1)S(1)}, bf16[144,512]{1,0:T(8,128)(2,1)S(1)}, bf16[144,512]{1,0:T(8,128)(2,1)S(1)}, bf16[144,512]{1,0:T(8,128)(2,1)S(1)}) custom-call(s32[1]{0:T(128)} %bitcast.place_ref, s32[1,256]{1,0:T(1,128)} %bitcast.3, s32[16,256]{1,0:T(8,128)} %flags_hbm.1, bf16[16,256,512]{2,1,0:T(8,128)(2,1)} %vis_hbm.1), custom_call_target="tpu_custom_call" | custom-call | flops 134217728 | bytes 4194304 | tf_op jit(solution)/shard_map/group_sums/pallas_call | solution.py:104
  3.3 14.4 %collective-permute-start = (bf16[144,512]{1,0:T(8,128)(2,1)S(1)}, bf16[144,512]{1,0:T(8,128)(2,1)S(1)}, u32[]{:S(2)}, u32[]{:S(2)}) collective-permute-start(bf16[144,512]{1,0:T(8,128)(2,1)S(1)} %get-tuple-element.13), channel_id=1, source_target_pairs={{0,16},{1,497},{2,18},{3,499},{4,20},{5,501},{6,22},{7,503},{8,24}... | collective-permute-start | bytes 442376 | tf_op jit(solution)/shard_map/ppermute | solution.py:31
  17.7 2.2 %collective-permute-start.1 = (bf16[144,512]{1,0:T(8,128)(2,1)S(1)}, bf16[144,512]{1,0:T(8,128)(2,1)S(1)}, u32[]{:S(2)}, u32[]{:S(2)}) collective-permute-start(bf16[144,512]{1,0:T(8,128)(2,1)S(1)} %get-tuple-element.14), channel_id=1, source_target_pairs={{0,8},{1,505},{2,10},{3,507},{4,12},{5,509},{6,14},{7,511},{8,16},... | collective-permute-start | bytes 442376 | tf_op jit(solution)/shard_map/ppermute | solution.py:31
  19.9 3.1 %collective-permute-start.2 = (bf16[144,512]{1,0:T(8,128)(2,1)S(1)}, bf16[144,512]{1,0:T(8,128)(2,1)S(1)}, u32[]{:S(2)}, u32[]{:S(2)}) collective-permute-start(bf16[144,512]{1,0:T(8,128)(2,1)S(1)} %get-tuple-element.15), channel_id=1, source_target_pairs={{0,504},{1,9},{2,506},{3,11},{4,508},{5,13},{6,510},{7,15},{8,0},{... | collective-permute-start | bytes 442376 | tf_op jit(solution)/shard_map/ppermute | solution.py:31
  23.0 0.0 copy-done.2
  23.0 0.1 reshape.338
  23.1 0.1 reshape.339
  23.2 0.0 copy-done
  23.2 0.0 copy-done.3
  23.2 0.0 copy-done.1
  23.3 0.6 convolution_convert_fusion.parts_ref
  23.9 0.0 collective-permute-done.d_ref
  24.0 0.7 %collective-permute-done.1.c_ref = bf16[144,512]{1,0:T(8,128)(2,1)S(1)} collective-permute-done((bf16[144,512]{1,0:T(8,128)(2,1)S(1)}, bf16[144,512]{1,0:T(8,128)(2,1)S(1)}, u32[]{:S(2)}, u32[]{:S(2)}) %collective-permute-start.1) | collective-permute-done | bytes 147488 | tf_op jit(solution)/shard_map/ppermute | solution.py:31
  24.7 4.4 %collective-permute-done.2.a_ref = bf16[144,512]{1,0:T(8,128)(2,1)S(1)} collective-permute-done((bf16[144,512]{1,0:T(8,128)(2,1)S(1)}, bf16[144,512]{1,0:T(8,128)(2,1)S(1)}, u32[]{:S(2)}, u32[]{:S(2)}) %collective-permute-start.2) | collective-permute-done | bytes 147488 | tf_op jit(solution)/shard_map/ppermute | solution.py:31
  29.1 1.2 %power_rows.1 = f32[64,1,384]{2,1,0:T(1,128)} custom-call(bf16[256,512]{1,0:T(8,128)(2,1)S(1)} %convolution_convert_fusion.parts_ref, bf16[144,512]{1,0:T(8,128)(2,1)S(1)} %collective-permute-done.d_ref, bf16[144,512]{1,0:T(8,128)(2,1)S(1)} %collective-permute-done.1.c_ref, bf16[144,512]{1,0:T(8,128)(2,1)S(1)} %collective-permute-done.2.a_ref, ...), custom_call_target="tpu_custom_call" | custom-call | tf_op jit(solution)/shard_map/power_rows/pallas_call | solution.py:269
  30.3 5.0 %all-to-all-start = ((f32[64,1,384]{2,1,0:T(1,128)}), f32[64,1,384]{2,1,0:T(1,128)S(1)}, u32[]{:S(2)}, u32[]{:S(2)}) async-start(f32[64,1,384]{2,1,0:T(1,128)} %power_rows.1), calls=%async_computation | async-start | bytes 196608 | tf_op jit(solution)/shard_map/all_to_all | solution.py:35
  35.3 0.1 copy.16.spot_ref
  35.4 10.5 %all-to-all-done.in_ref = f32[64,1,384]{2,1,0:T(1,128)S(1)} async-done(((f32[64,1,384]{2,1,0:T(1,128)}), f32[64,1,384]{2,1,0:T(1,128)S(1)}, u32[]{:S(2)}, u32[]{:S(2)}) %all-to-all-start) | async-done | bytes 98336 | tf_op jit(solution)/shard_map/all_to_all | solution.py:35
  45.8 0.5 choose_rows.1
  46.3 18.3 %all_to_all.10.in_ref = f32[64,1,384]{2,1,0:T(1,128)S(1)} all-to-all(f32[64,1,384]{2,1,0:T(1,128)S(1)} %choose_rows.1), channel_id=1, replica_groups=mesh['y'=8,'z'=8,'ta'=8] {'y','ta'}, dimensions={0} | all-to-all | bytes 196608 | tf_op jit(solution)/shard_map/all_to_all | solution.py:35
  64.7 0.7 %unpack_rows.1 = f32[8,256]{1,0:T(8,128)} custom-call(f32[64,1,384]{2,1,0:T(1,128)S(1)} %all_to_all.10.in_ref), custom_call_target="tpu_custom_call" | custom-call | tf_op jit(solution)/shard_map/unpack_rows/pallas_call | solution.py:275
  (4 shorter events, 0.1 us)
Async XLA Ops:
  0.0 23.2 %copy-start = (f32[256,512]{1,0:T(8,128)S(1)}, f32[256,512]{1,0:T(8,128)}, u32[]{:S(2)}) copy-start(f32[256,512]{1,0:T(8,128)} %constant.104.clone) | copy-start | bytes 1572868
  0.0 23.0 %copy-start.2 = (s32[512]{0:T(512)S(1)}, s32[512]{0:T(512)}, u32[]{:S(2)}) copy-start(s32[512]{0:T(512)} %param.10) | copy-start | bytes 6148
  0.0 23.2 %copy-start.3 = (f32[256]{0:T(256)S(1)}, f32[256]{0:T(256)}, u32[]{:S(2)}) copy-start(f32[256]{0:T(256)} %param.11) | copy-start | bytes 3076
  0.0 23.2 %copy-start.1 = (f32[256,256]{1,0:T(8,128)S(1)}, f32[256,256]{1,0:T(8,128)}, u32[]{:S(2)}) copy-start(f32[256,256]{1,0:T(8,128)} %param.12) | copy-start | bytes 786436
  3.3 20.7 %collective-permute-start = (bf16[144,512]{1,0:T(8,128)(2,1)S(1)}, bf16[144,512]{1,0:T(8,128)(2,1)S(1)}, u32[]{:S(2)}, u32[]{:S(2)}) collective-permute-start(bf16[144,512]{1,0:T(8,128)(2,1)S(1)} %get-tuple-element.13), channel_id=1, source_target_pairs={{0,16},{1,497},{2,18},{3,499},{4,20},{5,501},{6,22},{7,503},{8,24}... | collective-permute-start | bytes 442376 | tf_op jit(solution)/shard_map/ppermute | solution.py:31
  17.7 7.0 %collective-permute-start.1 = (bf16[144,512]{1,0:T(8,128)(2,1)S(1)}, bf16[144,512]{1,0:T(8,128)(2,1)S(1)}, u32[]{:S(2)}, u32[]{:S(2)}) collective-permute-start(bf16[144,512]{1,0:T(8,128)(2,1)S(1)} %get-tuple-element.14), channel_id=1, source_target_pairs={{0,8},{1,505},{2,10},{3,507},{4,12},{5,509},{6,14},{7,511},{8,16},... | collective-permute-start | bytes 442376 | tf_op jit(solution)/shard_map/ppermute | solution.py:31
  19.9 9.2 %collective-permute-start.2 = (bf16[144,512]{1,0:T(8,128)(2,1)S(1)}, bf16[144,512]{1,0:T(8,128)(2,1)S(1)}, u32[]{:S(2)}, u32[]{:S(2)}) collective-permute-start(bf16[144,512]{1,0:T(8,128)(2,1)S(1)} %get-tuple-element.15), channel_id=1, source_target_pairs={{0,504},{1,9},{2,506},{3,11},{4,508},{5,13},{6,510},{7,15},{8,0},{... | collective-permute-start | bytes 442376 | tf_op jit(solution)/shard_map/ppermute | solution.py:31
  30.3 15.5 %all-to-all-start = ((f32[64,1,384]{2,1,0:T(1,128)}), f32[64,1,384]{2,1,0:T(1,128)S(1)}, u32[]{:S(2)}, u32[]{:S(2)}) async-start(f32[64,1,384]{2,1,0:T(1,128)} %power_rows.1), calls=%async_computation | async-start | bytes 196608 | tf_op jit(solution)/shard_map/all_to_all | solution.py:35

commit v9 on v8

--- a/solution.py
+++ b/solution.py
@@ -14,10 +14,10 @@
 SPAN = 4
 LANES = 128
 BLOCK_AXES = ("y", "z")
-COUNT_ROWS = 16
+COUNT_ROWS = 8
 SLICE = 32
 PACK = 4
-TOGETHER = 8
+TOGETHER = 16
 
 
 def opposed(shard, by):
@@ -92,8 +92,7 @@
             ref[first * GR_DEV : (first + TOGETHER) * GR_DEV, :] = both.astype(jnp.bfloat16)
     for step, ref in zip(BLOCK_STEPS, refs):
         mine = counts[step * GR_DEV : (step + 1) * GR_DEV]
-        tile = jnp.concatenate([mine, jnp.zeros_like(mine)], axis=0)
-        tile = jnp.concatenate([tile, jnp.zeros((COUNT_ROWS, row_width - LANES), jnp.float32)], axis=1)
+        tile = jnp.concatenate([mine, jnp.zeros((COUNT_ROWS, row_width - LANES), jnp.float32)], axis=1)
         ref[time_count * GR_DEV :, :] = tile.astype(jnp.bfloat16)
 
 
@@ -158,7 +157,7 @@
     blocks = [delays(ref) for ref in (a_ref, b_ref, c_ref, d_ref)]
     pairs = pair_sum(*(re for re, _ in blocks)) + pair_sum(*(im for _, im in blocks))
     power = jnp.sum(pairs.reshape(rows // GR_DEV, GR_DEV, channels), axis=0)
-    counts = [ref[rows:, :LANES].astype(jnp.float32)[:GR_DEV] for ref in (a_ref, b_ref, c_ref, d_ref)]
+    counts = [ref[rows:, :LANES].astype(jnp.float32) for ref in (a_ref, b_ref, c_ref, d_ref)]
     count = jnp.sum(pair_sum(*counts), axis=1, keepdims=True)
     count = pack_counts(count)
     for j in range(slices):
@@ -183,7 +182,7 @@
     out_ref[index, :, 2 * LANES :] = count
 
 
-def choose_kernel(times, spot_ref, in_ref, out_ref):
+def choose_kernel(times, first_ref, second_ref, member_ref, in_ref, out_ref):
     planes = []
     for core in range(2):
         for z in range(in_ref.shape[0] // times):
@@ -192,9 +191,9 @@
                 total = total + in_ref[z * times + time]
             planes.append(total)
     planes = jnp.concatenate(planes, axis=0)
-    member = spot_ref[:, 2:3]
+    member = member_ref[...]
     column = lax.broadcasted_iota(jnp.int32, (member.shape[0], planes.shape[0]), 1)
-    pick = (spot_ref[:, 0:1] == column) | (spot_ref[:, 1:2] == column)
+    pick = (first_ref[...] == column) | (second_ref[...] == column)
     found = exact_dot(pick.astype(jnp.float32), planes)
     lanes = jnp.where(member < PACK, found[:, :LANES], found[:, LANES : 2 * LANES])
     rows = lanes
@@ -257,19 +256,18 @@
     parts = transform_parts(taper, inv_cov)
 
     order = group_order.reshape(y_size, z_size, GR_DEV)
-    wanted = lax.dynamic_index_in_dim(order, lax.axis_index("z"), 1, keepdims=False).reshape(-1)
+    wanted = lax.dynamic_index_in_dim(order, lax.axis_index("z"), 1, keepdims=False).reshape(-1, 1)
     columns = []
     for core in range(2):
         holder = (wanted // GR_DEV + 2 - core) % block_total
         column = core * z_size + holder % z_size
         columns.append(jnp.where(holder // z_size == lax.axis_index("y"), column, -1))
-    spot = jnp.stack([*columns, wanted % GR_DEV], axis=1)
-    parts, spot = lax.optimization_barrier((parts, spot))
+    parts, *spots = lax.optimization_barrier((parts, *columns, wanted % GR_DEV))
 
     power = small_call(power_kernel, (z_size * slices, 1, width), "power_rows")(parts, *blocks)
     choose = functools.partial(choose_kernel, times)
     shape = (y_size * times, 1, width)
-    chosen = small_call(choose, shape, "choose_rows")(spot, exchange(power, ("z", "ta")))
+    chosen = small_call(choose, shape, "choose_rows")(*spots, exchange(power, ("z", "ta")))
 
     found = exchange(chosen, ("y", "ta"))
     return small_call(unpack_kernel, (GR_DEV, channels), "unpack_rows")(found)

time: 65.6 us -> 64.6 us (0.985)
  blocking collectives: 18.3 us -> 33.6 us
  waiting for transfers between devices: 15.6 us -> 5 us
  starting transfers between devices: 24.6 us -> 19.7 us
  Pallas kernels: 5.66 us -> 4.98 us
    all_to_all x1 -> x2, blocking collectives: 18.3 us -> 33.6 us  [exchange(): return lax.all_to_all(chunks, axis, 0, 0, tiled=True)]
    all_to_all x1 -> x0, waiting for transfers between devices: 10.5 us -> none  [exchange(): return lax.all_to_all(chunks, axis, 0, 0, tiled=True)]
    all_to_all x1 -> x0, starting transfers between devices: 4.97 us -> none  [exchange(): return lax.all_to_all(chunks, axis, 0, 0, tiled=True)]
  transfers between devices with their start and end apart: 4 -> 3, of which waited for: 3 -> 2; matrix products, arithmetic and copies ran while one was open for 2% -> 1% of each run, Pallas kernels for 0% -> 0%
where the time goes in v9:
time: 64.6 us; the launch traced here: 64.4 us
  blocking collectives  33.6 us (52%)
  starting transfers between devices  19.7 us (30%)
  waiting for transfers between devices  5 us (8%)
  Pallas kernels  4.98 us (8%)
    all_to_all x2, blocking collectives, exchange(): return lax.all_to_all(chunks, axis, 0, 0, tiled=True)  33.6 us
    ppermute x3, starting transfers between devices, opposed(): return lax.ppermute(shard, (*BLOCK_AXES, 'ta'), pairs)  19.7 us
    ppermute x3, waiting for transfers between devices, opposed(): return lax.ppermute(shard, (*BLOCK_AXES, 'ta'), pairs)  5 us
    pallas_call x1, Pallas kernels, group_sums(): pl.pallas_call(functools.partial(group_kernel, block_total), in_specs=[pl...  3.2 us
  transfers between devices with their start and end apart: 3, of which 2 were waited for; matrix products, arithmetic and copies ran while one was open for 1% of the time, Pallas kernels for 0%

profile of v9, /device:TPU:1, one launch (start us, length us, event | category | flops | bytes accessed | tf_op | source)
XLA Modules:
  0.0 64.4 jit_solution(11070124368645844933)
XLA Ops:
  0.0 0.0 copy-start
  0.0 0.0 copy-start.2
  0.0 0.0 copy-start.3
  0.0 0.0 copy-start.1
  0.0 3.2 %group_sums.1 = (bf16[136,512]{1,0:T(8,128)(2,1)S(1)}, bf16[136,512]{1,0:T(8,128)(2,1)S(1)}, bf16[136,512]{1,0:T(8,128)(2,1)S(1)}, bf16[136,512]{1,0:T(8,128)(2,1)S(1)}) custom-call(s32[1]{0:T(128)} %bitcast.place_ref, s32[1,256]{1,0:T(1,128)} %bitcast.3, s32[16,256]{1,0:T(8,128)} %flags_hbm.1, bf16[16,256,512]{2,1,0:T(8,128)(2,1)} %vis_hbm.1), custom_call_target="tpu_custom_call" | custom-call | flops 134217728 | bytes 4194304 | tf_op jit(solution)/shard_map/group_sums/pallas_call | solution.py:103
  3.2 14.4 %collective-permute-start = (bf16[136,512]{1,0:T(8,128)(2,1)S(1)}, bf16[136,512]{1,0:T(8,128)(2,1)S(1)}, u32[]{:S(2)}, u32[]{:S(2)}) collective-permute-start(bf16[136,512]{1,0:T(8,128)(2,1)S(1)} %get-tuple-element.17), channel_id=1, source_target_pairs={{0,16},{1,497},{2,18},{3,499},{4,20},{5,501},{6,22},{7,503},{8,24}... | collective-permute-start | bytes 417800 | tf_op jit(solution)/shard_map/ppermute | solution.py:31
  17.6 2.2 %collective-permute-start.1 = (bf16[136,512]{1,0:T(8,128)(2,1)S(1)}, bf16[136,512]{1,0:T(8,128)(2,1)S(1)}, u32[]{:S(2)}, u32[]{:S(2)}) collective-permute-start(bf16[136,512]{1,0:T(8,128)(2,1)S(1)} %get-tuple-element.18), channel_id=1, source_target_pairs={{0,8},{1,505},{2,10},{3,507},{4,12},{5,509},{6,14},{7,511},{8,16},... | collective-permute-start | bytes 417800 | tf_op jit(solution)/shard_map/ppermute | solution.py:31
  19.8 3.1 %collective-permute-start.2 = (bf16[136,512]{1,0:T(8,128)(2,1)S(1)}, bf16[136,512]{1,0:T(8,128)(2,1)S(1)}, u32[]{:S(2)}, u32[]{:S(2)}) collective-permute-start(bf16[136,512]{1,0:T(8,128)(2,1)S(1)} %get-tuple-element.19), channel_id=1, source_target_pairs={{0,504},{1,9},{2,506},{3,11},{4,508},{5,13},{6,510},{7,15},{8,0},{... | collective-permute-start | bytes 417800 | tf_op jit(solution)/shard_map/ppermute | solution.py:31
  22.9 0.0 copy-done.2
  22.9 0.1 reshape.449
  23.1 0.1 reshape.451
  23.1 0.0 copy-done
  23.1 0.0 copy-done.3
  23.2 0.0 copy-done.1
  23.2 0.6 convolution_convert_fusion.parts_ref
  23.8 0.1 add_select_fusion
  23.9 0.0 collective-permute-done.d_ref
  23.9 0.5 collective-permute-done.1.c_ref
  24.5 4.5 %collective-permute-done.2.a_ref = bf16[136,512]{1,0:T(8,128)(2,1)S(1)} collective-permute-done((bf16[136,512]{1,0:T(8,128)(2,1)S(1)}, bf16[136,512]{1,0:T(8,128)(2,1)S(1)}, u32[]{:S(2)}, u32[]{:S(2)}) %collective-permute-start.2) | collective-permute-done | bytes 139296 | tf_op jit(solution)/shard_map/ppermute | solution.py:31
  28.9 0.6 power_rows.1
  29.5 15.3 %all_to_all.10.in_ref = f32[64,1,384]{2,1,0:T(1,128)S(1)} all-to-all(f32[64,1,384]{2,1,0:T(1,128)S(1)} %power_rows.1), channel_id=1, replica_groups=mesh['y'=8,'z'=8,'ta'=8] {'z','ta'}, dimensions={0} | all-to-all | bytes 196608 | tf_op jit(solution)/shard_map/all_to_all | solution.py:35
  44.9 0.5 choose_rows.1
  45.4 18.3 %all_to_all.11.in_ref = f32[64,1,384]{2,1,0:T(1,128)S(1)} all-to-all(f32[64,1,384]{2,1,0:T(1,128)S(1)} %choose_rows.1), channel_id=1, replica_groups=mesh['y'=8,'z'=8,'ta'=8] {'y','ta'}, dimensions={0} | all-to-all | bytes 196608 | tf_op jit(solution)/shard_map/all_to_all | solution.py:35
  63.7 0.7 %unpack_rows.1 = f32[8,256]{1,0:T(8,128)} custom-call(f32[64,1,384]{2,1,0:T(1,128)S(1)} %all_to_all.11.in_ref), custom_call_target="tpu_custom_call" | custom-call | tf_op jit(solution)/shard_map/unpack_rows/pallas_call | solution.py:273
  (1 shorter events, 0.0 us)
Async XLA Ops:
  0.0 23.1 %copy-start = (f32[256,512]{1,0:T(8,128)S(1)}, f32[256,512]{1,0:T(8,128)}, u32[]{:S(2)}) copy-start(f32[256,512]{1,0:T(8,128)} %constant.104.clone) | copy-start | bytes 1572868
  0.0 22.9 %copy-start.2 = (s32[512]{0:T(512)S(1)}, s32[512]{0:T(512)}, u32[]{:S(2)}) copy-start(s32[512]{0:T(512)} %param.10) | copy-start | bytes 6148
  0.0 23.1 %copy-start.3 = (f32[256]{0:T(256)S(1)}, f32[256]{0:T(256)}, u32[]{:S(2)}) copy-start(f32[256]{0:T(256)} %param.11) | copy-start | bytes 3076
  0.0 23.1 %copy-start.1 = (f32[256,256]{1,0:T(8,128)S(1)}, f32[256,256]{1,0:T(8,128)}, u32[]{:S(2)}) copy-start(f32[256,256]{1,0:T(8,128)} %param.12) | copy-start | bytes 786436
  3.2 20.7 %collective-permute-start = (bf16[136,512]{1,0:T(8,128)(2,1)S(1)}, bf16[136,512]{1,0:T(8,128)(2,1)S(1)}, u32[]{:S(2)}, u32[]{:S(2)}) collective-permute-start(bf16[136,512]{1,0:T(8,128)(2,1)S(1)} %get-tuple-element.17), channel_id=1, source_target_pairs={{0,16},{1,497},{2,18},{3,499},{4,20},{5,501},{6,22},{7,503},{8,24}... | collective-permute-start | bytes 417800 | tf_op jit(solution)/shard_map/ppermute | solution.py:31
  17.6 6.8 %collective-permute-start.1 = (bf16[136,512]{1,0:T(8,128)(2,1)S(1)}, bf16[136,512]{1,0:T(8,128)(2,1)S(1)}, u32[]{:S(2)}, u32[]{:S(2)}) collective-permute-start(bf16[136,512]{1,0:T(8,128)(2,1)S(1)} %get-tuple-element.18), channel_id=1, source_target_pairs={{0,8},{1,505},{2,10},{3,507},{4,12},{5,509},{6,14},{7,511},{8,16},... | collective-permute-start | bytes 417800 | tf_op jit(solution)/shard_map/ppermute | solution.py:31
  19.8 9.1 %collective-permute-start.2 = (bf16[136,512]{1,0:T(8,128)(2,1)S(1)}, bf16[136,512]{1,0:T(8,128)(2,1)S(1)}, u32[]{:S(2)}, u32[]{:S(2)}) collective-permute-start(bf16[136,512]{1,0:T(8,128)(2,1)S(1)} %get-tuple-element.19), channel_id=1, source_target_pairs={{0,504},{1,9},{2,506},{3,11},{4,508},{5,13},{6,510},{7,15},{8,0},{... | collective-permute-start | bytes 417800 | tf_op jit(solution)/shard_map/ppermute | solution.py:31

commit v10 on v9

--- a/solution.py
+++ b/solution.py
@@ -256,20 +256,20 @@
     parts = transform_parts(taper, inv_cov)
 
     order = group_order.reshape(y_size, z_size, GR_DEV)
-    wanted = lax.dynamic_index_in_dim(order, lax.axis_index("z"), 1, keepdims=False).reshape(-1, 1)
+    wanted = lax.dynamic_index_in_dim(order, lax.axis_index("y"), 0, keepdims=False).reshape(-1, 1)
     columns = []
     for core in range(2):
         holder = (wanted // GR_DEV + 2 - core) % block_total
-        column = core * z_size + holder % z_size
-        columns.append(jnp.where(holder // z_size == lax.axis_index("y"), column, -1))
+        column = core * y_size + holder // z_size
+        columns.append(jnp.where(holder % z_size == lax.axis_index("z"), column, -1))
     parts, *spots = lax.optimization_barrier((parts, *columns, wanted % GR_DEV))
 
-    power = small_call(power_kernel, (z_size * slices, 1, width), "power_rows")(parts, *blocks)
+    power = small_call(power_kernel, (y_size * slices, 1, width), "power_rows")(parts, *blocks)
     choose = functools.partial(choose_kernel, times)
-    shape = (y_size * times, 1, width)
-    chosen = small_call(choose, shape, "choose_rows")(*spots, exchange(power, ("z", "ta")))
-
-    found = exchange(chosen, ("y", "ta"))
+    shape = (z_size * times, 1, width)
+    chosen = small_call(choose, shape, "choose_rows")(*spots, exchange(power, ("y", "ta")))
+
+    found = exchange(chosen, ("z", "ta"))
     return small_call(unpack_kernel, (GR_DEV, channels), "unpack_rows")(found)
 
 

time: 64.6 us -> 64.6 us (level)
  no operation moved by 1% of the time
where the time goes in v10:
time: 64.6 us; the launch traced here: 64.4 us
  blocking collectives  33.6 us (52%)
  starting transfers between devices  19.7 us (30%)
  waiting for transfers between devices  5.01 us (8%)
  Pallas kernels  4.98 us (8%)
    all_to_all x2, blocking collectives, exchange(): return lax.all_to_all(chunks, axis, 0, 0, tiled=True)  33.6 us
    ppermute x3, starting transfers between devices, opposed(): return lax.ppermute(shard, (*BLOCK_AXES, 'ta'), pairs)  19.7 us
    ppermute x3, waiting for transfers between devices, opposed(): return lax.ppermute(shard, (*BLOCK_AXES, 'ta'), pairs)  5.01 us
    pallas_call x1, Pallas kernels, group_sums(): pl.pallas_call(functools.partial(group_kernel, block_total), in_specs=[pl...  3.2 us
  transfers between devices with their start and end apart: 3, of which 2 were waited for; matrix products, arithmetic and copies ran while one was open for 1% of the time, Pallas kernels for 0%

profile of v10, /device:TPU:1, one launch (start us, length us, event | category | flops | bytes accessed | tf_op | source)
XLA Modules:
  0.0 64.4 jit_solution(657225476767330107)
XLA Ops:
  0.0 0.0 copy-start
  0.0 0.0 copy-start.2
  0.0 0.0 copy-start.3
  0.0 0.0 copy-start.1
  0.0 3.2 %group_sums.1 = (bf16[136,512]{1,0:T(8,128)(2,1)S(1)}, bf16[136,512]{1,0:T(8,128)(2,1)S(1)}, bf16[136,512]{1,0:T(8,128)(2,1)S(1)}, bf16[136,512]{1,0:T(8,128)(2,1)S(1)}) custom-call(s32[1]{0:T(128)} %bitcast.place_ref, s32[1,256]{1,0:T(1,128)} %bitcast.3, s32[16,256]{1,0:T(8,128)} %flags_hbm.1, bf16[16,256,512]{2,1,0:T(8,128)(2,1)} %vis_hbm.1), custom_call_target="tpu_custom_call" | custom-call | flops 134217728 | bytes 4194304 | tf_op jit(solution)/shard_map/group_sums/pallas_call | solution.py:103
  3.2 14.4 %collective-permute-start = (bf16[136,512]{1,0:T(8,128)(2,1)S(1)}, bf16[136,512]{1,0:T(8,128)(2,1)S(1)}, u32[]{:S(2)}, u32[]{:S(2)}) collective-permute-start(bf16[136,512]{1,0:T(8,128)(2,1)S(1)} %get-tuple-element.17), channel_id=1, source_target_pairs={{0,16},{1,497},{2,18},{3,499},{4,20},{5,501},{6,22},{7,503},{8,24}... | collective-permute-start | bytes 417800 | tf_op jit(solution)/shard_map/ppermute | solution.py:31
  17.6 2.2 %collective-permute-start.1 = (bf16[136,512]{1,0:T(8,128)(2,1)S(1)}, bf16[136,512]{1,0:T(8,128)(2,1)S(1)}, u32[]{:S(2)}, u32[]{:S(2)}) collective-permute-start(bf16[136,512]{1,0:T(8,128)(2,1)S(1)} %get-tuple-element.18), channel_id=1, source_target_pairs={{0,8},{1,505},{2,10},{3,507},{4,12},{5,509},{6,14},{7,511},{8,16},... | collective-permute-start | bytes 417800 | tf_op jit(solution)/shard_map/ppermute | solution.py:31
  19.8 3.1 %collective-permute-start.2 = (bf16[136,512]{1,0:T(8,128)(2,1)S(1)}, bf16[136,512]{1,0:T(8,128)(2,1)S(1)}, u32[]{:S(2)}, u32[]{:S(2)}) collective-permute-start(bf16[136,512]{1,0:T(8,128)(2,1)S(1)} %get-tuple-element.19), channel_id=1, source_target_pairs={{0,504},{1,9},{2,506},{3,11},{4,508},{5,13},{6,510},{7,15},{8,0},{... | collective-permute-start | bytes 417800 | tf_op jit(solution)/shard_map/ppermute | solution.py:31
  22.9 0.0 copy-done.2
  22.9 0.1 reshape.449
  23.1 0.1 reshape.451
  23.1 0.0 copy-done
  23.1 0.0 copy-done.3
  23.1 0.0 copy-done.1
  23.2 0.6 convolution_convert_fusion.parts_ref
  23.8 0.1 add_select_fusion
  23.9 0.0 collective-permute-done.d_ref
  23.9 0.5 collective-permute-done.1.c_ref
  24.5 4.5 %collective-permute-done.2.a_ref = bf16[136,512]{1,0:T(8,128)(2,1)S(1)} collective-permute-done((bf16[136,512]{1,0:T(8,128)(2,1)S(1)}, bf16[136,512]{1,0:T(8,128)(2,1)S(1)}, u32[]{:S(2)}, u32[]{:S(2)}) %collective-permute-start.2) | collective-permute-done | bytes 139296 | tf_op jit(solution)/shard_map/ppermute | solution.py:31
  28.9 0.6 power_rows.1
  29.5 17.6 %all_to_all.10.in_ref = f32[64,1,384]{2,1,0:T(1,128)S(1)} all-to-all(f32[64,1,384]{2,1,0:T(1,128)S(1)} %power_rows.1), channel_id=1, replica_groups=mesh['y'=8,'z'=8,'ta'=8] {'y','ta'}, dimensions={0} | all-to-all | bytes 196608 | tf_op jit(solution)/shard_map/all_to_all | solution.py:35
  47.1 0.5 choose_rows.1
  47.6 16.1 %all_to_all.11.in_ref = f32[64,1,384]{2,1,0:T(1,128)S(1)} all-to-all(f32[64,1,384]{2,1,0:T(1,128)S(1)} %choose_rows.1), channel_id=1, replica_groups=mesh['y'=8,'z'=8,'ta'=8] {'z','ta'}, dimensions={0} | all-to-all | bytes 196608 | tf_op jit(solution)/shard_map/all_to_all | solution.py:35
  63.7 0.7 %unpack_rows.1 = f32[8,256]{1,0:T(8,128)} custom-call(f32[64,1,384]{2,1,0:T(1,128)S(1)} %all_to_all.11.in_ref), custom_call_target="tpu_custom_call" | custom-call | tf_op jit(solution)/shard_map/unpack_rows/pallas_call | solution.py:273
  (1 shorter events, 0.0 us)
Async XLA Ops:
  0.0 23.1 %copy-start = (f32[256,512]{1,0:T(8,128)S(1)}, f32[256,512]{1,0:T(8,128)}, u32[]{:S(2)}) copy-start(f32[256,512]{1,0:T(8,128)} %constant.104.clone) | copy-start | bytes 1572868
  0.0 22.9 %copy-start.2 = (s32[512]{0:T(512)S(1)}, s32[512]{0:T(512)}, u32[]{:S(2)}) copy-start(s32[512]{0:T(512)} %param.10) | copy-start | bytes 6148
  0.0 23.1 %copy-start.3 = (f32[256]{0:T(256)S(1)}, f32[256]{0:T(256)}, u32[]{:S(2)}) copy-start(f32[256]{0:T(256)} %param.11) | copy-start | bytes 3076
  0.0 23.1 %copy-start.1 = (f32[256,256]{1,0:T(8,128)S(1)}, f32[256,256]{1,0:T(8,128)}, u32[]{:S(2)}) copy-start(f32[256,256]{1,0:T(8,128)} %param.12) | copy-start | bytes 786436
  3.2 20.7 %collective-permute-start = (bf16[136,512]{1,0:T(8,128)(2,1)S(1)}, bf16[136,512]{1,0:T(8,128)(2,1)S(1)}, u32[]{:S(2)}, u32[]{:S(2)}) collective-permute-start(bf16[136,512]{1,0:T(8,128)(2,1)S(1)} %get-tuple-element.17), channel_id=1, source_target_pairs={{0,16},{1,497},{2,18},{3,499},{4,20},{5,501},{6,22},{7,503},{8,24}... | collective-permute-start | bytes 417800 | tf_op jit(solution)/shard_map/ppermute | solution.py:31
  17.6 6.8 %collective-permute-start.1 = (bf16[136,512]{1,0:T(8,128)(2,1)S(1)}, bf16[136,512]{1,0:T(8,128)(2,1)S(1)}, u32[]{:S(2)}, u32[]{:S(2)}) collective-permute-start(bf16[136,512]{1,0:T(8,128)(2,1)S(1)} %get-tuple-element.18), channel_id=1, source_target_pairs={{0,8},{1,505},{2,10},{3,507},{4,12},{5,509},{6,14},{7,511},{8,16},... | collective-permute-start | bytes 417800 | tf_op jit(solution)/shard_map/ppermute | solution.py:31
  19.8 9.1 %collective-permute-start.2 = (bf16[136,512]{1,0:T(8,128)(2,1)S(1)}, bf16[136,512]{1,0:T(8,128)(2,1)S(1)}, u32[]{:S(2)}, u32[]{:S(2)}) collective-permute-start(bf16[136,512]{1,0:T(8,128)(2,1)S(1)} %get-tuple-element.19), channel_id=1, source_target_pairs={{0,504},{1,9},{2,506},{3,11},{4,508},{5,13},{6,510},{7,15},{8,0},{... | collective-permute-start | bytes 417800 | tf_op jit(solution)/shard_map/ppermute | solution.py:31

commit v11 on v9

--- a/solution.py
+++ b/solution.py
@@ -18,6 +18,7 @@
 SLICE = 32
 PACK = 4
 TOGETHER = 16
+COPY_TIMES = 2
 
 
 def opposed(shard, by):
@@ -51,7 +52,7 @@
     return exact_dot(weighted, jnp.asarray(fourier_table(taper.shape[0]))).astype(jnp.bfloat16)
 
 
-BLOCK_STEPS = (3, 2, 0, 1)
+BLOCK_STEPS = (3, 0, 2, 1)
 
 
 def group_kernel(block_total, place_ref, ids_hbm, flags_hbm, vis_hbm, *rest):
@@ -61,7 +62,8 @@
         pltpu.make_async_copy(source, target, few_sems.at[i])
         for i, (source, target) in enumerate(((ids_hbm, ids_ref), (flags_hbm, flags_ref)))
     ]
-    copies = [pltpu.make_async_copy(vis_hbm.at[t], held_ref.at[t], sems.at[t]) for t in range(time_count)]
+    parts = [pl.ds(t, COPY_TIMES) for t in range(0, time_count, COPY_TIMES)]
+    copies = [pltpu.make_async_copy(vis_hbm.at[p], held_ref.at[p], sems.at[i]) for i, p in enumerate(parts)]
     for copy in few + copies:
         copy.start()
     for copy in few:
@@ -80,8 +82,8 @@
             table = onehot * flags_ref[t : t + 1, :].astype(jnp.float32)
             counts = jnp.where(lane == t, jnp.sum(table, axis=1, keepdims=True), counts)
             tables.append(table.astype(jnp.bfloat16))
-        for t in range(first, first + TOGETHER):
-            copies[t].wait()
+        for copy in copies[first // COPY_TIMES : (first + TOGETHER) // COPY_TIMES]:
+            copy.wait()
         sums = [
             jnp.dot(table, held_ref[first + i], preferred_element_type=jnp.float32)
             for i, table in enumerate(tables)
@@ -106,7 +108,7 @@
         out_specs=[pl.BlockSpec(memory_space=pltpu.VMEM)] * SPAN,
         out_shape=[block] * SPAN,
         scratch_shapes=[pltpu.VMEM(x.shape, x.dtype) for x in arrays]
-        + [pltpu.SemaphoreType.DMA((2,)), pltpu.SemaphoreType.DMA((time_count,))],
+        + [pltpu.SemaphoreType.DMA((2,)), pltpu.SemaphoreType.DMA((time_count // COPY_TIMES,))],
         compiler_params=pltpu.CompilerParams(vmem_limit_bytes=16 << 20),
         cost_estimate=pl.CostEstimate(
             flops=2 * time_count * SPAN * GR_DEV * block_length * row_width,
@@ -140,7 +142,7 @@
     )
 
 
-def power_kernel(parts_ref, d_ref, c_ref, a_ref, b_ref, out_ref):
+def power_kernel(parts_ref, d_ref, a_ref, c_ref, b_ref, out_ref):
     channels = parts_ref.shape[0]
     rows = a_ref.shape[0] - COUNT_ROWS
     slices = channels // SLICE
@@ -252,7 +254,7 @@
 
     place = (lax.axis_index(BLOCK_AXES) * 2 + lax.axis_index("ta") % 2)[None]
     blocks = group_sums(visibilities, flags, group_ids, place, block_total)
-    blocks = [opposed(block, by) if by else block for block, by in zip(blocks, (-2, -1, 1, 0))]
+    blocks = [opposed(block, by) if by else block for block, by in zip(blocks, (-2, 1, -1, 0))]
     parts = transform_parts(taper, inv_cov)
 
     order = group_order.reshape(y_size, z_size, GR_DEV)

time: 64.6 us -> 65.8 us (1.019)
  waiting for transfers between devices: 5 us -> 0.99 us
  starting transfers between devices: 19.7 us -> 23 us
  blocking collectives: 33.6 us -> 35.5 us
    ppermute x3, waiting for transfers between devices: 5 us -> 0.99 us  [opposed(): return lax.ppermute(shard, (*BLOCK_AXES, 'ta'), pairs)]
    ppermute x3, starting transfers between devices: 19.7 us -> 23 us  [opposed(): return lax.ppermute(shard, (*BLOCK_AXES, 'ta'), pairs)]
    all_to_all x2, blocking collectives: 33.6 us -> 35.5 us  [exchange(): return lax.all_to_all(chunks, axis, 0, 0, tiled=True)]
  transfers between devices with their start and end apart: 3 -> 3, of which waited for: 2 -> 1; matrix products, arithmetic and copies ran while one was open for 1% -> 1% of each run, Pallas kernels for 0% -> 0%
where the time goes in v11:
time: 65.8 us; the launch traced here: 65.5 us
  blocking collectives  35.5 us (54%)
  starting transfers between devices  23 us (35%)
  Pallas kernels  4.92 us (7%)
  waiting for transfers between devices  0.99 us (2%)
    all_to_all x2, blocking collectives, exchange(): return lax.all_to_all(chunks, axis, 0, 0, tiled=True)  35.5 us
    ppermute x3, starting transfers between devices, opposed(): return lax.ppermute(shard, (*BLOCK_AXES, 'ta'), pairs)  23 us
    pallas_call x1, Pallas kernels, group_sums(): pl.pallas_call(functools.partial(group_kernel, block_total), in_specs=[pl...  3.14 us
  transfers between devices with their start and end apart: 3, of which 1 were waited for; matrix products, arithmetic and copies ran while one was open for 1% of the time, Pallas kernels for 0%

profile of v11, /device:TPU:1, one launch (start us, length us, event | category | flops | bytes accessed | tf_op | source)
XLA Modules:
  0.0 65.5 jit_solution(16306154680166335956)
XLA Ops:
  0.0 0.0 copy-start
  0.0 0.0 copy-start.2
  0.0 0.0 copy-start.3
  0.0 0.0 copy-start.1
  0.0 3.1 %group_sums.1 = (bf16[136,512]{1,0:T(8,128)(2,1)S(1)}, bf16[136,512]{1,0:T(8,128)(2,1)S(1)}, bf16[136,512]{1,0:T(8,128)(2,1)S(1)}, bf16[136,512]{1,0:T(8,128)(2,1)S(1)}) custom-call(s32[1]{0:T(128)} %bitcast.place_ref, s32[1,256]{1,0:T(1,128)} %bitcast.3, s32[16,256]{1,0:T(8,128)} %flags_hbm.1, bf16[16,256,512]{2,1,0:T(8,128)(2,1)} %vis_hbm.1), custom_call_target="tpu_custom_call" | custom-call | flops 134217728 | bytes 4194304 | tf_op jit(solution)/shard_map/group_sums/pallas_call | solution.py:105
  3.2 14.4 %collective-permute-start = (bf16[136,512]{1,0:T(8,128)(2,1)S(1)}, bf16[136,512]{1,0:T(8,128)(2,1)S(1)}, u32[]{:S(2)}, u32[]{:S(2)}) collective-permute-start(bf16[136,512]{1,0:T(8,128)(2,1)S(1)} %get-tuple-element.17), channel_id=1, source_target_pairs={{0,16},{1,497},{2,18},{3,499},{4,20},{5,501},{6,22},{7,503},{8,24}... | collective-permute-start | bytes 417800 | tf_op jit(solution)/shard_map/ppermute | solution.py:32
  17.6 3.1 %collective-permute-start.1 = (bf16[136,512]{1,0:T(8,128)(2,1)S(1)}, bf16[136,512]{1,0:T(8,128)(2,1)S(1)}, u32[]{:S(2)}, u32[]{:S(2)}) collective-permute-start(bf16[136,512]{1,0:T(8,128)(2,1)S(1)} %get-tuple-element.18), channel_id=1, source_target_pairs={{0,504},{1,9},{2,506},{3,11},{4,508},{5,13},{6,510},{7,15},{8,0},{... | collective-permute-start | bytes 417800 | tf_op jit(solution)/shard_map/ppermute | solution.py:32
  20.7 5.5 %collective-permute-start.2 = (bf16[136,512]{1,0:T(8,128)(2,1)S(1)}, bf16[136,512]{1,0:T(8,128)(2,1)S(1)}, u32[]{:S(2)}, u32[]{:S(2)}) collective-permute-start(bf16[136,512]{1,0:T(8,128)(2,1)S(1)} %get-tuple-element.19), channel_id=1, source_target_pairs={{0,8},{1,505},{2,10},{3,507},{4,12},{5,509},{6,14},{7,511},{8,16},... | collective-permute-start | bytes 417800 | tf_op jit(solution)/shard_map/ppermute | solution.py:32
  26.2 0.0 copy-done.2
  26.2 0.1 reshape.449
  26.3 0.1 reshape.451
  26.4 0.0 copy-done
  26.4 0.0 copy-done.3
  26.4 0.0 copy-done.1
  26.4 0.6 convolution_convert_fusion.parts_ref
  27.1 0.1 add_select_fusion
  27.2 0.0 collective-permute-done.d_ref
  27.2 0.0 collective-permute-done.1.a_ref
  27.2 1.0 %collective-permute-done.2.c_ref = bf16[136,512]{1,0:T(8,128)(2,1)S(1)} collective-permute-done((bf16[136,512]{1,0:T(8,128)(2,1)S(1)}, bf16[136,512]{1,0:T(8,128)(2,1)S(1)}, u32[]{:S(2)}, u32[]{:S(2)}) %collective-permute-start.2) | collective-permute-done | bytes 139296 | tf_op jit(solution)/shard_map/ppermute | solution.py:32
  28.2 0.6 power_rows.1
  28.8 17.8 %all_to_all.10.in_ref = f32[64,1,384]{2,1,0:T(1,128)S(1)} all-to-all(f32[64,1,384]{2,1,0:T(1,128)S(1)} %power_rows.1), channel_id=1, replica_groups=mesh['y'=8,'z'=8,'ta'=8] {'z','ta'}, dimensions={0} | all-to-all | bytes 196608 | tf_op jit(solution)/shard_map/all_to_all | solution.py:36
  46.5 0.5 choose_rows.1
  47.0 17.8 %all_to_all.11.in_ref = f32[64,1,384]{2,1,0:T(1,128)S(1)} all-to-all(f32[64,1,384]{2,1,0:T(1,128)S(1)} %choose_rows.1), channel_id=1, replica_groups=mesh['y'=8,'z'=8,'ta'=8] {'y','ta'}, dimensions={0} | all-to-all | bytes 196608 | tf_op jit(solution)/shard_map/all_to_all | solution.py:36
  64.8 0.7 %unpack_rows.1 = f32[8,256]{1,0:T(8,128)} custom-call(f32[64,1,384]{2,1,0:T(1,128)S(1)} %all_to_all.11.in_ref), custom_call_target="tpu_custom_call" | custom-call | tf_op jit(solution)/shard_map/unpack_rows/pallas_call | solution.py:275
  (1 shorter events, 0.0 us)
Async XLA Ops:
  0.0 26.4 %copy-start = (f32[256,512]{1,0:T(8,128)S(1)}, f32[256,512]{1,0:T(8,128)}, u32[]{:S(2)}) copy-start(f32[256,512]{1,0:T(8,128)} %constant.104.clone) | copy-start | bytes 1572868
  0.0 26.2 %copy-start.2 = (s32[512]{0:T(512)S(1)}, s32[512]{0:T(512)}, u32[]{:S(2)}) copy-start(s32[512]{0:T(512)} %param.10) | copy-start | bytes 6148
  0.0 26.4 %copy-start.3 = (f32[256]{0:T(256)S(1)}, f32[256]{0:T(256)}, u32[]{:S(2)}) copy-start(f32[256]{0:T(256)} %param.11) | copy-start | bytes 3076
  0.0 26.4 %copy-start.1 = (f32[256,256]{1,0:T(8,128)S(1)}, f32[256,256]{1,0:T(8,128)}, u32[]{:S(2)}) copy-start(f32[256,256]{1,0:T(8,128)} %param.12) | copy-start | bytes 786436
  3.2 24.0 %collective-permute-start = (bf16[136,512]{1,0:T(8,128)(2,1)S(1)}, bf16[136,512]{1,0:T(8,128)(2,1)S(1)}, u32[]{:S(2)}, u32[]{:S(2)}) collective-permute-start(bf16[136,512]{1,0:T(8,128)(2,1)S(1)} %get-tuple-element.17), channel_id=1, source_target_pairs={{0,16},{1,497},{2,18},{3,499},{4,20},{5,501},{6,22},{7,503},{8,24}... | collective-permute-start | bytes 417800 | tf_op jit(solution)/shard_map/ppermute | solution.py:32
  17.6 9.6 %collective-permute-start.1 = (bf16[136,512]{1,0:T(8,128)(2,1)S(1)}, bf16[136,512]{1,0:T(8,128)(2,1)S(1)}, u32[]{:S(2)}, u32[]{:S(2)}) collective-permute-start(bf16[136,512]{1,0:T(8,128)(2,1)S(1)} %get-tuple-element.18), channel_id=1, source_target_pairs={{0,504},{1,9},{2,506},{3,11},{4,508},{5,13},{6,510},{7,15},{8,0},{... | collective-permute-start | bytes 417800 | tf_op jit(solution)/shard_map/ppermute | solution.py:32
  20.7 7.5 %collective-permute-start.2 = (bf16[136,512]{1,0:T(8,128)(2,1)S(1)}, bf16[136,512]{1,0:T(8,128)(2,1)S(1)}, u32[]{:S(2)}, u32[]{:S(2)}) collective-permute-start(bf16[136,512]{1,0:T(8,128)(2,1)S(1)} %get-tuple-element.19), channel_id=1, source_target_pairs={{0,8},{1,505},{2,10},{3,507},{4,12},{5,509},{6,14},{7,511},{8,16},... | collective-permute-start | bytes 417800 | tf_op jit(solution)/shard_map/ppermute | solution.py:32

commit v12 on v9

--- a/solution.py
+++ b/solution.py
@@ -14,6 +14,7 @@
 SPAN = 4
 LANES = 128
 BLOCK_AXES = ("y", "z")
+TIME_AXES = ("x", "core")
 COUNT_ROWS = 8
 SLICE = 32
 PACK = 4
@@ -22,13 +23,13 @@
 
 def opposed(shard, by):
     blocks = lax.axis_size(BLOCK_AXES)
-    times = lax.axis_size("ta")
+    times = lax.axis_size(TIME_AXES)
     pairs = []
     for block in range(blocks):
         for time in range(times):
             target = (block + (by if time % 2 else -by)) % blocks
             pairs.append((block * times + time, target * times + time))
-    return lax.ppermute(shard, (*BLOCK_AXES, "ta"), pairs)
+    return lax.ppermute(shard, (*BLOCK_AXES, *TIME_AXES), pairs)
 
 
 def exchange(chunks, axis):
@@ -161,8 +162,8 @@
     count = jnp.sum(pair_sum(*counts), axis=1, keepdims=True)
     count = pack_counts(count)
     for j in range(slices):
-        half = power[:, j // PACK * LANES : (j // PACK + 1) * LANES]
-        chunk = packed(half, j % PACK)
+        half = power[:, j % 2 * LANES : (j % 2 + 1) * LANES]
+        chunk = packed(half, j // 2)
         for copy in range(out_ref.shape[0] // slices):
             store_chunk(out_ref, copy * slices + j, chunk, count)
 
@@ -202,7 +203,7 @@
     lane = lax.broadcasted_iota(jnp.int32, rows.shape, 1)
     count = jnp.where(lane == member * (LANES // GR_DEV), found[:, 2 * LANES :], 0.0)
     count = jnp.sum(count, axis=1, keepdims=True)
-    copies = times
+    copies = times // 2
     for y in range(out_ref.shape[0] // copies):
         span = slice(y * GR_DEV, (y + 1) * GR_DEV)
         chunk, counts = packed(rows[span], 0), pack_counts(count[span])
@@ -211,27 +212,20 @@
 
 
 def unpack_kernel(in_ref, out_ref):
-    slices = out_ref.shape[1] // SLICE
     group = lane_group((GR_DEV, LANES))
     member = lax.broadcasted_iota(jnp.int32, (GR_DEV, LANES), 0) % PACK
-    totals = []
-    for j in range(slices):
-        total = in_ref[j]
-        for y in range(1, in_ref.shape[0] // slices):
-            total = total + in_ref[y * slices + j]
-        totals.append(total)
-    count = jnp.where(count_lanes(GR_DEV), jnp.broadcast_to(totals[0][:, 2 * LANES :], (GR_DEV, LANES)), 0.0)
-    count = jnp.maximum(jnp.sum(count, axis=1, keepdims=True), 1.0)
-    for half in range(slices // PACK):
-        result = jnp.zeros((GR_DEV, LANES), jnp.float32)
-        for k in range(PACK):
-            total = totals[half * PACK + k]
-            rows = jnp.concatenate(
-                [jnp.broadcast_to(total[:, a * LANES : (a + 1) * LANES], (PACK, LANES)) for a in range(2)], axis=0
-            )
-            for b in range(PACK):
-                result = jnp.where((group == k) & (member == b), turned(rows, k - b), result)
-        out_ref[:, half * LANES : (half + 1) * LANES] = result / count
+    result = jnp.zeros((GR_DEV, LANES), jnp.float32)
+    for k in range(PACK):
+        total = in_ref[k]
+        for y in range(1, in_ref.shape[0] // PACK):
+            total = total + in_ref[y * PACK + k]
+        rows = jnp.concatenate(
+            [jnp.broadcast_to(total[:, a * LANES : (a + 1) * LANES], (PACK, LANES)) for a in range(2)], axis=0
+        )
+        for b in range(PACK):
+            result = jnp.where((group == k) & (member == b), turned(rows, k - b), result)
+    count = jnp.where(count_lanes(GR_DEV), jnp.broadcast_to(total[:, 2 * LANES :], (GR_DEV, LANES)), 0.0)
+    out_ref[...] = result / jnp.maximum(jnp.sum(count, axis=1, keepdims=True), 1.0)
 
 
 def small_call(kernel, shape, name):
@@ -245,12 +239,13 @@
 
 def on_device(visibilities, flags, group_ids, group_order, taper, inv_cov):
     channels = taper.shape[0]
-    y_size, z_size, times = (lax.axis_size(axis) for axis in ("y", "z", "ta"))
+    y_size, z_size, times = (lax.axis_size(axis) for axis in ("y", "z", TIME_AXES))
     block_total = y_size * z_size
     slices = channels // SLICE
     width = GR_DEV * SLICE + LANES
 
-    place = (lax.axis_index(BLOCK_AXES) * 2 + lax.axis_index("ta") % 2)[None]
+    core = lax.axis_index("core")
+    place = (lax.axis_index(BLOCK_AXES) * 2 + core)[None]
     blocks = group_sums(visibilities, flags, group_ids, place, block_total)
     blocks = [opposed(block, by) if by else block for block, by in zip(blocks, (-2, -1, 1, 0))]
     parts = transform_parts(taper, inv_cov)
@@ -258,29 +253,34 @@
     order = group_order.reshape(y_size, z_size, GR_DEV)
     wanted = lax.dynamic_index_in_dim(order, lax.axis_index("z"), 1, keepdims=False).reshape(-1, 1)
     columns = []
-    for core in range(2):
-        holder = (wanted // GR_DEV + 2 - core) % block_total
-        column = core * z_size + holder % z_size
+    for side in range(2):
+        holder = (wanted // GR_DEV + 2 - side) % block_total
+        column = side * z_size + holder % z_size
         columns.append(jnp.where(holder // z_size == lax.axis_index("y"), column, -1))
     parts, *spots = lax.optimization_barrier((parts, *columns, wanted % GR_DEV))
 
     power = small_call(power_kernel, (z_size * slices, 1, width), "power_rows")(parts, *blocks)
     choose = functools.partial(choose_kernel, times)
-    shape = (y_size * times, 1, width)
-    chosen = small_call(choose, shape, "choose_rows")(*spots, exchange(power, ("z", "ta")))
-
-    found = exchange(chosen, ("y", "ta"))
-    return small_call(unpack_kernel, (GR_DEV, channels), "unpack_rows")(found)
+    shape = (y_size * times // 2, 1, width)
+    chosen = small_call(choose, shape, "choose_rows")(*spots, exchange(power, ("z", *TIME_AXES)))
+
+    found = exchange(chosen, ("y", "x"))
+    mine = small_call(unpack_kernel, (GR_DEV, LANES), "unpack_rows")(found)
+    other = lax.ppermute(mine, "core", [(0, 1), (1, 0)])
+    first = core == 0
+    return jnp.concatenate([jnp.where(first, mine, other), jnp.where(first, other, mine)], axis=1)
 
 
 def solution(mesh):
     blocks, times = mesh.devices.shape
     y_size = 2 ** (int(math.log2(blocks)) // 2)
-    cut = Mesh(mesh.devices.reshape(y_size, blocks // y_size, times), ("y", "z", "ta"))
+    cut = Mesh(
+        mesh.devices.reshape(y_size, blocks // y_size, times // 2, 2), (*BLOCK_AXES, *TIME_AXES)
+    )
     return jax.shard_map(
         on_device,
         mesh=cut,
-        in_specs=(P("ta", BLOCK_AXES, None), P("ta", BLOCK_AXES), P(BLOCK_AXES), P(), P(), P()),
+        in_specs=(P(TIME_AXES, BLOCK_AXES, None), P(TIME_AXES, BLOCK_AXES), P(BLOCK_AXES), P(), P(), P()),
         out_specs=P(BLOCK_AXES, None),
         check_vma=False,
     )

time: 64.6 us -> 66.5 us (1.029)
  starting transfers between devices: 19.7 us -> 23.3 us
  blocking collectives: 33.6 us -> 31 us
  waiting for transfers between devices: 5 us -> 5.8 us
    ppermute x3 -> x4, starting transfers between devices: 19.7 us -> 23.3 us  [the longest x3 19.7 us: opposed(): return lax.ppermute(shard, (*BLOCK_AXES, *TIME_AXES), pairs)]
    all_to_all x2, blocking collectives: 33.6 us -> 31 us  [exchange(): return lax.all_to_all(chunks, axis, 0, 0, tiled=True)]
    ppermute x3 -> x4, waiting for transfers between devices: 5 us -> 5.8 us  [the longest x3 5 us: opposed(): return lax.ppermute(shard, (*BLOCK_AXES, *TIME_AXES), pairs)]
  transfers between devices with their start and end apart: 3 -> 4, of which waited for: 2 -> 3; matrix products, arithmetic and copies ran while one was open for 1% -> 1% of each run, Pallas kernels for 0% -> 0%
where the time goes in v12:
time: 66.5 us; the launch traced here: 66.2 us
  blocking collectives  31 us (47%)
  starting transfers between devices  23.3 us (35%)
  waiting for transfers between devices  5.8 us (9%)
  Pallas kernels  4.37 us (7%)
  other arithmetic  0.73 us (1%)
    all_to_all x2, blocking collectives, exchange(): return lax.all_to_all(chunks, axis, 0, 0, tiled=True)  31 us
    ppermute x3, starting transfers between devices, opposed(): return lax.ppermute(shard, (*BLOCK_AXES, *TIME_AXES), pairs)  19.7 us
    ppermute x3, waiting for transfers between devices, opposed(): return lax.ppermute(shard, (*BLOCK_AXES, *TIME_AXES), pairs)  5 us
    ppermute x1, starting transfers between devices, on_device(): other = lax.ppermute(mine, 'core', [(0, 1), (1, 0)])  3.66 us
    pallas_call x1, Pallas kernels, group_sums(): pl.pallas_call(functools.partial(group_kernel, block_total), in_specs=[pl...  3.2 us
  transfers between devices with their start and end apart: 4, of which 3 were waited for; matrix products, arithmetic and copies ran while one was open for 1% of the time, Pallas kernels for 0%

profile of v12, /device:TPU:1, one launch (start us, length us, event | category | flops | bytes accessed | tf_op | source)
XLA Modules:
  0.0 66.2 jit_solution(7301394425132934881)
XLA Ops:
  0.0 0.0 copy-start
  0.0 0.0 copy-start.2
  0.0 0.0 copy-start.1
  0.0 0.0 copy-start.3
  0.0 3.2 %group_sums.1 = (bf16[136,512]{1,0:T(8,128)(2,1)S(1)}, bf16[136,512]{1,0:T(8,128)(2,1)S(1)}, bf16[136,512]{1,0:T(8,128)(2,1)S(1)}, bf16[136,512]{1,0:T(8,128)(2,1)S(1)}) custom-call(s32[1]{0:T(128)} %bitcast.place_ref, s32[1,256]{1,0:T(1,128)} %bitcast.3, s32[16,256]{1,0:T(8,128)} %flags_hbm.1, bf16[16,256,512]{2,1,0:T(8,128)(2,1)} %vis_hbm.1), custom_call_target="tpu_custom_call" | custom-call | flops 134217728 | bytes 4194304 | tf_op jit(solution)/shard_map/group_sums/pallas_call | solution.py:104
  3.2 14.4 %collective-permute-start = (bf16[136,512]{1,0:T(8,128)(2,1)S(1)}, bf16[136,512]{1,0:T(8,128)(2,1)S(1)}, u32[]{:S(2)}, u32[]{:S(2)}) collective-permute-start(bf16[136,512]{1,0:T(8,128)(2,1)S(1)} %get-tuple-element.17), channel_id=1, source_target_pairs={{0,16},{1,497},{2,18},{3,499},{4,20},{5,501},{6,22},{7,503},{8,24}... | collective-permute-start | bytes 417800 | tf_op jit(solution)/shard_map/ppermute | solution.py:32
  17.6 2.2 %collective-permute-start.1 = (bf16[136,512]{1,0:T(8,128)(2,1)S(1)}, bf16[136,512]{1,0:T(8,128)(2,1)S(1)}, u32[]{:S(2)}, u32[]{:S(2)}) collective-permute-start(bf16[136,512]{1,0:T(8,128)(2,1)S(1)} %get-tuple-element.18), channel_id=1, source_target_pairs={{0,8},{1,505},{2,10},{3,507},{4,12},{5,509},{6,14},{7,511},{8,16},... | collective-permute-start | bytes 417800 | tf_op jit(solution)/shard_map/ppermute | solution.py:32
  19.8 3.1 %collective-permute-start.2 = (bf16[136,512]{1,0:T(8,128)(2,1)S(1)}, bf16[136,512]{1,0:T(8,128)(2,1)S(1)}, u32[]{:S(2)}, u32[]{:S(2)}) collective-permute-start(bf16[136,512]{1,0:T(8,128)(2,1)S(1)} %get-tuple-element.19), channel_id=1, source_target_pairs={{0,504},{1,9},{2,506},{3,11},{4,508},{5,13},{6,510},{7,15},{8,0},{... | collective-permute-start | bytes 417800 | tf_op jit(solution)/shard_map/ppermute | solution.py:32
  22.9 0.0 copy-done.2
  22.9 0.1 reshape.449
  23.1 0.1 reshape.451
  23.1 0.0 copy-done
  23.1 0.0 copy-done.1
  23.1 0.0 copy-done.3
  23.2 0.6 convolution_convert_fusion.parts_ref
  23.8 0.1 add_select_fusion
  23.9 0.0 collective-permute-done.d_ref
  23.9 0.5 collective-permute-done.1.c_ref
  24.4 4.5 %collective-permute-done.2.a_ref = bf16[136,512]{1,0:T(8,128)(2,1)S(1)} collective-permute-done((bf16[136,512]{1,0:T(8,128)(2,1)S(1)}, bf16[136,512]{1,0:T(8,128)(2,1)S(1)}, u32[]{:S(2)}, u32[]{:S(2)}) %collective-permute-start.2) | collective-permute-done | bytes 139296 | tf_op jit(solution)/shard_map/ppermute | solution.py:32
  28.9 0.6 power_rows.1
  29.5 15.3 %all_to_all.10.in_ref = f32[64,1,384]{2,1,0:T(1,128)S(1)} all-to-all(f32[64,1,384]{2,1,0:T(1,128)S(1)} %power_rows.1), channel_id=1, replica_groups=mesh['y'=8,'z'=8,'x'=4,'core'=2] {'z','x','core'}, dimensions={0} | all-to-all | bytes 196608 | tf_op jit(solution)/shard_map/all_to_all | solution.py:36
  44.9 0.5 choose_rows.1
  45.4 15.7 %all_to_all.11.in_ref = f32[32,1,384]{2,1,0:T(1,128)S(1)} all-to-all(f32[32,1,384]{2,1,0:T(1,128)S(1)} %choose_rows.1), channel_id=1, replica_groups=mesh['y'=8,'z'=8,'x'=4,'core'=2] {'y','x'}, dimensions={0} | all-to-all | bytes 98304 | tf_op jit(solution)/shard_map/all_to_all | solution.py:36
  61.0 0.1 unpack_rows.1
  61.1 3.7 %collective-permute-start.3 = (f32[8,128]{1,0:T(8,128)S(1)}, f32[8,128]{1,0:T(8,128)S(1)}, u32[]{:S(2)}, u32[]{:S(2)}) collective-permute-start(f32[8,128]{1,0:T(8,128)S(1)} %unpack_rows.1), channel_id=1, source_target_pairs={{0,1},{1,0},{2,3},{3,2},{4,5},{5,4},{6,7},{7,6},{8,9},{9,8},{10,11... | collective-permute-start | bytes 12296 | tf_op jit(solution)/shard_map/ppermute | solution.py:269
  64.8 0.8 %collective-permute-done.3 = f32[8,128]{1,0:T(8,128)S(1)} collective-permute-done((f32[8,128]{1,0:T(8,128)S(1)}, f32[8,128]{1,0:T(8,128)S(1)}, u32[]{:S(2)}, u32[]{:S(2)}) %collective-permute-start.3) | collective-permute-done | bytes 4128 | tf_op jit(solution)/shard_map/ppermute | solution.py:269
  65.6 0.6 pad_maximum_fusion
  (2 shorter events, 0.0 us)
Async XLA Ops:
  0.0 23.1 %copy-start = (f32[256,512]{1,0:T(8,128)S(1)}, f32[256,512]{1,0:T(8,128)}, u32[]{:S(2)}) copy-start(f32[256,512]{1,0:T(8,128)} %constant.98.clone) | copy-start | bytes 1572868
  0.0 22.9 %copy-start.2 = (s32[512]{0:T(512)S(1)}, s32[512]{0:T(512)}, u32[]{:S(2)}) copy-start(s32[512]{0:T(512)} %param.10) | copy-start | bytes 6148
  0.0 23.1 %copy-start.1 = (f32[256,256]{1,0:T(8,128)S(1)}, f32[256,256]{1,0:T(8,128)}, u32[]{:S(2)}) copy-start(f32[256,256]{1,0:T(8,128)} %param.12) | copy-start | bytes 786436
  0.0 23.1 %copy-start.3 = (f32[256]{0:T(256)S(1)}, f32[256]{0:T(256)}, u32[]{:S(2)}) copy-start(f32[256]{0:T(256)} %param.11) | copy-start | bytes 3076
  3.2 20.7 %collective-permute-start = (bf16[136,512]{1,0:T(8,128)(2,1)S(1)}, bf16[136,512]{1,0:T(8,128)(2,1)S(1)}, u32[]{:S(2)}, u32[]{:S(2)}) collective-permute-start(bf16[136,512]{1,0:T(8,128)(2,1)S(1)} %get-tuple-element.17), channel_id=1, source_target_pairs={{0,16},{1,497},{2,18},{3,499},{4,20},{5,501},{6,22},{7,503},{8,24}... | collective-permute-start | bytes 417800 | tf_op jit(solution)/shard_map/ppermute | solution.py:32
  17.6 6.8 %collective-permute-start.1 = (bf16[136,512]{1,0:T(8,128)(2,1)S(1)}, bf16[136,512]{1,0:T(8,128)(2,1)S(1)}, u32[]{:S(2)}, u32[]{:S(2)}) collective-permute-start(bf16[136,512]{1,0:T(8,128)(2,1)S(1)} %get-tuple-element.18), channel_id=1, source_target_pairs={{0,8},{1,505},{2,10},{3,507},{4,12},{5,509},{6,14},{7,511},{8,16},... | collective-permute-start | bytes 417800 | tf_op jit(solution)/shard_map/ppermute | solution.py:32
  19.8 9.1 %collective-permute-start.2 = (bf16[136,512]{1,0:T(8,128)(2,1)S(1)}, bf16[136,512]{1,0:T(8,128)(2,1)S(1)}, u32[]{:S(2)}, u32[]{:S(2)}) collective-permute-start(bf16[136,512]{1,0:T(8,128)(2,1)S(1)} %get-tuple-element.19), channel_id=1, source_target_pairs={{0,504},{1,9},{2,506},{3,11},{4,508},{5,13},{6,510},{7,15},{8,0},{... | collective-permute-start | bytes 417800 | tf_op jit(solution)/shard_map/ppermute | solution.py:32
  61.1 4.5 %collective-permute-start.3 = (f32[8,128]{1,0:T(8,128)S(1)}, f32[8,128]{1,0:T(8,128)S(1)}, u32[]{:S(2)}, u32[]{:S(2)}) collective-permute-start(f32[8,128]{1,0:T(8,128)S(1)} %unpack_rows.1), channel_id=1, source_target_pairs={{0,1},{1,0},{2,3},{3,2},{4,5},{5,4},{6,7},{7,6},{8,9},{9,8},{10,11... | collective-permute-start | bytes 12296 | tf_op jit(solution)/shard_map/ppermute | solution.py:269
